TPU v7x, 32 devices: a whole 2x2x4 slice. The times are simulated.
32 devices in a mesh: section: 2 (over core), expert: 4 (over y, x), shard: 4 (over z).
Axes of the slice: x: 2, y: 2, z: 4, core: 2. Of those that a mesh axis runs over, the one named last changes fastest.
Arguments:
- feed: bfloat16 [2, 2, 1024, 768], P('section', None, ('expert', 'shard')), may hold values from -6 to 6
- segments: int32 [2, 16, 64], P(None, ('expert', 'shard')), may hold values from 0 to 3, never falling along the last dimension, each value on 1 to 32 neighbouring positions
- routes: int32 [2, 2, 16, 64], P('section', None, ('expert', 'shard')), may hold values from 0 to 3, as said below
- rel_bucket: int32 [127], replicated, may hold values from 0 to 31
- gain_attn: bfloat16 [2, 768], P('section', ('expert', 'shard')), may hold values from 0.099609375 to 1.8984375
- gain_ffn: bfloat16 [2, 768], P('section', ('expert', 'shard')), may hold values from 0.099609375 to 1.8984375
- w_query: bfloat16 [2, 768, 768], P('section', ('expert', 'shard')), may hold values from -0.21875 to 0.21875
- w_key: bfloat16 [2, 768, 768], P('section', ('expert', 'shard')), may hold values from -0.21875 to 0.21875
- w_value: bfloat16 [2, 768, 768], P('section', ('expert', 'shard')), may hold values from -0.21875 to 0.21875
- w_out_attn: bfloat16 [2, 768, 768], P('section', ('expert', 'shard')), may hold values from -0.875 to 0.875
- rel_table: bfloat16 [2, 384], P('section', ('expert', 'shard')), may hold values from -4 to 4
- router: bfloat16 [2, 768, 4], P('section', ('expert', 'shard')), may hold values from -0.15625 to 0.15625
- expert_in: bfloat16 [2, 4, 768, 3072], P('section', 'expert', None, 'shard'), may hold values from -0.21875 to 0.21875
- expert_out: bfloat16 [2, 4, 3072, 768], P('section', 'expert', 'shard'), may hold values from -0.4375 to 0.4375
Outputs:
- layer_out: bfloat16 [2, 2, 1024, 768], P('section', None, ('expert', 'shard'))
- layer_in_grad: bfloat16 [2, 2, 1024, 768], P('section', None, ('expert', 'shard'))
- grad_gain_attn: float32 [2, 768], P('section', ('expert', 'shard'))
- grad_gain_ffn: float32 [2, 768], P('section', ('expert', 'shard'))
- grad_w_query: float32 [2, 768, 768], P('section', ('expert', 'shard'))
- grad_w_key: float32 [2, 768, 768], P('section', ('expert', 'shard'))
- grad_w_value: float32 [2, 768, 768], P('section', ('expert', 'shard'))
- grad_w_out_attn: float32 [2, 768, 768], P('section', ('expert', 'shard'))
- grad_rel_table: float32 [2, 384], P('section', ('expert', 'shard'))
- grad_router: float32 [2, 768, 4], P('section', ('expert', 'shard'))
- grad_expert_in: float32 [2, 4, 768, 3072], P('section', 'expert', None, 'shard')
- grad_expert_out: float32 [2, 4, 3072, 768], P('section', 'expert', 'shard')
Inputs may be any that keep to these rules, and one draw needn't show every extreme that they name: `routes`: in each micro-batch of each layer no expert is named by more than 32 tokens of one sequence, and one expert, drawn from the seed, is named by exactly 32 tokens of every sequence. `segments`: along each sequence the segment numbers never fall.
All inputs are finite; a program needn't handle non-finite values.
Results may differ from a plain program's by a relative error of at most 0.022.
Values may be sent and summed in bfloat16 or wider, within the bound.
No kernel may reach another device: no remote copies, remote signals or barrier semaphores. Data moves between devices by JAX's collectives and lax.ppermute only.
A program may use at most 128 MiB of HBM per device.

v0:
```python
import math

import jax
import jax.numpy as jnp
from jax import lax
from jax.sharding import PartitionSpec as P

HEADS = 12
HEAD_DIM = 64
NB = 32


EPSILON = 1e-06
MASK_FILL = -1e30


def shifted(value, axis, steps):
    count = lax.axis_size(axis)
    initial, last = (max(0, -steps), min(count, count - steps))
    return lax.ppermute(value, axis, [(source, source + steps) for source in range(initial, last)])


def normalize(resid_in, gain_in):
    return (
        resid_in
        * lax.rsqrt(jnp.mean(resid_in * resid_in, axis=-1, keepdims=True) + EPSILON)
        * gain_in
    )


def relative_bias(rel_flat, rel_bucket):
    table_grid = rel_flat.reshape(NB, HEADS)
    bucket_hot = (rel_bucket[:, None] == jnp.arange(NB, dtype=jnp.int32)[None, :]).astype(
        jnp.float32
    )
    per_offset = jnp.dot(bucket_hot, table_grid, precision=lax.Precision.HIGHEST)
    span_len = (rel_bucket.shape[0] + 1) // 2
    positions = jnp.arange(span_len, dtype=jnp.int32)
    offsets = positions[None, :] - positions[:, None] + (span_len - 1)
    return jnp.transpose(per_offset[offsets], (2, 0, 1))


def gate_of(logits, chosen):
    return jnp.sum(jax.nn.softmax(logits, axis=-1) * chosen, axis=-1)


def body(
    feed,
    segments,
    routes,
    rel_bucket,
    gain_attn,
    gain_ffn,
    w_query,
    w_key,
    w_value,
    w_out_attn,
    rel_table,
    router,
    expert_in,
    expert_out,
):
    micro_count = feed.shape[1]
    seq_length = feed.shape[2]
    model_width = feed.shape[3]
    expert_count = lax.axis_size("expert")
    capacity = max(2, 2 * seq_length // expert_count)
    slot_count = expert_count * capacity
    score_scale = 1.0 / math.sqrt(HEAD_DIM)
    section_index = lax.axis_index("section")
    last_section = section_index == 1
    gathered = (
        lax.all_gather(w_query[0], ("expert", "shard"), axis=0, tiled=True),
        lax.all_gather(w_key[0], ("expert", "shard"), axis=0, tiled=True),
        lax.all_gather(w_value[0], ("expert", "shard"), axis=0, tiled=True),
        lax.all_gather(w_out_attn[0], ("expert", "shard"), axis=0, tiled=True),
        lax.all_gather(router[0], ("expert", "shard"), axis=0, tiled=True),
        lax.all_gather(gain_attn[0], ("expert", "shard"), axis=0, tiled=True),
        lax.all_gather(gain_ffn[0], ("expert", "shard"), axis=0, tiled=True),
        lax.all_gather(rel_table[0], ("expert", "shard"), axis=0, tiled=True),
    )
    w_joint = jnp.concatenate([gathered[0], gathered[1], gathered[2]], axis=1)
    w_attn_out = gathered[3]
    w_router = gathered[4]
    norm_one = gathered[5].astype(jnp.float32)
    norm_two = gathered[6].astype(jnp.float32)
    rel_bias, bias_back = jax.vjp(
        lambda flat_table: relative_bias(flat_table, rel_bucket), gathered[7].astype(jnp.float32)
    )
    expert_ids = jnp.arange(expert_count, dtype=jnp.int32)
    slot_ids = jnp.arange(slot_count, dtype=jnp.int32)
    full_in, full_out = (expert_in[0, 0], expert_out[0, 0])

    def expert_forward(expert_rows):
        in_rows = lax.all_gather(expert_rows, "shard", axis=0, tiled=True)
        pre_act = jnp.dot(in_rows, full_in, preferred_element_type=jnp.float32)
        activated = jax.nn.gelu(pre_act).astype(jnp.bfloat16)
        partial_value = jnp.dot(activated, full_out, preferred_element_type=jnp.float32)
        own_part = lax.psum_scatter(partial_value, "shard", scatter_dimension=0, tiled=True)
        return (own_part.astype(jnp.bfloat16), (in_rows, pre_act, activated))

    def expert_backward(grad_rows, expert_saved):
        in_rows, pre_act, activated = expert_saved
        spread = lax.all_gather(grad_rows, "shard", axis=0, tiled=True)
        grad_act = jnp.einsum("rd,fd->rf", spread, full_out, preferred_element_type=jnp.float32)
        _, gelu_back = jax.vjp(jax.nn.gelu, pre_act)
        grad_pre = gelu_back(grad_act)[0].astype(jnp.bfloat16)
        grad_in_rows = jnp.einsum(
            "rf,df->rd", grad_pre, full_in, preferred_element_type=jnp.float32
        )
        own_grad = lax.psum_scatter(grad_in_rows, "shard", scatter_dimension=0, tiled=True)
        return (own_grad.astype(jnp.bfloat16), (in_rows, activated, spread, grad_pre))

    def backward_tick(grad_in, saved_state):
        (
            resid_in,
            normed_one,
            queries,
            keys_all,
            values,
            attn_probs,
            context,
            hidden,
            normed_two,
            logits,
            chosen,
            gate_value,
            dispatch,
            expert_tok,
            expert_saved,
        ) = saved_state
        grad_out = grad_in.astype(jnp.float32)
        grad_gate = jnp.sum(grad_out * expert_tok, axis=-1)
        grad_expert = (gate_value[:, None] * grad_out).astype(jnp.bfloat16)
        outgoing = jnp.einsum(
            "sc,sd->cd", dispatch, grad_expert, preferred_element_type=jnp.float32
        ).astype(jnp.bfloat16)
        arrived = lax.all_to_all(
            outgoing.reshape(expert_count, capacity, model_width),
            "expert",
            split_axis=0,
            concat_axis=0,
            tiled=True,
        )
        grad_rows_own, expert_record = expert_backward(
            arrived.reshape(slot_count, model_width), expert_saved
        )
        returned = lax.all_to_all(
            grad_rows_own.reshape(expert_count, capacity, model_width),
            "expert",
            split_axis=0,
            concat_axis=0,
            tiled=True,
        )
        grad_norm_two = jnp.einsum(
            "sc,cd->sd",
            dispatch,
            returned.reshape(slot_count, model_width),
            preferred_element_type=jnp.float32,
        )
        _, gate_back = jax.vjp(lambda logits_in: gate_of(logits_in, chosen), logits)
        grad_logits = gate_back(grad_gate)[0].astype(jnp.bfloat16)
        grad_norm_two = grad_norm_two + jnp.einsum(
            "se,de->sd", grad_logits, w_router, preferred_element_type=jnp.float32
        )
        _, norm_back_two = jax.vjp(normalize, hidden, norm_two)
        grad_hidden_norm, grad_gain_two = norm_back_two(grad_norm_two)
        grad_hidden = grad_out + grad_hidden_norm
        grad_hidden_low = grad_hidden.astype(jnp.bfloat16)
        grad_context = jnp.einsum(
            "sd,cd->sc", grad_hidden_low, w_attn_out, preferred_element_type=jnp.float32
        )
        grad_context = grad_context.astype(jnp.bfloat16).reshape(seq_length, HEADS, HEAD_DIM)
        grad_probs = jnp.einsum(
            "qhd,khd->hqk", grad_context, values, preferred_element_type=jnp.float32
        )
        grad_scores = attn_probs * (
            grad_probs - jnp.sum(attn_probs * grad_probs, axis=-1, keepdims=True)
        )
        grad_scores = grad_scores.astype(jnp.bfloat16)
        grad_queries = (
            jnp.einsum("hqk,khd->qhd", grad_scores, keys_all, preferred_element_type=jnp.float32)
            * score_scale
        ).astype(jnp.bfloat16)
        grad_keys = (
            jnp.einsum("hqk,qhd->khd", grad_scores, queries, preferred_element_type=jnp.float32)
            * score_scale
        ).astype(jnp.bfloat16)
        grad_values = jnp.einsum(
            "hqk,qhd->khd",
            attn_probs.astype(jnp.bfloat16),
            grad_context,
            preferred_element_type=jnp.float32,
        ).astype(jnp.bfloat16)
        grad_joint = jnp.concatenate(
            [
                grad_queries.reshape(seq_length, model_width),
                grad_keys.reshape(seq_length, model_width),
                grad_values.reshape(seq_length, model_width),
            ],
            axis=1,
        )
        grad_normed = jnp.einsum(
            "sc,dc->sd", grad_joint, w_joint, preferred_element_type=jnp.float32
        )
        _, norm_back_one = jax.vjp(normalize, resid_in, norm_one)
        grad_resid_norm, grad_gain_one = norm_back_one(grad_normed)
        grad_resid = grad_hidden + grad_resid_norm
        record = (
            normed_one,
            grad_joint,
            context,
            grad_hidden_low,
            normed_two,
            grad_logits,
            grad_gain_one,
            grad_gain_two,
            grad_scores,
            expert_record,
        )
        return (grad_resid.astype(jnp.bfloat16), record)

    outputs = []
    saved = []
    incoming = jnp.zeros((seq_length, model_width), jnp.bfloat16)
    for tick_num in range(micro_count + 1):
        own_feed = feed[0, min(tick_num, micro_count - 1)]
        layer_in = jnp.where(section_index == 0, own_feed, incoming)
        batch_index = jnp.clip(tick_num - section_index, 0, micro_count - 1)
        seg_ids = segments[batch_index, 0]
        route_ids = routes[0, batch_index, 0]
        forward_resid_in = layer_in.astype(jnp.float32)
        forward_normed_one = normalize(forward_resid_in, norm_one).astype(jnp.bfloat16)
        qkv_joint = jnp.dot(forward_normed_one, w_joint, preferred_element_type=jnp.float32).astype(
            jnp.bfloat16
        )
        forward_queries = qkv_joint[:, :model_width].reshape(seq_length, HEADS, HEAD_DIM)
        forward_keys_all = qkv_joint[:, model_width : 2 * model_width].reshape(
            seq_length, HEADS, HEAD_DIM
        )
        forward_values = qkv_joint[:, 2 * model_width :].reshape(seq_length, HEADS, HEAD_DIM)
        scores = (
            jnp.einsum(
                "qhd,khd->hqk",
                forward_queries,
                forward_keys_all,
                preferred_element_type=jnp.float32,
            )
            * score_scale
            + rel_bias
        )
        same_doc = seg_ids[:, None] == seg_ids[None, :]
        scores = jnp.where(same_doc[None], scores, MASK_FILL)
        row_max = jnp.max(scores, axis=-1, keepdims=True)
        exp_scores = jnp.exp(scores - row_max)
        forward_attn_probs = exp_scores / jnp.sum(exp_scores, axis=-1, keepdims=True)
        forward_context = jnp.einsum(
            "hqk,khd->qhd",
            forward_attn_probs.astype(jnp.bfloat16),
            forward_values,
            preferred_element_type=jnp.float32,
        )
        forward_context = forward_context.reshape(seq_length, model_width).astype(jnp.bfloat16)
        forward_hidden = forward_resid_in + jnp.dot(
            forward_context, w_attn_out, preferred_element_type=jnp.float32
        )
        forward_normed_two = normalize(forward_hidden, norm_two).astype(jnp.bfloat16)
        forward_logits = jnp.dot(forward_normed_two, w_router, preferred_element_type=jnp.float32)
        one_hot = (route_ids[:, None] == expert_ids[None, :]).astype(jnp.int32)
        forward_chosen = one_hot.astype(jnp.float32)
        forward_gate_value = gate_of(forward_logits, forward_chosen)
        slot_rank = jnp.sum((jnp.cumsum(one_hot, axis=0) - one_hot) * one_hot, axis=1)
        forward_dispatch = (
            (route_ids * capacity + slot_rank)[:, None] == slot_ids[None, :]
        ).astype(jnp.bfloat16)
        forward_outgoing = jnp.einsum(
            "sc,sd->cd", forward_dispatch, forward_normed_two, preferred_element_type=jnp.float32
        ).astype(jnp.bfloat16)
        forward_arrived = lax.all_to_all(
            forward_outgoing.reshape(expert_count, capacity, model_width),
            "expert",
            split_axis=0,
            concat_axis=0,
            tiled=True,
        )
        expert_result, forward_expert_saved = expert_forward(
            forward_arrived.reshape(slot_count, model_width)
        )
        forward_returned = lax.all_to_all(
            expert_result.reshape(expert_count, capacity, model_width),
            "expert",
            split_axis=0,
            concat_axis=0,
            tiled=True,
        )
        forward_expert_tok = jnp.einsum(
            "sc,cd->sd",
            forward_dispatch,
            forward_returned.reshape(slot_count, model_width),
            preferred_element_type=jnp.float32,
        )
        output = forward_hidden + forward_gate_value[:, None] * forward_expert_tok
        forward_saved_state = (
            forward_resid_in,
            forward_normed_one,
            forward_queries,
            forward_keys_all,
            forward_values,
            forward_attn_probs,
            forward_context,
            forward_hidden,
            forward_normed_two,
            forward_logits,
            forward_chosen,
            forward_gate_value,
            forward_dispatch,
            forward_expert_tok,
            forward_expert_saved,
        )
        produced = output.astype(jnp.bfloat16)
        saved_state = forward_saved_state
        outputs.append(produced)
        saved.append(saved_state)
        if tick_num < micro_count:
            incoming = shifted(produced, "section", 1)
    results = []
    records = []
    flags = []
    coming_back = jnp.zeros((seq_length, model_width), jnp.bfloat16)
    for tick_num in range(micro_count + 1):
        batch_num = tick_num + section_index - 1
        flags.append((batch_num >= 0) & (batch_num < micro_count))
        late_state = saved[min(tick_num + 1, micro_count)]
        early_state = saved[max(tick_num - 1, 0)]
        picked_state = jax.tree.map(
            lambda later_one, earlier_one: jnp.where(last_section, later_one, earlier_one),
            late_state,
            early_state,
        )
        grad_feed = feed[0, min(tick_num, micro_count - 1)]
        grad_in = jnp.where(last_section, grad_feed, coming_back)
        produced, record = backward_tick(grad_in, picked_state)
        results.append(produced)
        records.append(record)
        if tick_num < micro_count:
            coming_back = shifted(produced, "section", -1)

    def masked_rows(pieces):
        return jnp.concatenate(
            [piece * flag_now.astype(piece.dtype) for piece, flag_now in zip(pieces, flags)], axis=0
        )

    def plain_rows(pieces):
        return jnp.concatenate(pieces, axis=0)

    normed_rows = plain_rows([record[0] for record in records])
    joint_rows = masked_rows([record[1] for record in records])
    context_rows = plain_rows([record[2] for record in records])
    hidden_rows = masked_rows([record[3] for record in records])
    router_rows = plain_rows([record[4] for record in records])
    logit_rows = masked_rows([record[5] for record in records])
    gain_one_sum = sum(
        (record[6] * flag_now.astype(jnp.float32) for record, flag_now in zip(records, flags))
    )
    gain_two_sum = sum(
        (record[7] * flag_now.astype(jnp.float32) for record, flag_now in zip(records, flags))
    )
    scores_sum = sum(
        (
            record[8].astype(jnp.float32) * flag_now.astype(jnp.float32)
            for record, flag_now in zip(records, flags)
        )
    )
    table_grad = bias_back(scores_sum)[0]
    grad_query_full = jnp.einsum(
        "rd,rc->dc", normed_rows, joint_rows[:, :model_width], preferred_element_type=jnp.float32
    )
    grad_key_full = jnp.einsum(
        "rd,rc->dc",
        normed_rows,
        joint_rows[:, model_width : 2 * model_width],
        preferred_element_type=jnp.float32,
    )
    grad_value_full = jnp.einsum(
        "rd,rc->dc",
        normed_rows,
        joint_rows[:, 2 * model_width :],
        preferred_element_type=jnp.float32,
    )
    grad_attn_out = jnp.einsum(
        "rc,rd->cd", context_rows, hidden_rows, preferred_element_type=jnp.float32
    )
    grad_router_full = jnp.einsum(
        "rd,re->de", router_rows, logit_rows, preferred_element_type=jnp.float32
    )
    reduced = (
        lax.psum_scatter(grad_query_full, ("expert", "shard"), scatter_dimension=0, tiled=True),
        lax.psum_scatter(grad_key_full, ("expert", "shard"), scatter_dimension=0, tiled=True),
        lax.psum_scatter(grad_value_full, ("expert", "shard"), scatter_dimension=0, tiled=True),
        lax.psum_scatter(grad_attn_out, ("expert", "shard"), scatter_dimension=0, tiled=True),
        lax.psum_scatter(grad_router_full, ("expert", "shard"), scatter_dimension=0, tiled=True),
        lax.psum_scatter(gain_one_sum, ("expert", "shard"), scatter_dimension=0, tiled=True),
        lax.psum_scatter(gain_two_sum, ("expert", "shard"), scatter_dimension=0, tiled=True),
        lax.psum_scatter(table_grad, ("expert", "shard"), scatter_dimension=0, tiled=True),
    )
    expert_in_rows = plain_rows([record[9][0] for record in records])
    expert_act_rows = plain_rows([record[9][1] for record in records])
    expert_grad_rows = masked_rows([record[9][2] for record in records])
    expert_pre_rows = masked_rows([record[9][3] for record in records])
    grad_full_in = jnp.einsum(
        "rd,rf->df", expert_in_rows, expert_pre_rows, preferred_element_type=jnp.float32
    )
    grad_full_out = jnp.einsum(
        "rf,rd->fd", expert_act_rows, expert_grad_rows, preferred_element_type=jnp.float32
    )
    own_in, own_out = (grad_full_in, grad_full_out)
    layer_out = jnp.stack(
        [
            jnp.where(last_section, outputs[batch_num + 1], outputs[batch_num])
            for batch_num in range(micro_count)
        ]
    )
    layer_in_grad = jnp.stack(
        [
            jnp.where(last_section, results[batch_num], results[batch_num + 1])
            for batch_num in range(micro_count)
        ]
    )
    return (
        layer_out[None],
        layer_in_grad[None],
        reduced[5][None],
        reduced[6][None],
        reduced[0][None],
        reduced[1][None],
        reduced[2][None],
        reduced[3][None],
        reduced[7][None],
        reduced[4][None],
        own_in[None, None],
        own_out[None, None],
    )


def solution(mesh):
    in_specs = (
        P("section", None, ("expert", "shard"), None),
        P(None, ("expert", "shard"), None),
        P("section", None, ("expert", "shard"), None),
        P(),
        P("section", ("expert", "shard")),
        P("section", ("expert", "shard")),
        P("section", ("expert", "shard"), None),
        P("section", ("expert", "shard"), None),
        P("section", ("expert", "shard"), None),
        P("section", ("expert", "shard"), None),
        P("section", ("expert", "shard")),
        P("section", ("expert", "shard"), None),
        P("section", "expert", None, "shard"),
        P("section", "expert", "shard", None),
    )
    out_specs = (
        P("section", None, ("expert", "shard"), None),
        P("section", None, ("expert", "shard"), None),
        P("section", ("expert", "shard")),
        P("section", ("expert", "shard")),
        P("section", ("expert", "shard"), None),
        P("section", ("expert", "shard"), None),
        P("section", ("expert", "shard"), None),
        P("section", ("expert", "shard"), None),
        P("section", ("expert", "shard")),
        P("section", ("expert", "shard"), None),
        P("section", "expert", None, "shard"),
        P("section", "expert", "shard", None),
    )
    return jax.shard_map(body, mesh=mesh, in_specs=in_specs, out_specs=out_specs, check_vma=False)
```

profile of v0, /device:TPU:1, one launch (start us, length us, event | category | flops | bytes accessed | tf_op | source)
XLA Modules:
  0.0 1462.1 jit_solution(17094900646351161820)
XLA Ops:
  16.0 37.2 %all-reduce.7 = (bf16[768]{0:T(1024)(128)(2,1)S(1)}, bf16[384]{0:T(512)(128)(2,1)S(1)}, bf16[768]{0:T(1024)(128)(2,1)S(1)}) all-reduce(bf16[768]{0:T(1024)(128)(2,1)S(1)} %dynamic-update-slice, bf16[384]{0:T(512)(128)(2,1)S(1)} %dynamic-update-slice.1, ...), channel_id=2, replica_groups=mesh['section'=2,'expert'=4,'shard'=4] {'expert','shard'}, use_global_device_ids=true, to_apply=%add | all-reduce | flops 1920 | bytes 7680
  55.2 14.2 gather_fusion
  72.5 53.1 %all-gather.15.cloned.1.call-done = bf16[1,768,768]{2,1,0:T(8,128)(2,1)} async-done(((bf16[1,48,768]{2,1,0:T(8,128)(2,1)}), bf16[1,768,768]{2,1,0:T(8,128)(2,1)}) %all-gather.15.cloned.1.call-update) | async-done | bytes 1179664 | tf_op jit(solution)/shard_map/all_gather | solution.py:74
  125.6 57.8 %all-gather.17.cloned.1.call-done = bf16[1,768,768]{2,1,0:T(8,128)(2,1)} async-done(((bf16[1,48,768]{2,1,0:T(8,128)(2,1)}), bf16[1,768,768]{2,1,0:T(8,128)(2,1)}) %all-gather.17.cloned.1.call-update) | async-done | bytes 1179664 | tf_op jit(solution)/shard_map/all_gather | solution.py:75
  188.2 52.9 %all-gather.19.cloned.1.call-done = bf16[1,768,768]{2,1,0:T(8,128)(2,1)} async-done(((bf16[1,48,768]{2,1,0:T(8,128)(2,1)}), bf16[1,768,768]{2,1,0:T(8,128)(2,1)}) %all-gather.19.cloned.1.call-update) | async-done | bytes 1179664 | tf_op jit(solution)/shard_map/all_gather | solution.py:76
  243.4 6.8 all_to_all.60
  250.2 14.4 all_gather.50
  270.5 41.6 %all-gather.7 = bf16[1,768,4]{2,0,1:T(2,128)(2,1)S(1)} all-gather(bf16[1,48,4]{2,0,1:T(2,128)(2,1)S(1)} %copy.308), channel_id=9, replica_groups=mesh['section'=2,'expert'=4,'shard'=4] {'expert','shard'}, dimensions={1}, use_global_device_ids=true | all-gather | bytes 6528 | tf_op jit(solution)/shard_map/all_gather | solution.py:77
  319.5 4.2 all-to-all-done.1
  326.0 12.6 collective-permute-done
  349.9 7.4 all_to_all.61
  357.3 15.6 %all_gather.51 = bf16[512,768]{1,0:T(8,128)(2,1)S(1)} all-gather(bf16[128,768]{1,0:T(8,128)(2,1)S(1)} %bitcast.397), channel_id=1, replica_groups=mesh['section'=2,'expert'=4,'shard'=4] {'shard'}, dimensions={0}, use_global_device_ids=true | all-gather | bytes 983040 | tf_op jit(solution)/shard_map/all_gather | solution.py:95
  379.6 34.3 %reduce-scatter.16.cloned.1.call-done = f32[128,768]{1,0:T(8,128)} async-done(((f32[512,768]{1,0:T(8,128)}), f32[128,768]{1,0:T(8,128)}) %reduce-scatter.16.cloned.1.call-update) | async-done | bytes 393232 | tf_op jit(solution)/shard_map/reduce_scatter | solution.py:99
  415.7 4.2 all-to-all-start.3
  420.5 3.5 all-to-all-done.3
  428.7 4.0 all-to-all-start.6
  432.8 4.0 all-to-all-done.6
  436.8 14.7 %all_gather.53 = bf16[512,768]{1,0:T(8,128)(2,1)S(1)} all-gather(bf16[128,768]{1,0:T(8,128)(2,1)} %bitcast.47), channel_id=1, replica_groups=mesh['section'=2,'expert'=4,'shard'=4] {'shard'}, dimensions={0}, use_global_device_ids=true | all-gather | bytes 983040 | tf_op jit(solution)/shard_map/all_gather | solution.py:104
  451.6 4.2 broadcast_multiply_fusion.5
  470.8 26.5 %reduce-scatter.20.cloned.1.call-done = f32[128,768]{1,0:T(8,128)} async-done(((f32[512,768]{1,0:T(8,128)}), f32[128,768]{1,0:T(8,128)}) %reduce-scatter.20.cloned.1.call-update) | async-done | bytes 393232 | tf_op jit(solution)/shard_map/reduce_scatter | solution.py:111
  499.1 4.0 all-to-all-start.7
  529.4 4.8 multiply_reduce_fusion.8
  547.0 6.8 all_to_all.62
  553.8 15.3 %all_gather.52 = bf16[512,768]{1,0:T(8,128)(2,1)S(1)} all-gather(bf16[128,768]{1,0:T(8,128)(2,1)S(1)} %bitcast.398), channel_id=1, replica_groups=mesh['section'=2,'expert'=4,'shard'=4] {'shard'}, dimensions={0}, use_global_device_ids=true | all-gather | bytes 983040 | tf_op jit(solution)/shard_map/all_gather | solution.py:95
  569.1 3.5 broadcast_select_fusion.2
  578.6 7.3 collective-permute-start.2
  587.5 26.4 %reduce-scatter.18.cloned.1.call-done = f32[128,768]{1,0:T(8,128)} async-done(((f32[512,768]{1,0:T(8,128)}), f32[128,768]{1,0:T(8,128)}) %reduce-scatter.18.cloned.1.call-update) | async-done | bytes 393232 | tf_op jit(solution)/shard_map/reduce_scatter | solution.py:99
  619.5 3.5 all-to-all-done.5
  627.5 3.8 all-to-all-start.8
  631.3 4.0 all-to-all-done.8
  635.2 14.8 %all_gather.54 = bf16[512,768]{1,0:T(8,128)(2,1)S(1)} all-gather(bf16[128,768]{1,0:T(8,128)(2,1)S(1)} %bitcast.395), channel_id=1, replica_groups=mesh['section'=2,'expert'=4,'shard'=4] {'shard'}, dimensions={0}, use_global_device_ids=true | all-gather | bytes 983040 | tf_op jit(solution)/shard_map/all_gather | solution.py:104
  650.0 4.3 broadcast_multiply_fusion.3
  662.1 34.3 %reduce-scatter.22.cloned.1.call-done = f32[128,768]{1,0:T(8,128)} async-done(((f32[512,768]{1,0:T(8,128)}), f32[128,768]{1,0:T(8,128)}) %reduce-scatter.22.cloned.1.call-update) | async-done | bytes 393232 | tf_op jit(solution)/shard_map/reduce_scatter | solution.py:111
  702.0 3.4 all-to-all-done.9
  717.1 4.1 multiply_reduce_fusion.7
  732.3 4.1 all-to-all-done.10
  736.5 15.4 %all_gather.55 = bf16[512,768]{1,0:T(8,128)(2,1)S(1)} all-gather(bf16[128,768]{1,0:T(8,128)(2,1)S(1)} %bitcast.394), channel_id=1, replica_groups=mesh['section'=2,'expert'=4,'shard'=4] {'shard'}, dimensions={0}, use_global_device_ids=true | all-gather | bytes 983040 | tf_op jit(solution)/shard_map/all_gather | solution.py:104
  751.9 4.3 broadcast_multiply_fusion.1
  768.5 26.4 %reduce-scatter.24.cloned.1.call-done = f32[128,768]{1,0:T(8,128)} async-done(((f32[512,768]{1,0:T(8,128)}), f32[128,768]{1,0:T(8,128)}) %reduce-scatter.24.cloned.1.call-update) | async-done | bytes 393232 | tf_op jit(solution)/shard_map/reduce_scatter | solution.py:111
  838.5 86.8 %reduce-scatter.34.cloned.1.call-done = f32[48,4]{1,0:T(8,128)} async-done(((f32[768,4]{1,0:T(8,128)}), f32[48,4]{1,0:T(8,128)}) %reduce-scatter.34.cloned.1.call-update) | async-done | bytes 784
  928.1 5.0 fusion.22
  933.3 3.5 fusion.27
  940.5 22.7 %scatter_custom_fusion = f32[127,12]{1,0:T(8,128)S(1)} fusion(s32[4096]{0:T(1024)} %copy-done.117, f32[4096,12]{1,0:T(8,128)} %bitcast.367, f32[]{:T(128)} %constant.71.clone.1), kind=kCustom, calls=%fused_computation.406 | custom fusion | flops 49152 | bytes 6608 | tf_op jit(solution)/shard_map/transpose(jvp())/scatter-add | solution.py:40
  966.7 61.7 %all-reduce.6 = (f32[768]{0:T(1024)S(1)}, f32[768]{0:T(1024)S(1)}, f32[384]{0:T(512)S(1)}) all-reduce(f32[768]{0:T(1024)S(1)} %multiply_add_fusion.2, f32[768]{0:T(1024)S(1)} %multiply_add_fusion.1, f32[384]{0:T(512)S(1)} %reshape.615), channel_id=16, replica_groups=mesh['section'=2,'expert'=4,'shard'=4] {'expert','shard'}, use_global_device_ids=true, to_apply=%region_63.64.clone | all-reduce | flops 1920 | bytes 15360
  1031.0 27.3 %reduce-scatter.32.cloned.1.call-done = f32[48,768]{1,0:T(8,128)} async-done(((f32[768,768]{1,0:T(8,128)}), f32[48,768]{1,0:T(8,128)}) %reduce-scatter.32.cloned.1.call-update) | async-done | bytes 147472 | tf_op jit(solution)/shard_map/reduce_scatter | solution.py:400
  1058.3 132.2 %reduce-scatter.30.cloned.1.call-done = f32[48,768]{1,0:T(8,128)} async-done(((f32[768,768]{1,0:T(8,128)}), f32[48,768]{1,0:T(8,128)}) %reduce-scatter.30.cloned.1.call-update) | async-done | bytes 147472 | tf_op jit(solution)/shard_map/reduce_scatter | solution.py:399
  1190.6 132.8 %reduce-scatter.28.cloned.1.call-done = f32[48,768]{1,0:T(8,128)} async-done(((f32[768,768]{1,0:T(8,128)}), f32[48,768]{1,0:T(8,128)}) %reduce-scatter.28.cloned.1.call-update) | async-done | bytes 147472 | tf_op jit(solution)/shard_map/reduce_scatter | solution.py:398
  1323.4 132.0 %reduce-scatter.26.cloned.1.call-done = f32[48,768]{1,0:T(8,128)} async-done(((f32[768,768]{1,0:T(8,128)}), f32[48,768]{1,0:T(8,128)}) %reduce-scatter.26.cloned.1.call-update) | async-done | bytes 147472 | tf_op jit(solution)/shard_map/reduce_scatter | solution.py:397
  (710 shorter events, 235.1 us)
Async XLA Ops:
  7.2 259.5 %copy-start = (bf16[1,1,768,768]{3,2,1,0:T(8,128)(2,1)S(1)}, bf16[1,1,768,768]{3,2,1,0:T(8,128)(2,1)}, u32[]{:S(2)}) copy-start(bf16[1,1,768,768]{3,2,1,0:T(8,128)(2,1)} %param.27) | copy-start | bytes 3538948
  7.2 65.3 %all-gather.13.cloned.1.call-start = ((), (), s32[]{:S(2)}) async-start(), calls=%async_computation.33 | async-start | bytes 1253376 | tf_op jit(solution)/shard_map/all_gather | solution.py:73
  7.9 117.7 %all-gather.15.cloned.1.call-start = ((), (), s32[]{:S(2)}) async-start(), calls=%async_computation.34 | async-start | bytes 1253376 | tf_op jit(solution)/shard_map/all_gather | solution.py:74
  8.7 174.8 %all-gather.17.cloned.1.call-start = ((), (), s32[]{:S(2)}) async-start(), calls=%async_computation.35 | async-start | bytes 1253376 | tf_op jit(solution)/shard_map/all_gather | solution.py:75
  9.4 231.7 %all-gather.19.cloned.1.call-start = ((), (), s32[]{:S(2)}) async-start(), calls=%async_computation.36 | async-start | bytes 1253376 | tf_op jit(solution)/shard_map/all_gather | solution.py:76
  10.0 304.4 %reduce-scatter.14.cloned.1.call-start = ((), (), s32[]{:S(2)}) async-start(), calls=%async_computation.23 | async-start | bytes 1966080 | tf_op jit(solution)/shard_map/reduce_scatter | solution.py:99
  13.5 256.2 %copy-start.143 = (s32[64]{0:T(128)}, s32[64]{0:T(128)S(1)}, u32[]{:S(2)}) copy-start(s32[64]{0:T(128)S(1)} %get-tuple-element.125) | copy-start | bytes 772
  13.5 312.5 %copy-start.145 = (s32[64]{0:T(128)}, s32[64]{0:T(128)S(1)}, u32[]{:S(2)}) copy-start(s32[64]{0:T(128)S(1)} %get-tuple-element.127) | copy-start | bytes 772
  13.5 413.0 %copy-start.135 = (s32[64]{0:T(128)}, s32[64]{0:T(128)S(1)}, u32[]{:S(2)}) copy-start(s32[64]{0:T(128)S(1)} %get-tuple-element.126) | copy-start | bytes 772
  53.3 667.9 %copy-start.115 = (f32[768]{0:T(1024)}, f32[768]{0:T(1024)S(1)}, u32[]{:S(2)}) copy-start(f32[768]{0:T(1024)S(1)} %convert_element_type.475) | copy-start | bytes 9220
  72.3 113.9 %copy-start.188 = (f32[64]{0:T(128)}, f32[64]{0:T(128)S(1)}, u32[]{:S(2)}) copy-start(f32[64]{0:T(128)S(1)} %add_rsqrt_fusion.5) | copy-start | bytes 772
  72.4 251.4 %copy-start.150 = (s32[64]{0:T(128)}, s32[64]{0:T(128)S(1)}, u32[]{:S(2)}) copy-start(s32[64]{0:T(128)S(1)} %multiply_add_fusion.11) | copy-start | bytes 772
  72.4 114.3 %copy-start.109 = (pred[64,64]{0,1:T(8,128)(4,1)}, pred[64,64]{0,1:T(8,128)(4,1)S(1)}, u32[]{:S(2)}) copy-start(pred[64,64]{0,1:T(8,128)(4,1)S(1)} %broadcast_compare_fusion.2) | copy-start | bytes 12292
  313.3 65.8 %copy-start.118 = (f32[64,4]{0,1:T(4,128)}, f32[64,4]{0,1:T(4,128)S(1)}, u32[]{:S(2)}) copy-start(f32[64,4]{0,1:T(4,128)S(1)} %get-tuple-element.139) | copy-start | bytes 3076
  316.0 7.7 all-to-all-start.1
  319.4 94.6 %reduce-scatter.16.cloned.1.call-start = ((), (), s32[]{:S(2)}) async-start(), calls=%async_computation.24 | async-start | bytes 1966080 | tf_op jit(solution)/shard_map/reduce_scatter | solution.py:99
  324.6 13.9 collective-permute-start
  338.7 238.1 %copy-start.21 = (bf16[64,768]{1,0:T(8,128)(2,1)}, bf16[64,768]{1,0:T(8,128)(2,1)S(1)}, u32[]{:S(2)}) copy-start(bf16[64,768]{1,0:T(8,128)(2,1)S(1)} %get-tuple-element.87) | copy-start | bytes 294916
  379.0 72.5 %copy-start.141 = (f32[64,4]{0,1:T(4,128)}, f32[64,4]{0,1:T(4,128)S(1)}, u32[]{:S(2)}) copy-start(f32[64,4]{0,1:T(4,128)S(1)} %get-tuple-element.145) | copy-start | bytes 3076
  379.6 71.9 %copy-start.139 = (f32[64,4]{0,1:T(4,128)}, f32[64,4]{0,1:T(4,128)S(1)}, u32[]{:S(2)}) copy-start(f32[64,4]{0,1:T(4,128)S(1)} %get-tuple-element.83) | copy-start | bytes 3076
  379.6 71.9 %copy-start.163 = (f32[64]{0:T(128)}, f32[64]{0:T(128)S(1)}, u32[]{:S(2)}) copy-start(f32[64]{0:T(128)S(1)} %get-tuple-element.82) | copy-start | bytes 772
  415.7 8.3 all-to-all-start.3
  428.7 8.1 all-to-all-start.6
  432.7 64.6 %reduce-scatter.20.cloned.1.call-start = ((), (), s32[]{:S(2)}) async-start(), calls=%async_computation.26 | async-start | bytes 1966080 | tf_op jit(solution)/shard_map/reduce_scatter | solution.py:111
  468.9 60.4 %collective-permute-start.1 = (bf16[64,768]{1,0:T(8,128)(2,1)}, bf16[64,768]{1,0:T(8,128)(2,1)}, u32[]{:S(2)}, u32[]{:S(2)}) collective-permute-start(bf16[64,768]{1,0:T(8,128)(2,1)} %get-tuple-element.70), channel_id=1, source_target_pairs={{0,16},{1,17},{2,18},{3,19},{4,20},{5,21},{6,22},{7,23},{8,24},{9,... | collective-permute-start | bytes 294920 | tf_op jit(solution)/shard_map/ppermute | solution.py:20
  499.1 8.1 all-to-all-start.7
  503.1 110.8 %reduce-scatter.18.cloned.1.call-start = ((), (), s32[]{:S(2)}) async-start(), calls=%async_computation.25 | async-start | bytes 1966080 | tf_op jit(solution)/shard_map/reduce_scatter | solution.py:99
  578.6 44.6 %collective-permute-start.2 = (bf16[64,768]{1,0:T(8,128)(2,1)}, bf16[64,768]{1,0:T(8,128)(2,1)S(1)}, u32[]{:S(2)}, u32[]{:S(2)}) collective-permute-start(bf16[64,768]{1,0:T(8,128)(2,1)} %fusion.200), channel_id=1, source_target_pairs={{16,0},{17,1},{18,2},{19,3},{20,4},{21,5},{22,6},{23,7},{24,8},{25... | collective-permute-start | bytes 294920 | tf_op jit(solution)/shard_map/ppermute | solution.py:20
  615.6 7.4 all-to-all-start.5
  627.5 7.8 all-to-all-start.8
  631.2 65.1 %reduce-scatter.22.cloned.1.call-start = ((), (), s32[]{:S(2)}) async-start(), calls=%async_computation.27 | async-start | bytes 1966080 | tf_op jit(solution)/shard_map/reduce_scatter | solution.py:111
  698.0 7.4 all-to-all-start.9
  723.0 103.2 %copy-start.35 = (bf16[64,768]{1,0:T(8,128)(2,1)}, bf16[64,768]{1,0:T(8,128)(2,1)S(1)}, u32[]{:S(2)}) copy-start(bf16[64,768]{1,0:T(8,128)(2,1)S(1)} %get-tuple-element.96) | copy-start | bytes 294916
  723.0 4.2 collective-permute-start.3
  728.9 7.6 all-to-all-start.10
  732.3 62.5 %reduce-scatter.24.cloned.1.call-start = ((), (), s32[]{:S(2)}) async-start(), calls=%async_computation.28 | async-start | bytes 1966080 | tf_op jit(solution)/shard_map/reduce_scatter | solution.py:111
  796.5 7.4 all-to-all-start.11
  799.9 125.4 %reduce-scatter.34.cloned.1.call-start = ((), (), s32[]{:S(2)}) async-start(), calls=%async_computation.37 | async-start | bytes 417792
  803.3 255.0 %reduce-scatter.32.cloned.1.call-start = ((), (), s32[]{:S(2)}) async-start(), calls=%async_computation.32 | async-start | bytes 2506752 | tf_op jit(solution)/shard_map/reduce_scatter | solution.py:400
  810.2 380.4 %reduce-scatter.30.cloned.1.call-start = ((), (), s32[]{:S(2)}) async-start(), calls=%async_computation.31 | async-start | bytes 2506752 | tf_op jit(solution)/shard_map/reduce_scatter | solution.py:399
  826.2 497.2 %reduce-scatter.28.cloned.1.call-start = ((), (), s32[]{:S(2)}) async-start(), calls=%async_computation.30 | async-start | bytes 2506752 | tf_op jit(solution)/shard_map/reduce_scatter | solution.py:398
  828.2 627.2 %reduce-scatter.26.cloned.1.call-start = ((), (), s32[]{:S(2)}) async-start(), calls=%async_computation.29 | async-start | bytes 2506752 | tf_op jit(solution)/shard_map/reduce_scatter | solution.py:397
  836.8 89.9 %copy-start.15 = (bf16[512,768]{1,0:T(8,128)(2,1)S(1)}, bf16[512,768]{1,0:T(8,128)(2,1)}, u32[]{:S(2)}) copy-start(bf16[512,768]{1,0:T(8,128)(2,1)} %copy-done.14) | copy-start | bytes 2359300
  837.6 89.2 %copy-start.76 = (bf16[512,768]{1,0:T(8,128)(2,1)S(1)}, bf16[512,768]{1,0:T(8,128)(2,1)}, u32[]{:S(2)}) copy-start(bf16[512,768]{1,0:T(8,128)(2,1)} %broadcast_multiply_fusion.4) | copy-start | bytes 2359300
  963.8 66.4 %copy-start.209 = (f32[64]{0:T(128)S(1)}, f32[64]{0:T(128)}, u32[]{:S(2)}) copy-start(f32[64]{0:T(128)} %get-tuple-element.25) | copy-start | bytes 772
  963.8 66.4 %copy-start.28 = (f32[64,768]{1,0:T(8,128)S(1)}, f32[64,768]{1,0:T(8,128)}, u32[]{:S(2)}) copy-start(f32[64,768]{1,0:T(8,128)} %copy-done.27) | copy-start | bytes 589828
  963.8 66.4 %copy-start.100 = (bf16[64,768]{1,0:T(8,128)(2,1)S(1)}, bf16[64,768]{1,0:T(8,128)(2,1)}, u32[]{:S(2)}) copy-start(bf16[64,768]{1,0:T(8,128)(2,1)} %copy-done.99) | copy-start | bytes 294916
  963.8 66.5 %copy-start.98 = (bf16[1,64,768]{2,1,0:T(8,128)(2,1)S(1)}, bf16[1,64,768]{2,1,0:T(8,128)(2,1)}, u32[]{:S(2)}) copy-start(bf16[1,64,768]{2,1,0:T(8,128)(2,1)} %get-tuple-element.55) | copy-start | bytes 294916
  (201 other events, 2169.7 us)
Sparse Core Ops, SparseCore 0:
  10.8 56.9 all-gather.12
  70.5 55.0 all-gather.14
  128.4 55.0 all-gather.16
  186.0 55.0 all-gather.18
  269.0 45.2 reduce-scatter.13
  378.1 35.8 reduce-scatter.15
  458.0 39.3 reduce-scatter.19
  576.2 37.6 reduce-scatter.17
  656.4 39.8 reduce-scatter.21
  758.3 36.4 reduce-scatter.23
  805.4 119.8 reduce-scatter.33
  931.4 126.8 reduce-scatter.31
  1063.8 126.7 reduce-scatter.29
  1196.7 126.6 reduce-scatter.27
  1328.7 126.6 reduce-scatter.25
where the time goes:
time: 1480 us; the launch traced here: 1460 us
  waiting for transfers between devices  871 us (59%)
  blocking collectives  252 us (17%)
  matrix products  110 us (7%)
  other arithmetic  88.9 us (6%)
  local copies, waits for them, and re-layouts  75.5 us (5%)
  starting transfers between devices  46.7 us (3%)
  between operations  19.3 us (1%)
    reduce_scatter x1, waiting for transfers between devices, body(): lax.psum_scatter(grad_key_full, ('expert', 'shard'), scatter_dimension=0,...  133 us
    reduce_scatter x1, waiting for transfers between devices, body(): lax.psum_scatter(grad_value_full, ('expert', 'shard'), scatter_dimension=...  132 us
    reduce_scatter x1, waiting for transfers between devices, body(): lax.psum_scatter(grad_query_full, ('expert', 'shard'), scatter_dimension=...  132 us
    unnamed x2, blocking collectives  98.9 us
    unnamed x16, waiting for transfers between devices  89.5 us
    reduce_scatter x3, waiting for transfers between devices, expert_backward(): lax.psum_scatter(grad_in_rows, 'shard', scatter_dimension=0, tiled=True)  87.2 us
    reduce_scatter x3, waiting for transfers between devices, expert_forward(): lax.psum_scatter(partial_value, 'shard', scatter_dimension=0, tiled=True)  61.7 us
    all_gather x1, waiting for transfers between devices, body(): lax.all_gather(w_value[0], ('expert', 'shard'), axis=0, tiled=True)  57.8 us
  transfers between devices with their start and end apart: 28, of which 25 were waited for; matrix products, arithmetic and copies ran while one was open for 11% of the time, Pallas kernels for 0%

commit v1 on v0

v1 whole, which is shorter than its diff:
```python
import math

import jax
import jax.numpy as jnp
from jax import lax
from jax.sharding import PartitionSpec as P

HEADS = 12
HEAD_DIM = 64
NB = 32
EXT = 128
EPSILON = 1e-06
MASK_FILL = -1e30
BF = jnp.bfloat16
F32 = jnp.float32


def dot(a, b):
    return jnp.dot(a, b, preferred_element_type=F32)


def dot_t(a, b):
    return lax.dot_general(a, b, (((1,), (1,)), ((), ())), preferred_element_type=F32)


def t_dot(a, b):
    return lax.dot_general(a, b, (((0,), (0,)), ((), ())), preferred_element_type=F32)


def swap(value):
    return lax.ppermute(value, "section", [(0, 1), (1, 0)])


def direct(axis):
    count = lax.axis_size(axis)
    return count <= 4 and count & (count - 1) == 0


def peer_ids(axis):
    count = lax.axis_size(axis)
    ids = jnp.arange(count, dtype=jnp.int32)
    return ids ^ lax.axis_index(axis) if direct(axis) else ids


def hop(value, axis, step):
    count = lax.axis_size(axis)
    return lax.ppermute(value, axis, [(i, i ^ step) for i in range(count)])


def spread(value, axis):
    count = lax.axis_size(axis)
    if direct(axis):
        return [value] + [hop(value, axis, step) for step in range(1, count)]
    every = lax.all_gather(value, axis, axis=0)
    return [every[i] for i in range(count)]


def exchange(blocks, axis):
    count = lax.axis_size(axis)
    if direct(axis):
        return [blocks[0]] + [hop(blocks[step], axis, step) for step in range(1, count)]
    swapped = lax.all_to_all(jnp.stack(blocks), axis, 0, 0, tiled=True)
    return [swapped[i] for i in range(count)]


def ordered(pieces, axis):
    count = len(pieces)
    ids = peer_ids(axis)
    rows = pieces[0].shape[0]
    joined = jnp.zeros((count * rows,) + pieces[0].shape[1:], pieces[0].dtype)
    for place in range(count):
        joined = lax.dynamic_update_slice(joined, pieces[place], (ids[place] * rows, 0))
    return joined


def gather_rows(part):
    if direct("expert") and direct("shard"):
        plane = ordered(spread(part, "shard"), "shard")
        return ordered(spread(plane, "expert"), "expert")
    return lax.all_gather(part, ("expert", "shard"), axis=0, tiled=True)


def scatter_rows(whole):
    for axis in ("expert", "shard"):
        count = lax.axis_size(axis)
        rows = whole.shape[0] // count
        ids = peer_ids(axis)
        blocks = [
            lax.dynamic_slice_in_dim(whole, ids[i] * rows, rows, axis=0).astype(BF)
            for i in range(count)
        ]
        whole = sum(block.astype(F32) for block in exchange(blocks, axis))
    return whole


def inverse_rms(value):
    return lax.rsqrt(jnp.mean(value * value, axis=-1, keepdims=True) + EPSILON)


def norm_back(value, gain, grad):
    scale = inverse_rms(value)
    scaled = value * scale
    gained = grad * gain
    back = scale * (gained - scaled * jnp.mean(gained * scaled, axis=-1, keepdims=True))
    return back, jnp.sum(grad * scaled, axis=0)


def gelu_parts(value):
    c = math.sqrt(2.0 / math.pi)
    inner = jnp.tanh(c * (value + 0.044715 * value * value * value))
    grad = 0.5 * (1.0 + inner) + 0.5 * value * (1.0 - inner * inner) * (
        c * (1.0 + 3.0 * 0.044715 * value * value)
    )
    return 0.5 * value * (1.0 + inner), grad


def body(
    feed, segments, routes, rel_bucket, gain_attn, gain_ffn, w_query, w_key, w_value, w_out_attn,
    rel_table, router, expert_in, expert_out,
):
    seq = feed.shape[2]
    width = feed.shape[3]
    experts = lax.axis_size("expert")
    shards = lax.axis_size("shard")
    cap = max(2, 2 * seq // experts)
    own_rows = w_query.shape[1]
    sec = lax.axis_index("section")
    first = sec == 0
    score_scale = 1.0 / math.sqrt(HEAD_DIM)

    table_rows = rel_table.shape[1]
    ext = jnp.concatenate(
        [
            gain_attn[0][:, None],
            gain_ffn[0][:, None],
            jnp.pad(rel_table[0], (0, own_rows - table_rows))[:, None],
            router[0],
            jnp.zeros((own_rows, EXT - 3 - experts), BF),
        ],
        axis=1,
    )
    half_a = jnp.concatenate([w_query[0], w_key[0], ext], axis=1)
    half_b = jnp.concatenate([w_value[0], w_out_attn[0], ext], axis=1)
    came = swap(jnp.where(first, half_b, half_a))
    parts = [jnp.where(first, half_a, came), jnp.where(first, came, half_b)]

    came = swap(jnp.where(first, feed[0, 1], feed[0, 0]))
    layer_x = jnp.where(first, feed[0, 0], came)
    layer_dy = jnp.where(first, came, feed[0, 1])
    came = swap(jnp.where(first, routes[0, 1, 0], routes[0, 0, 0]))
    kept = jnp.where(first, routes[0, 0, 0], routes[0, 1, 0])
    my_routes = jnp.stack([jnp.where(first, kept, came), jnp.where(first, came, kept)])
    seg_ids = jnp.where(first, segments[0, 0], segments[1, 0])
    came_in = swap(expert_in[0, 0])
    came_out = swap(expert_out[0, 0])
    w_in = [jnp.where(first, expert_in[0, 0], came_in), jnp.where(first, came_in, expert_in[0, 0])]
    w_out = [
        jnp.where(first, expert_out[0, 0], came_out),
        jnp.where(first, came_out, expert_out[0, 0]),
    ]

    all_routes = jnp.stack(spread(my_routes, "shard"), axis=1)
    hot = (all_routes[..., None] == peer_ids("expert")).astype(BF)
    positions = jnp.arange(seq, dtype=jnp.int32)
    before = (positions[:, None] > positions[None, :]).astype(BF)
    rank = jnp.einsum("ij,lzje->lzie", before, hot, preferred_element_type=F32)
    slot_in = jnp.arange(cap, dtype=jnp.int32).astype(F32)
    dispatch = (hot[..., None] * (rank[..., None] == slot_in).astype(BF)).reshape(
        2, shards, seq, experts * cap
    )
    chosen = (my_routes[..., None] == jnp.arange(experts, dtype=jnp.int32)).astype(F32)
    bucket_ij = jnp.stack([rel_bucket[seq - 1 - i : 2 * seq - 1 - i] for i in range(seq)])
    bucket_hot = (
        bucket_ij.reshape(1, seq * seq) == jnp.arange(NB, dtype=jnp.int32)[:, None]
    ).astype(BF)
    same_doc = seg_ids[:, None] == seg_ids[None, :]

    weights = []
    for layer in range(2):
        mine = gather_rows(parts[layer])
        other = swap(mine)
        whole_a = jnp.where(first, mine, other)
        whole_b = jnp.where(first, other, mine)
        side = whole_a[:, 2 * width :]
        table = side[:, 2].reshape(-1, own_rows)[:, :table_rows].reshape(NB, HEADS)
        weights.append(
            dict(
                qkv=jnp.concatenate([whole_a[:, : 2 * width], whole_b[:, :width]], axis=1),
                out=whole_b[:, width : 2 * width],
                gain_one=side[:, 0].astype(F32),
                gain_two=side[:, 1].astype(F32),
                router=side[:, 3 : 3 + experts],
                bias=t_dot(table, bucket_hot).reshape(HEADS, seq, seq),
            )
        )

    def to_experts(layer, tokens):
        every = jnp.stack(spread(tokens, "shard"))
        slots = jnp.einsum("zsc,zsd->czd", dispatch[layer], every, preferred_element_type=F32)
        slots = slots.astype(BF).reshape(experts, cap * shards, width)
        return jnp.concatenate(exchange([slots[i] for i in range(experts)], "expert"), axis=0)

    def to_tokens(layer, rows):
        rows = rows.astype(BF).reshape(experts, cap * shards, width)
        back = jnp.stack(exchange([rows[i] for i in range(experts)], "expert"))
        back = back.reshape(experts * cap, shards, width)
        tokens = jnp.einsum("zsc,czd->zsd", dispatch[layer], back, preferred_element_type=F32)
        tokens = tokens.astype(BF)
        return sum(
            piece.astype(F32) for piece in exchange([tokens[i] for i in range(shards)], "shard")
        )

    def heads(value):
        return value.reshape(seq, HEADS, HEAD_DIM)

    def forward(layer, x_low):
        w = weights[layer]
        x = x_low.astype(F32)
        normed_one = (x * inverse_rms(x) * w["gain_one"]).astype(BF)
        qkv = dot(normed_one, w["qkv"]).astype(BF)
        queries, keys_all, values = [heads(qkv[:, i * width : (i + 1) * width]) for i in range(3)]
        scores = jnp.einsum("qhd,khd->hqk", queries, keys_all, preferred_element_type=F32)
        scores = jnp.where(same_doc[None], scores * score_scale + w["bias"], MASK_FILL)
        exp_scores = jnp.exp(scores - jnp.max(scores, axis=-1, keepdims=True))
        probs = exp_scores / jnp.sum(exp_scores, axis=-1, keepdims=True)
        context = jnp.einsum("hqk,khd->qhd", probs.astype(BF), values, preferred_element_type=F32)
        context = context.reshape(seq, width).astype(BF)
        hidden = x + dot(context, w["out"])
        normed_two = (hidden * inverse_rms(hidden) * w["gain_two"]).astype(BF)
        gates = jax.nn.softmax(dot(normed_two, w["router"]), axis=-1)
        gate_value = jnp.sum(gates * chosen[layer], axis=-1, keepdims=True)
        rows = to_experts(layer, normed_two)
        pre_act = dot(rows, w_in[layer])
        activated = gelu_parts(pre_act)[0].astype(BF)
        expert_tok = to_tokens(layer, dot(activated, w_out[layer])).astype(BF).astype(F32)
        out = (hidden + gate_value * expert_tok).astype(BF)
        return out, (
            x, normed_one, queries, keys_all, values, probs, context, hidden, normed_two, gates,
            gate_value, rows, pre_act, activated, expert_tok,
        )

    def backward(layer, dy_low, state):
        (
            x, normed_one, queries, keys_all, values, probs, context, hidden, normed_two, gates,
            gate_value, rows, pre_act, activated, expert_tok,
        ) = state
        w = weights[layer]
        dy = dy_low.astype(F32)
        grad_gate = jnp.sum(dy * expert_tok, axis=-1, keepdims=True)
        spread_rows = to_experts(layer, (gate_value * dy).astype(BF))
        grad_act = dot_t(spread_rows, w_out[layer])
        grad_pre = (grad_act * gelu_parts(pre_act)[1]).astype(BF)
        grad_rows = to_tokens(layer, dot_t(grad_pre, w_in[layer]))
        grad_in = t_dot(rows, grad_pre)
        grad_out = t_dot(activated, spread_rows)
        grad_logits = (grad_gate * gate_value * (chosen[layer] - gates)).astype(BF)
        grad_norm_two = grad_rows.astype(BF).astype(F32) + dot_t(grad_logits, w["router"])
        back, grad_gain_two = norm_back(hidden, w["gain_two"], grad_norm_two)
        grad_hidden = dy + back
        grad_hidden_low = grad_hidden.astype(BF)
        grad_context = heads(dot_t(grad_hidden_low, w["out"]).astype(BF))
        grad_probs = jnp.einsum("qhd,khd->hqk", grad_context, values, preferred_element_type=F32)
        grad_scores = probs * (grad_probs - jnp.sum(probs * grad_probs, axis=-1, keepdims=True))
        grad_scores = grad_scores.astype(BF)
        grad_q = jnp.einsum("hqk,khd->qhd", grad_scores, keys_all, preferred_element_type=F32)
        grad_k = jnp.einsum("hqk,qhd->khd", grad_scores, queries, preferred_element_type=F32)
        grad_v = jnp.einsum(
            "hqk,qhd->khd", probs.astype(BF), grad_context, preferred_element_type=F32
        )
        grad_joint = jnp.concatenate(
            [
                (grad_q * score_scale).reshape(seq, width),
                (grad_k * score_scale).reshape(seq, width),
                grad_v.reshape(seq, width),
            ],
            axis=1,
        ).astype(BF)
        grad_normed = dot_t(grad_joint, w["qkv"])
        back, grad_gain_one = norm_back(x, w["gain_one"], grad_normed)
        dx = (grad_hidden + back).astype(BF)
        grad_table = dot_t(bucket_hot, grad_scores.reshape(HEADS, seq * seq))
        grad_table = jnp.pad(
            grad_table.reshape(-1, table_rows), ((0, 0), (0, own_rows - table_rows))
        ).reshape(width, 1)
        side = jnp.concatenate(
            [
                grad_gain_one[:, None],
                grad_gain_two[:, None],
                grad_table,
                t_dot(normed_two, grad_logits),
                jnp.zeros((width, EXT - 3 - experts), F32),
            ],
            axis=1,
        ).astype(BF)
        grad_qkv = t_dot(normed_one, grad_joint).astype(BF)
        grad_attn = t_dot(context, grad_hidden_low).astype(BF)
        grad_a = jnp.concatenate([grad_qkv[:, : 2 * width], side], axis=1)
        grad_b = jnp.concatenate([grad_qkv[:, 2 * width :], grad_attn, jnp.zeros_like(side)], axis=1)
        kept = jnp.where(first, grad_a, grad_b).astype(F32)
        summed = kept + swap(jnp.where(first, grad_b, grad_a)).astype(F32)
        return dx, scatter_rows(summed), (grad_in, grad_out)

    out_zero, state_zero = forward(0, layer_x)
    out_one, state_one = forward(1, out_zero)
    dx_one, sum_one, experts_one = backward(1, layer_dy, state_one)
    dx_zero, sum_zero, experts_zero = backward(0, dx_one, state_zero)

    came = swap(jnp.where(first, sum_one, sum_zero))
    kept = jnp.where(first, sum_zero, sum_one)
    final_a = jnp.where(first, kept, came)
    final_b = jnp.where(first, came, kept)

    def own_expert(zero, one):
        return jnp.where(first, zero, one) + swap(jnp.where(first, one, zero).astype(BF)).astype(F32)

    def by_batch(zero, one):
        came = swap(jnp.where(first, one, zero))
        kept = jnp.where(first, zero, one)
        return jnp.stack([jnp.where(first, kept, came), jnp.where(first, came, kept)])

    side = final_a[:, 2 * width :]
    return (
        by_batch(out_zero, out_one)[None],
        by_batch(dx_zero, dx_one)[None],
        side[:, 0][None],
        side[:, 1][None],
        final_a[:, :width][None],
        final_a[:, width : 2 * width][None],
        final_b[:, :width][None],
        final_b[:, width : 2 * width][None],
        side[:table_rows, 2][None],
        side[:, 3 : 3 + experts][None],
        own_expert(experts_zero[0], experts_one[0])[None, None],
        own_expert(experts_zero[1], experts_one[1])[None, None],
    )


def solution(mesh):
    rows = ("expert", "shard")
    tokens = P("section", None, rows, None)
    matrix = P("section", rows, None)
    vector = P("section", rows)
    expert_specs = (P("section", "expert", None, "shard"), P("section", "expert", "shard", None))
    in_specs = (
        tokens, P(None, rows, None), tokens, P(), vector, vector, matrix, matrix, matrix, matrix,
        vector, matrix, *expert_specs,
    )
    out_specs = (
        tokens, tokens, vector, vector, matrix, matrix, matrix, matrix, vector, matrix,
        *expert_specs,
    )
    return jax.shard_map(body, mesh=mesh, in_specs=in_specs, out_specs=out_specs, check_vma=False)
```

time: 1480 us -> 580 us (0.39)
  waiting for transfers between devices: 871 us -> 155 us
  blocking collectives: 252 us -> 0 us
  starting transfers between devices: 46.7 us -> 129 us
  local copies, waits for them, and re-layouts: 75.5 us -> 153 us
  other arithmetic: 88.9 us -> 34.8 us
  matrix products: 110 us -> 87.2 us
    reduce_scatter x10 -> x0, waiting for transfers between devices: 573 us -> none  [the longest x1 133 us: body(): lax.psum_scatter(grad_key_full, ('expert', 'shard'), scatter_dimension=0,...]
    all_gather x4 -> x0, waiting for transfers between devices: 164 us -> none  [the longest x1 57.8 us: body(): lax.all_gather(w_value[0], ('expert', 'shard'), axis=0, tiled=True)]
    ppermute x4 -> x89, waiting for transfers between devices: 13.5 us -> 155 us  [the longest x75 148 us: hop(): return lax.ppermute(value, axis, [(i, i ^ step) for i in range(count)])]
    all_gather x7 -> x0, blocking collectives: 132 us -> none  [the longest x3 45.4 us: expert_forward(): in_rows = lax.all_gather(expert_rows, 'shard', axis=0, tiled=True)]
    ppermute x4 -> x89, starting transfers between devices: 13.1 us -> 129 us  [the longest x75 95.8 us: hop(): return lax.ppermute(value, axis, [(i, i ^ step) for i in range(count)])]
    unnamed x2 -> x0, blocking collectives: 98.9 us -> none
    unnamed x16 -> x0, waiting for transfers between devices: 89.5 us -> none
    slice x3 -> x41, local copies, waits for them, and re-layouts: 0.76 us -> 44.2 us  [the longest x20 24.8 us: to_experts(): slots[i]]
  transfers between devices with their start and end apart: 28 -> 89, of which waited for: 25 -> 28; matrix products, arithmetic and copies ran while one was open for 11% -> 29% of each run, Pallas kernels for 0% -> 0%
where the time goes in v1:
time: 580 us; the launch traced here: 568 us
  waiting for transfers between devices  155 us (27%)
  local copies, waits for them, and re-layouts  153 us (26%)
  starting transfers between devices  129 us (22%)
  matrix products  87.2 us (15%)
  other arithmetic  34.8 us (6%)
  between operations  8.56 us (1%)
    ppermute x75, waiting for transfers between devices, hop(): return lax.ppermute(value, axis, [(i, i ^ step) for i in range(count)])  148 us
    ppermute x75, starting transfers between devices, hop(): return lax.ppermute(value, axis, [(i, i ^ step) for i in range(count)])  95.8 us
    ppermute x14, starting transfers between devices, swap(): return lax.ppermute(value, 'section', [(0, 1), (1, 0)])  33.5 us
    dot_general x12, matrix products, dot_t(): lax.dot_general(a, b, (((1,), (1,)), ((), ())), preferred_element_type=F32)  26.9 us
    slice x20, local copies, waits for them, and re-layouts, to_experts(): slots[i]  24.8 us
    squeeze x16, local copies, waits for them, and re-layouts, to_experts(): slots[i]  22.4 us
    unnamed x260, local copies, waits for them, and re-layouts  21 us
    dot_general x10, matrix products, dot(): return jnp.dot(a, b, preferred_element_type=F32)  18.5 us
  transfers between devices with their start and end apart: 89, of which 28 were waited for; matrix products, arithmetic and copies ran while one was open for 29% of the time, Pallas kernels for 0%

profile of v1, /device:TPU:1, one launch (start us, length us, event | category | flops | bytes accessed | tf_op | source)
XLA Modules:
  0.0 567.9 jit_solution(1257054636871930178)
XLA Ops:
  15.9 2.8 collective-permute-start.10
  22.2 3.0 collective-permute-done.12
  26.5 2.7 collective-permute-start.4
  29.1 2.6 collective-permute-done.2
  31.8 6.2 %collective-permute-done.3 = bf16[48,1664]{1,0:T(8,128)(2,1)S(1)} collective-permute-done((bf16[48,1664]{1,0:T(8,128)(2,1)S(1)}, bf16[48,1664]{1,0:T(8,128)(2,1)S(1)}, u32[]{:S(2)}, u32[]{:S(2)}) %collective-permute-start.3) | collective-permute-done | bytes 159776 | tf_op jit(solution)/shard_map/ppermute | solution.py:47
  41.3 9.2 %collective-permute-done.5 = bf16[192,1664]{1,0:T(8,128)(2,1)S(1)} collective-permute-done((bf16[192,1664]{1,0:T(8,128)(2,1)S(1)}, bf16[192,1664]{1,0:T(8,128)(2,1)S(1)}, u32[]{:S(2)}, u32[]{:S(2)}) %collective-permute-start.5) | collective-permute-done | bytes 639008 | tf_op jit(solution)/shard_map/ppermute | solution.py:47
  51.6 13.6 %collective-permute-done.7 = bf16[192,1664]{1,0:T(8,128)(2,1)S(1)} collective-permute-done((bf16[192,1664]{1,0:T(8,128)(2,1)S(1)}, bf16[192,1664]{1,0:T(8,128)(2,1)S(1)}, u32[]{:S(2)}, u32[]{:S(2)}) %collective-permute-start.7) | collective-permute-done | bytes 639008 | tf_op jit(solution)/shard_map/ppermute | solution.py:47
  65.2 4.9 collective-permute-start.8
  70.2 3.7 collective-permute-start.27
  74.7 4.9 collective-permute-done.27
  81.7 6.2 %collective-permute-done.28 = bf16[48,1664]{1,0:T(8,128)(2,1)S(1)} collective-permute-done((bf16[48,1664]{1,0:T(8,128)(2,1)S(1)}, bf16[48,1664]{1,0:T(8,128)(2,1)S(1)}, u32[]{:S(2)}, u32[]{:S(2)}) %collective-permute-start.28) | collective-permute-done | bytes 159776 | tf_op jit(solution)/shard_map/ppermute | solution.py:47
  93.5 8.6 %collective-permute-done.30 = bf16[192,1664]{1,0:T(8,128)(2,1)S(1)} collective-permute-done((bf16[192,1664]{1,0:T(8,128)(2,1)S(1)}, bf16[192,1664]{1,0:T(8,128)(2,1)S(1)}, u32[]{:S(2)}, u32[]{:S(2)}) %collective-permute-start.30) | collective-permute-done | bytes 639008 | tf_op jit(solution)/shard_map/ppermute | solution.py:47
  102.1 5.1 collective-permute-start.20
  108.9 7.8 %collective-permute-done.32 = bf16[192,1664]{1,0:T(8,128)(2,1)S(1)} collective-permute-done((bf16[192,1664]{1,0:T(8,128)(2,1)S(1)}, bf16[192,1664]{1,0:T(8,128)(2,1)S(1)}, u32[]{:S(2)}, u32[]{:S(2)}) %collective-permute-start.32) | collective-permute-done | bytes 639008 | tf_op jit(solution)/shard_map/ppermute | solution.py:47
  117.6 2.8 collective-permute-start.33
  133.5 3.7 collective-permute-start.13
  139.4 3.0 broadcast_select_fusion.3
  154.2 3.2 slice.779
  165.1 6.6 %collective-permute-done.17 = bf16[128,768]{1,0:T(8,128)(2,1)} collective-permute-done((bf16[128,768]{1,0:T(8,128)(2,1)}, bf16[128,768]{1,0:T(8,128)(2,1)}, u32[]{:S(2)}, u32[]{:S(2)}) %collective-permute-start.17) | collective-permute-done | bytes 196640 | tf_op jit(solution)/shard_map/ppermute | solution.py:47
  172.7 2.7 fusion.55
  175.4 3.7 convolution_convert_fusion.9
  187.2 3.6 collective-permute-done.23
  199.1 5.9 %collective-permute-done.25 = bf16[64,768]{1,0:T(8,128)(2,1)S(1)} collective-permute-done((bf16[64,768]{1,0:T(8,128)(2,1)S(1)}, bf16[64,768]{1,0:T(8,128)(2,1)S(1)}, u32[]{:S(2)}, u32[]{:S(2)}) %collective-permute-start.25) | collective-permute-done | bytes 98336 | tf_op jit(solution)/shard_map/ppermute | solution.py:47
  268.2 2.9 convolution_convert_fusion.8
  275.9 3.1 fusion.13
  291.5 7.6 %collective-permute-start.43 = (bf16[64,768]{1,0:T(8,128)(2,1)}, bf16[64,768]{1,0:T(8,128)(2,1)}, u32[]{:S(2)}, u32[]{:S(2)}) collective-permute-start(bf16[64,768]{1,0:T(8,128)(2,1)} %get-tuple-element.140), channel_id=1, source_target_pairs={{0,1},{1,0},{2,3},{3,2},{4,5},{5,4},{6,7},{7,6},{8,9},{9,8},{10,11... | collective-permute-start | bytes 294920 | tf_op jit(solution)/shard_map/ppermute | solution.py:47
  312.7 4.5 collective-permute-done.57
  327.4 3.1 fusion.113
  367.8 4.0 fusion.19
  371.7 2.8 convolution_convert_fusion.6
  382.4 2.6 reshape.417
  401.7 3.8 concatenate.65
  423.4 4.1 convolution_convert_fusion.1
  427.5 2.5 fusion.105
  430.8 3.2 slice.827
  442.2 5.3 concatenate.63
  447.5 4.0 broadcast_select_fusion
  451.5 9.4 %collective-permute-start.72 = (bf16[768,1664]{1,0:T(8,128)(2,1)S(1)}, bf16[768,1664]{1,0:T(8,128)(2,1)S(1)}, u32[]{:S(2)}, u32[]{:S(2)}) collective-permute-start(bf16[768,1664]{1,0:T(8,128)(2,1)S(1)} %get-tuple-element.165), channel_id=1, source_target_pairs={{0,16},{16,0},{1,17},{17,1},{2,18},{18,2},{3,19},{19,3},{4,20},{20... | collective-permute-start | bytes 7667720 | tf_op jit(solution)/shard_map/ppermute | solution.py:31
  461.6 7.5 %collective-permute-done.46 = bf16[64,768]{1,0:T(8,128)(2,1)S(1)} collective-permute-done((bf16[64,768]{1,0:T(8,128)(2,1)S(1)}, bf16[64,768]{1,0:T(8,128)(2,1)S(1)}, u32[]{:S(2)}, u32[]{:S(2)}) %collective-permute-start.46) | collective-permute-done | bytes 98336 | tf_op jit(solution)/shard_map/ppermute | solution.py:31
  476.6 2.6 convert_add_fusion
  484.8 10.4 %collective-permute-done.80 = bf16[192,1664]{1,0:T(8,128)(2,1)S(1)} collective-permute-done((bf16[192,1664]{1,0:T(8,128)(2,1)S(1)}, bf16[192,1664]{1,0:T(8,128)(2,1)S(1)}, u32[]{:S(2)}, u32[]{:S(2)}) %collective-permute-start.80) | collective-permute-done | bytes 639008 | tf_op jit(solution)/shard_map/ppermute | solution.py:47
  497.2 12.4 %collective-permute-done.82 = bf16[192,1664]{1,0:T(8,128)(2,1)S(1)} collective-permute-done((bf16[192,1664]{1,0:T(8,128)(2,1)S(1)}, bf16[192,1664]{1,0:T(8,128)(2,1)S(1)}, u32[]{:S(2)}, u32[]{:S(2)}) %collective-permute-start.82) | collective-permute-done | bytes 639008 | tf_op jit(solution)/shard_map/ppermute | solution.py:47
  511.6 11.0 %collective-permute-done.73 = bf16[192,1664]{1,0:T(8,128)(2,1)S(1)} collective-permute-done((bf16[192,1664]{1,0:T(8,128)(2,1)S(1)}, bf16[192,1664]{1,0:T(8,128)(2,1)S(1)}, u32[]{:S(2)}, u32[]{:S(2)}) %collective-permute-start.73) | collective-permute-done | bytes 639008 | tf_op jit(solution)/shard_map/ppermute | solution.py:47
  524.6 12.4 %collective-permute-done.75 = bf16[192,1664]{1,0:T(8,128)(2,1)S(1)} collective-permute-done((bf16[192,1664]{1,0:T(8,128)(2,1)S(1)}, bf16[192,1664]{1,0:T(8,128)(2,1)S(1)}, u32[]{:S(2)}, u32[]{:S(2)}) %collective-permute-start.75) | collective-permute-done | bytes 639008 | tf_op jit(solution)/shard_map/ppermute | solution.py:47
  544.6 4.8 collective-permute-done.76
  549.4 2.5 collective-permute-done.77
  551.9 2.9 collective-permute-done.78
  555.0 7.7 %collective-permute-start.86 = (f32[48,1664]{1,0:T(8,128)S(1)}, f32[48,1664]{1,0:T(8,128)S(1)}, u32[]{:S(2)}, u32[]{:S(2)}) collective-permute-start(f32[48,1664]{1,0:T(8,128)S(1)} %get-tuple-element.62), channel_id=1, source_target_pairs={{0,16},{16,0},{1,17},{17,1},{2,18},{18,2},{3,19},{19,3},{4,20},{20... | collective-permute-start | bytes 958472 | tf_op jit(solution)/shard_map/ppermute | solution.py:31
  (667 shorter events, 305.9 us)
Async XLA Ops:
  5.8 19.4 %collective-permute-start.1 = (bf16[48,1664]{1,0:T(8,128)(2,1)S(1)}, bf16[48,1664]{1,0:T(8,128)(2,1)S(1)}, u32[]{:S(2)}, u32[]{:S(2)}) collective-permute-start(bf16[48,1664]{1,0:T(8,128)(2,1)S(1)} %broadcast_select_fusion.24), channel_id=1, source_target_pairs={{0,16},{16,0},{1,17},{17,1},{2,18},{18,2},{3,19},{19,3},{4,20},{20... | collective-permute-start | bytes 479240 | tf_op jit(solution)/shard_map/ppermute | solution.py:31
  6.9 81.9 %collective-permute-start = (bf16[64,768]{1,0:T(8,128)(2,1)S(1)}, bf16[64,768]{1,0:T(8,128)(2,1)S(1)}, u32[]{:S(2)}, u32[]{:S(2)}) collective-permute-start(bf16[64,768]{1,0:T(8,128)(2,1)S(1)} %bitcast_select_fusion.1), channel_id=1, source_target_pairs={{0,16},{16,0},{1,17},{17,1},{2,18},{18,2},{3,19},{19,3},{4,20},{20... | collective-permute-start | bytes 294920 | tf_op jit(solution)/shard_map/ppermute | solution.py:31
  21.6 151.1 %collective-permute-start.19 = (bf16[768,768]{1,0:T(8,128)(2,1)}, bf16[768,768]{1,0:T(8,128)(2,1)}, u32[]{:S(2)}, u32[]{:S(2)}) collective-permute-start(bf16[768,768]{1,0:T(8,128)(2,1)} %bitcast.106), channel_id=1, source_target_pairs={{0,16},{16,0},{1,17},{17,1},{2,18},{18,2},{3,19},{19,3},{4,20},{20... | collective-permute-start | bytes 3538952 | tf_op jit(solution)/shard_map/ppermute | solution.py:31
  25.6 12.4 %collective-permute-start.3 = (bf16[48,1664]{1,0:T(8,128)(2,1)S(1)}, bf16[48,1664]{1,0:T(8,128)(2,1)S(1)}, u32[]{:S(2)}, u32[]{:S(2)}) collective-permute-start(bf16[48,1664]{1,0:T(8,128)(2,1)S(1)} %get-tuple-element.81), channel_id=1, source_target_pairs={{0,2},{1,3},{2,0},{3,1},{4,6},{5,7},{6,4},{7,5},{8,10},{9,11},{10,... | collective-permute-start | bytes 479240 | tf_op jit(solution)/shard_map/ppermute | solution.py:47
  38.0 12.4 %collective-permute-start.5 = (bf16[192,1664]{1,0:T(8,128)(2,1)S(1)}, bf16[192,1664]{1,0:T(8,128)(2,1)S(1)}, u32[]{:S(2)}, u32[]{:S(2)}) collective-permute-start(bf16[192,1664]{1,0:T(8,128)(2,1)S(1)} %constant_dynamic-update-slice_fusion.28), channel_id=1, source_target_pairs={{0,4},{4,0},{8,12},{12,8},{1,5},{5,1},{9,13},{13,9},{2,6},{6,2},{1... | collective-permute-start | bytes 1916936 | tf_op jit(solution)/shard_map/ppermute | solution.py:47
  40.8 24.4 %collective-permute-start.7 = (bf16[192,1664]{1,0:T(8,128)(2,1)S(1)}, bf16[192,1664]{1,0:T(8,128)(2,1)S(1)}, u32[]{:S(2)}, u32[]{:S(2)}) collective-permute-start(bf16[192,1664]{1,0:T(8,128)(2,1)S(1)} %constant_dynamic-update-slice_fusion.28), channel_id=1, source_target_pairs={{0,12},{4,8},{8,4},{12,0},{1,13},{5,9},{9,5},{13,1},{2,14},{6,10},... | collective-permute-start | bytes 1916936 | tf_op jit(solution)/shard_map/ppermute | solution.py:47
  65.2 55.2 %collective-permute-start.8 = (bf16[768,1664]{1,0:T(8,128)(2,1)S(1)}, bf16[768,1664]{1,0:T(8,128)(2,1)S(1)}, u32[]{:S(2)}, u32[]{:S(2)}) collective-permute-start(bf16[768,1664]{1,0:T(8,128)(2,1)S(1)} %constant_dynamic-update-slice_fusion.24), channel_id=1, source_target_pairs={{0,16},{16,0},{1,17},{17,1},{2,18},{18,2},{3,19},{19,3},{4,20},{20... | collective-permute-start | bytes 7667720 | tf_op jit(solution)/shard_map/ppermute | solution.py:31
  74.7 13.2 %collective-permute-start.28 = (bf16[48,1664]{1,0:T(8,128)(2,1)S(1)}, bf16[48,1664]{1,0:T(8,128)(2,1)S(1)}, u32[]{:S(2)}, u32[]{:S(2)}) collective-permute-start(bf16[48,1664]{1,0:T(8,128)(2,1)S(1)} %get-tuple-element.83), channel_id=1, source_target_pairs={{0,2},{1,3},{2,0},{3,1},{4,6},{5,7},{6,4},{7,5},{8,10},{9,11},{10,... | collective-permute-start | bytes 479240 | tf_op jit(solution)/shard_map/ppermute | solution.py:47
  88.0 14.1 %collective-permute-start.30 = (bf16[192,1664]{1,0:T(8,128)(2,1)S(1)}, bf16[192,1664]{1,0:T(8,128)(2,1)S(1)}, u32[]{:S(2)}, u32[]{:S(2)}) collective-permute-start(bf16[192,1664]{1,0:T(8,128)(2,1)S(1)} %constant_dynamic-update-slice_fusion.20), channel_id=1, source_target_pairs={{0,4},{4,0},{8,12},{12,8},{1,5},{5,1},{9,13},{13,9},{2,6},{6,2},{1... | collective-permute-start | bytes 1916936 | tf_op jit(solution)/shard_map/ppermute | solution.py:47
  89.0 19.1 %collective-permute-start.31 = (bf16[192,1664]{1,0:T(8,128)(2,1)S(1)}, bf16[192,1664]{1,0:T(8,128)(2,1)S(1)}, u32[]{:S(2)}, u32[]{:S(2)}) collective-permute-start(bf16[192,1664]{1,0:T(8,128)(2,1)S(1)} %constant_dynamic-update-slice_fusion.20), channel_id=1, source_target_pairs={{0,8},{4,12},{8,0},{12,4},{1,9},{5,13},{9,1},{13,5},{2,10},{6,14},... | collective-permute-start | bytes 1916936 | tf_op jit(solution)/shard_map/ppermute | solution.py:47
  89.7 27.0 %collective-permute-start.32 = (bf16[192,1664]{1,0:T(8,128)(2,1)S(1)}, bf16[192,1664]{1,0:T(8,128)(2,1)S(1)}, u32[]{:S(2)}, u32[]{:S(2)}) collective-permute-start(bf16[192,1664]{1,0:T(8,128)(2,1)S(1)} %constant_dynamic-update-slice_fusion.20), channel_id=1, source_target_pairs={{0,12},{4,8},{8,4},{12,0},{1,13},{5,9},{9,5},{13,1},{2,14},{6,10},... | collective-permute-start | bytes 1916936 | tf_op jit(solution)/shard_map/ppermute | solution.py:47
  102.1 73.4 %collective-permute-start.20 = (bf16[768,768]{1,0:T(8,128)(2,1)}, bf16[768,768]{1,0:T(8,128)(2,1)}, u32[]{:S(2)}, u32[]{:S(2)}) collective-permute-start(bf16[768,768]{1,0:T(8,128)(2,1)} %bitcast.107), channel_id=1, source_target_pairs={{0,16},{16,0},{1,17},{17,1},{2,18},{18,2},{3,19},{19,3},{4,20},{20... | collective-permute-start | bytes 3538952 | tf_op jit(solution)/shard_map/ppermute | solution.py:31
  117.6 19.7 %collective-permute-start.33 = (bf16[768,1664]{1,0:T(8,128)(2,1)}, bf16[768,1664]{1,0:T(8,128)(2,1)}, u32[]{:S(2)}, u32[]{:S(2)}) collective-permute-start(bf16[768,1664]{1,0:T(8,128)(2,1)} %constant_dynamic-update-slice_fusion.16), channel_id=1, source_target_pairs={{0,16},{16,0},{1,17},{17,1},{2,18},{18,2},{3,19},{19,3},{4,20},{20... | collective-permute-start | bytes 7667720 | tf_op jit(solution)/shard_map/ppermute | solution.py:31
  133.5 13.2 %collective-permute-start.13 = (bf16[64,768]{1,0:T(8,128)(2,1)S(1)}, bf16[64,768]{1,0:T(8,128)(2,1)}, u32[]{:S(2)}, u32[]{:S(2)}) collective-permute-start(bf16[64,768]{1,0:T(8,128)(2,1)S(1)} %multiply_convert_fusion.5), channel_id=1, source_target_pairs={{0,1},{1,0},{2,3},{3,2},{4,5},{5,4},{6,7},{7,6},{8,9},{9,8},{10,11... | collective-permute-start | bytes 294920 | tf_op jit(solution)/shard_map/ppermute | solution.py:47
  151.4 12.7 %collective-permute-start.16 = (bf16[128,768]{1,0:T(8,128)(2,1)}, bf16[128,768]{1,0:T(8,128)(2,1)}, u32[]{:S(2)}, u32[]{:S(2)}) collective-permute-start(bf16[128,768]{1,0:T(8,128)(2,1)} %squeeze.95), channel_id=1, source_target_pairs={{0,4},{4,0},{8,12},{12,8},{1,5},{5,1},{9,13},{13,9},{2,6},{6,2},{1... | collective-permute-start | bytes 589832 | tf_op jit(solution)/shard_map/ppermute | solution.py:47
  222.6 19.5 %collective-permute-start.47 = (bf16[64,768]{1,0:T(8,128)(2,1)}, bf16[64,768]{1,0:T(8,128)(2,1)}, u32[]{:S(2)}, u32[]{:S(2)}) collective-permute-start(bf16[64,768]{1,0:T(8,128)(2,1)} %get-tuple-element.69), channel_id=1, source_target_pairs={{0,1},{1,0},{2,3},{3,2},{4,5},{5,4},{6,7},{7,6},{8,9},{9,8},{10,11... | collective-permute-start | bytes 294920 | tf_op jit(solution)/shard_map/ppermute | solution.py:47
  223.1 19.7 %collective-permute-start.48 = (bf16[64,768]{1,0:T(8,128)(2,1)}, bf16[64,768]{1,0:T(8,128)(2,1)}, u32[]{:S(2)}, u32[]{:S(2)}) collective-permute-start(bf16[64,768]{1,0:T(8,128)(2,1)} %get-tuple-element.69), channel_id=1, source_target_pairs={{0,2},{1,3},{2,0},{3,1},{4,6},{5,7},{6,4},{7,5},{8,10},{9,11},{10,... | collective-permute-start | bytes 294920 | tf_op jit(solution)/shard_map/ppermute | solution.py:47
  224.1 18.7 %collective-permute-start.49 = (bf16[64,768]{1,0:T(8,128)(2,1)}, bf16[64,768]{1,0:T(8,128)(2,1)}, u32[]{:S(2)}, u32[]{:S(2)}) collective-permute-start(bf16[64,768]{1,0:T(8,128)(2,1)} %get-tuple-element.69), channel_id=1, source_target_pairs={{0,3},{1,2},{2,1},{3,0},{4,7},{5,6},{6,5},{7,4},{8,11},{9,10},{10,... | collective-permute-start | bytes 294920 | tf_op jit(solution)/shard_map/ppermute | solution.py:47
  233.3 28.3 %collective-permute-start.37 = (bf16[128,768]{1,0:T(8,128)(2,1)}, bf16[128,768]{1,0:T(8,128)(2,1)}, u32[]{:S(2)}, u32[]{:S(2)}) collective-permute-start(bf16[128,768]{1,0:T(8,128)(2,1)} %squeeze.106), channel_id=1, source_target_pairs={{0,4},{4,0},{8,12},{12,8},{1,5},{5,1},{9,13},{13,9},{2,6},{6,2},{1... | collective-permute-start | bytes 589832 | tf_op jit(solution)/shard_map/ppermute | solution.py:47
  237.3 26.0 %collective-permute-start.38 = (bf16[128,768]{1,0:T(8,128)(2,1)}, bf16[128,768]{1,0:T(8,128)(2,1)}, u32[]{:S(2)}, u32[]{:S(2)}) collective-permute-start(bf16[128,768]{1,0:T(8,128)(2,1)} %squeeze.107), channel_id=1, source_target_pairs={{0,8},{4,12},{8,0},{12,4},{1,9},{5,13},{9,1},{13,5},{2,10},{6,14},... | collective-permute-start | bytes 589832 | tf_op jit(solution)/shard_map/ppermute | solution.py:47
  242.1 22.2 %collective-permute-start.39 = (bf16[128,768]{1,0:T(8,128)(2,1)}, bf16[128,768]{1,0:T(8,128)(2,1)}, u32[]{:S(2)}, u32[]{:S(2)}) collective-permute-start(bf16[128,768]{1,0:T(8,128)(2,1)} %squeeze.108), channel_id=1, source_target_pairs={{0,12},{4,8},{8,4},{12,0},{1,13},{5,9},{9,5},{13,1},{2,14},{6,10},... | collective-permute-start | bytes 589832 | tf_op jit(solution)/shard_map/ppermute | solution.py:47
  250.9 22.3 %collective-permute-start.50 = (bf16[128,768]{1,0:T(8,128)(2,1)}, bf16[128,768]{1,0:T(8,128)(2,1)}, u32[]{:S(2)}, u32[]{:S(2)}) collective-permute-start(bf16[128,768]{1,0:T(8,128)(2,1)} %squeeze.113), channel_id=1, source_target_pairs={{0,4},{4,0},{8,12},{12,8},{1,5},{5,1},{9,13},{13,9},{2,6},{6,2},{1... | collective-permute-start | bytes 589832 | tf_op jit(solution)/shard_map/ppermute | solution.py:47
  254.9 20.0 %collective-permute-start.51 = (bf16[128,768]{1,0:T(8,128)(2,1)}, bf16[128,768]{1,0:T(8,128)(2,1)}, u32[]{:S(2)}, u32[]{:S(2)}) collective-permute-start(bf16[128,768]{1,0:T(8,128)(2,1)} %squeeze.228), channel_id=1, source_target_pairs={{0,8},{4,12},{8,0},{12,4},{1,9},{5,13},{9,1},{13,5},{2,10},{6,14},... | collective-permute-start | bytes 589832 | tf_op jit(solution)/shard_map/ppermute | solution.py:47
  261.6 14.3 %collective-permute-start.52 = (bf16[128,768]{1,0:T(8,128)(2,1)}, bf16[128,768]{1,0:T(8,128)(2,1)S(1)}, u32[]{:S(2)}, u32[]{:S(2)}) collective-permute-start(bf16[128,768]{1,0:T(8,128)(2,1)} %squeeze.229), channel_id=1, source_target_pairs={{0,12},{4,8},{8,4},{12,0},{1,13},{5,9},{9,5},{13,1},{2,14},{6,10},... | collective-permute-start | bytes 589832 | tf_op jit(solution)/shard_map/ppermute | solution.py:47
  271.3 13.1 %collective-permute-start.40 = (bf16[128,768]{1,0:T(8,128)(2,1)S(1)}, bf16[128,768]{1,0:T(8,128)(2,1)S(1)}, u32[]{:S(2)}, u32[]{:S(2)}) collective-permute-start(bf16[128,768]{1,0:T(8,128)(2,1)S(1)} %get-tuple-element.115), channel_id=1, source_target_pairs={{0,4},{4,0},{8,12},{12,8},{1,5},{5,1},{9,13},{13,9},{2,6},{6,2},{1... | collective-permute-start | bytes 589832 | tf_op jit(solution)/shard_map/ppermute | solution.py:47
  271.9 13.3 %collective-permute-start.41 = (bf16[128,768]{1,0:T(8,128)(2,1)S(1)}, bf16[128,768]{1,0:T(8,128)(2,1)S(1)}, u32[]{:S(2)}, u32[]{:S(2)}) collective-permute-start(bf16[128,768]{1,0:T(8,128)(2,1)S(1)} %get-tuple-element.114), channel_id=1, source_target_pairs={{0,8},{4,12},{8,0},{12,4},{1,9},{5,13},{9,1},{13,5},{2,10},{6,14},... | collective-permute-start | bytes 589832 | tf_op jit(solution)/shard_map/ppermute | solution.py:47
  282.4 16.7 %collective-permute-start.53 = (bf16[128,768]{1,0:T(8,128)(2,1)}, bf16[128,768]{1,0:T(8,128)(2,1)}, u32[]{:S(2)}, u32[]{:S(2)}) collective-permute-start(bf16[128,768]{1,0:T(8,128)(2,1)} %get-tuple-element.107), channel_id=1, source_target_pairs={{0,4},{4,0},{8,12},{12,8},{1,5},{5,1},{9,13},{13,9},{2,6},{6,2},{1... | collective-permute-start | bytes 589832 | tf_op jit(solution)/shard_map/ppermute | solution.py:47
  282.9 18.3 %collective-permute-start.54 = (bf16[128,768]{1,0:T(8,128)(2,1)}, bf16[128,768]{1,0:T(8,128)(2,1)}, u32[]{:S(2)}, u32[]{:S(2)}) collective-permute-start(bf16[128,768]{1,0:T(8,128)(2,1)} %get-tuple-element.106), channel_id=1, source_target_pairs={{0,8},{4,12},{8,0},{12,4},{1,9},{5,13},{9,1},{13,5},{2,10},{6,14},... | collective-permute-start | bytes 589832 | tf_op jit(solution)/shard_map/ppermute | solution.py:47
  284.3 16.9 %collective-permute-start.55 = (bf16[128,768]{1,0:T(8,128)(2,1)}, bf16[128,768]{1,0:T(8,128)(2,1)}, u32[]{:S(2)}, u32[]{:S(2)}) collective-permute-start(bf16[128,768]{1,0:T(8,128)(2,1)} %get-tuple-element.105), channel_id=1, source_target_pairs={{0,12},{4,8},{8,4},{12,0},{1,13},{5,9},{9,5},{13,1},{2,14},{6,10},... | collective-permute-start | bytes 589832 | tf_op jit(solution)/shard_map/ppermute | solution.py:47
  291.5 17.2 %collective-permute-start.43 = (bf16[64,768]{1,0:T(8,128)(2,1)}, bf16[64,768]{1,0:T(8,128)(2,1)}, u32[]{:S(2)}, u32[]{:S(2)}) collective-permute-start(bf16[64,768]{1,0:T(8,128)(2,1)} %get-tuple-element.140), channel_id=1, source_target_pairs={{0,1},{1,0},{2,3},{3,2},{4,5},{5,4},{6,7},{7,6},{8,9},{9,8},{10,11... | collective-permute-start | bytes 294920 | tf_op jit(solution)/shard_map/ppermute | solution.py:47
  348.3 15.5 %collective-permute-start.62 = (bf16[128,768]{1,0:T(8,128)(2,1)}, bf16[128,768]{1,0:T(8,128)(2,1)}, u32[]{:S(2)}, u32[]{:S(2)}) collective-permute-start(bf16[128,768]{1,0:T(8,128)(2,1)} %squeeze.234), channel_id=1, source_target_pairs={{0,4},{4,0},{8,12},{12,8},{1,5},{5,1},{9,13},{13,9},{2,6},{6,2},{1... | collective-permute-start | bytes 589832 | tf_op jit(solution)/shard_map/ppermute | solution.py:47
  388.0 17.5 %collective-permute-start.68 = (bf16[64,768]{1,0:T(8,128)(2,1)}, bf16[64,768]{1,0:T(8,128)(2,1)}, u32[]{:S(2)}, u32[]{:S(2)}) collective-permute-start(bf16[64,768]{1,0:T(8,128)(2,1)} %get-tuple-element.134), channel_id=1, source_target_pairs={{0,1},{1,0},{2,3},{3,2},{4,5},{5,4},{6,7},{7,6},{8,9},{9,8},{10,11... | collective-permute-start | bytes 294920 | tf_op jit(solution)/shard_map/ppermute | solution.py:47
  388.6 16.9 %collective-permute-start.69 = (bf16[64,768]{1,0:T(8,128)(2,1)}, bf16[64,768]{1,0:T(8,128)(2,1)}, u32[]{:S(2)}, u32[]{:S(2)}) collective-permute-start(bf16[64,768]{1,0:T(8,128)(2,1)} %get-tuple-element.136), channel_id=1, source_target_pairs={{0,2},{1,3},{2,0},{3,1},{4,6},{5,7},{6,4},{7,5},{8,10},{9,11},{10,... | collective-permute-start | bytes 294920 | tf_op jit(solution)/shard_map/ppermute | solution.py:47
  389.9 15.6 %collective-permute-start.70 = (bf16[64,768]{1,0:T(8,128)(2,1)}, bf16[64,768]{1,0:T(8,128)(2,1)}, u32[]{:S(2)}, u32[]{:S(2)}) collective-permute-start(bf16[64,768]{1,0:T(8,128)(2,1)} %get-tuple-element.135), channel_id=1, source_target_pairs={{0,3},{1,2},{2,1},{3,0},{4,7},{5,6},{6,5},{7,4},{8,11},{9,10},{10,... | collective-permute-start | bytes 294920 | tf_op jit(solution)/shard_map/ppermute | solution.py:47
  451.5 23.6 %collective-permute-start.72 = (bf16[768,1664]{1,0:T(8,128)(2,1)S(1)}, bf16[768,1664]{1,0:T(8,128)(2,1)S(1)}, u32[]{:S(2)}, u32[]{:S(2)}) collective-permute-start(bf16[768,1664]{1,0:T(8,128)(2,1)S(1)} %get-tuple-element.165), channel_id=1, source_target_pairs={{0,16},{16,0},{1,17},{17,1},{2,18},{18,2},{3,19},{19,3},{4,20},{20... | collective-permute-start | bytes 7667720 | tf_op jit(solution)/shard_map/ppermute | solution.py:31
  460.9 14.2 %collective-permute-start.79 = (bf16[768,1664]{1,0:T(8,128)(2,1)S(1)}, bf16[768,1664]{1,0:T(8,128)(2,1)S(1)}, u32[]{:S(2)}, u32[]{:S(2)}) collective-permute-start(bf16[768,1664]{1,0:T(8,128)(2,1)S(1)} %get-tuple-element.164), channel_id=1, source_target_pairs={{0,16},{16,0},{1,17},{17,1},{2,18},{18,2},{3,19},{19,3},{4,20},{20... | collective-permute-start | bytes 7667720 | tf_op jit(solution)/shard_map/ppermute | solution.py:31
  473.4 65.6 %collective-permute-start.88 = (bf16[768,768]{1,0:T(8,128)(2,1)}, bf16[768,768]{1,0:T(8,128)(2,1)S(1)}, u32[]{:S(2)}, u32[]{:S(2)}) collective-permute-start(bf16[768,768]{1,0:T(8,128)(2,1)} %get-tuple-element.264), channel_id=1, source_target_pairs={{0,16},{16,0},{1,17},{17,1},{2,18},{18,2},{3,19},{19,3},{4,20},{20... | collective-permute-start | bytes 3538952 | tf_op jit(solution)/shard_map/ppermute | solution.py:31
  479.3 15.9 %collective-permute-start.80 = (bf16[192,1664]{1,0:T(8,128)(2,1)S(1)}, bf16[192,1664]{1,0:T(8,128)(2,1)S(1)}, u32[]{:S(2)}, u32[]{:S(2)}) collective-permute-start(bf16[192,1664]{1,0:T(8,128)(2,1)S(1)} %get-tuple-element.88), channel_id=1, source_target_pairs={{0,4},{4,0},{8,12},{12,8},{1,5},{5,1},{9,13},{13,9},{2,6},{6,2},{1... | collective-permute-start | bytes 1916936 | tf_op jit(solution)/shard_map/ppermute | solution.py:47
  480.8 15.9 %collective-permute-start.81 = (bf16[192,1664]{1,0:T(8,128)(2,1)S(1)}, bf16[192,1664]{1,0:T(8,128)(2,1)S(1)}, u32[]{:S(2)}, u32[]{:S(2)}) collective-permute-start(bf16[192,1664]{1,0:T(8,128)(2,1)S(1)} %get-tuple-element.90), channel_id=1, source_target_pairs={{0,8},{4,12},{8,0},{12,4},{1,9},{5,13},{9,1},{13,5},{2,10},{6,14},... | collective-permute-start | bytes 1916936 | tf_op jit(solution)/shard_map/ppermute | solution.py:47
  481.3 28.3 %collective-permute-start.82 = (bf16[192,1664]{1,0:T(8,128)(2,1)S(1)}, bf16[192,1664]{1,0:T(8,128)(2,1)S(1)}, u32[]{:S(2)}, u32[]{:S(2)}) collective-permute-start(bf16[192,1664]{1,0:T(8,128)(2,1)S(1)} %get-tuple-element.89), channel_id=1, source_target_pairs={{0,12},{4,8},{8,4},{12,0},{1,13},{5,9},{9,5},{13,1},{2,14},{6,10},... | collective-permute-start | bytes 1916936 | tf_op jit(solution)/shard_map/ppermute | solution.py:47
  482.9 79.9 %collective-permute-start.87 = (bf16[768,768]{1,0:T(8,128)(2,1)S(1)}, bf16[768,768]{1,0:T(8,128)(2,1)S(1)}, u32[]{:S(2)}, u32[]{:S(2)}) collective-permute-start(bf16[768,768]{1,0:T(8,128)(2,1)S(1)} %get-tuple-element.262), channel_id=1, source_target_pairs={{0,16},{16,0},{1,17},{17,1},{2,18},{18,2},{3,19},{19,3},{4,20},{20... | collective-permute-start | bytes 3538952 | tf_op jit(solution)/shard_map/ppermute | solution.py:31
  495.2 27.4 %collective-permute-start.73 = (bf16[192,1664]{1,0:T(8,128)(2,1)S(1)}, bf16[192,1664]{1,0:T(8,128)(2,1)S(1)}, u32[]{:S(2)}, u32[]{:S(2)}) collective-permute-start(bf16[192,1664]{1,0:T(8,128)(2,1)S(1)} %get-tuple-element.91), channel_id=1, source_target_pairs={{0,4},{4,0},{8,12},{12,8},{1,5},{5,1},{9,13},{13,9},{2,6},{6,2},{1... | collective-permute-start | bytes 1916936 | tf_op jit(solution)/shard_map/ppermute | solution.py:47
  496.7 25.9 %collective-permute-start.74 = (bf16[192,1664]{1,0:T(8,128)(2,1)S(1)}, bf16[192,1664]{1,0:T(8,128)(2,1)S(1)}, u32[]{:S(2)}, u32[]{:S(2)}) collective-permute-start(bf16[192,1664]{1,0:T(8,128)(2,1)S(1)} %get-tuple-element.93), channel_id=1, source_target_pairs={{0,8},{4,12},{8,0},{12,4},{1,9},{5,13},{9,1},{13,5},{2,10},{6,14},... | collective-permute-start | bytes 1916936 | tf_op jit(solution)/shard_map/ppermute | solution.py:47
  509.6 27.4 %collective-permute-start.75 = (bf16[192,1664]{1,0:T(8,128)(2,1)S(1)}, bf16[192,1664]{1,0:T(8,128)(2,1)S(1)}, u32[]{:S(2)}, u32[]{:S(2)}) collective-permute-start(bf16[192,1664]{1,0:T(8,128)(2,1)S(1)} %get-tuple-element.92), channel_id=1, source_target_pairs={{0,12},{4,8},{8,4},{12,0},{1,13},{5,9},{9,5},{13,1},{2,14},{6,10},... | collective-permute-start | bytes 1916936 | tf_op jit(solution)/shard_map/ppermute | solution.py:47
  522.6 16.5 %collective-permute-start.83 = (bf16[48,1664]{1,0:T(8,128)(2,1)S(1)}, bf16[48,1664]{1,0:T(8,128)(2,1)S(1)}, u32[]{:S(2)}, u32[]{:S(2)}) collective-permute-start(bf16[48,1664]{1,0:T(8,128)(2,1)S(1)} %get-tuple-element.128), channel_id=1, source_target_pairs={{0,1},{1,0},{2,3},{3,2},{4,5},{5,4},{6,7},{7,6},{8,9},{9,8},{10,11... | collective-permute-start | bytes 479240 | tf_op jit(solution)/shard_map/ppermute | solution.py:47
  522.6 18.4 %collective-permute-start.84 = (bf16[48,1664]{1,0:T(8,128)(2,1)S(1)}, bf16[48,1664]{1,0:T(8,128)(2,1)S(1)}, u32[]{:S(2)}, u32[]{:S(2)}) collective-permute-start(bf16[48,1664]{1,0:T(8,128)(2,1)S(1)} %get-tuple-element.130), channel_id=1, source_target_pairs={{0,2},{1,3},{2,0},{3,1},{4,6},{5,7},{6,4},{7,5},{8,10},{9,11},{10,... | collective-permute-start | bytes 479240 | tf_op jit(solution)/shard_map/ppermute | solution.py:47
  539.2 12.8 %collective-permute-start.77 = (bf16[48,1664]{1,0:T(8,128)(2,1)S(1)}, bf16[48,1664]{1,0:T(8,128)(2,1)S(1)}, u32[]{:S(2)}, u32[]{:S(2)}) collective-permute-start(bf16[48,1664]{1,0:T(8,128)(2,1)S(1)} %get-tuple-element.133), channel_id=1, source_target_pairs={{0,2},{1,3},{2,0},{3,1},{4,6},{5,7},{6,4},{7,5},{8,10},{9,11},{10,... | collective-permute-start | bytes 479240 | tf_op jit(solution)/shard_map/ppermute | solution.py:47
  541.0 13.8 %collective-permute-start.78 = (bf16[48,1664]{1,0:T(8,128)(2,1)S(1)}, bf16[48,1664]{1,0:T(8,128)(2,1)S(1)}, u32[]{:S(2)}, u32[]{:S(2)}) collective-permute-start(bf16[48,1664]{1,0:T(8,128)(2,1)S(1)} %get-tuple-element.132), channel_id=1, source_target_pairs={{0,3},{1,2},{2,1},{3,0},{4,7},{5,6},{6,5},{7,4},{8,11},{9,10},{10,... | collective-permute-start | bytes 479240 | tf_op jit(solution)/shard_map/ppermute | solution.py:47
  (164 other events, 1462.5 us)

commit v2 on v1

v2 whole, which is shorter than its diff:
```python
import functools
import math

import jax
import jax.numpy as jnp
import numpy as np
from jax import lax
from jax.experimental import pallas as pl
from jax.experimental.pallas import tpu as pltpu
from jax.sharding import PartitionSpec as P

HEADS = 12
HEAD_DIM = 64
NB = 32
EXT = 128
LEAD = 3
EPSILON = 1e-06
MASK_FILL = -1e30
BF = jnp.bfloat16
F32 = jnp.float32
VM = pl.BlockSpec(memory_space=pltpu.VMEM)
SM = pl.BlockSpec(memory_space=pltpu.SMEM)
HB = pl.BlockSpec(memory_space=pl.ANY)


def dot(a, b):
    return jnp.dot(a, b, preferred_element_type=F32)


def dot_t(a, b):
    return lax.dot_general(a, b, (((1,), (1,)), ((), ())), preferred_element_type=F32)


def t_dot(a, b):
    return lax.dot_general(a, b, (((0,), (0,)), ((), ())), preferred_element_type=F32)


def swap(value):
    return lax.ppermute(value, "section", [(0, 1), (1, 0)])


def direct(axis):
    count = lax.axis_size(axis)
    return count <= 4 and count & (count - 1) == 0


def peer_ids(axis):
    count = lax.axis_size(axis)
    ids = jnp.arange(count, dtype=jnp.int32)
    return ids ^ lax.axis_index(axis) if direct(axis) else ids


def hop(value, axis, step):
    count = lax.axis_size(axis)
    return lax.ppermute(value, axis, [(i, i ^ step) for i in range(count)])


def spread(value, axis):
    count = lax.axis_size(axis)
    if direct(axis):
        return [value] + [hop(value, axis, step) for step in range(1, count)]
    every = lax.all_gather(value, axis, axis=0)
    return [every[i] for i in range(count)]


def exchange(blocks, axis):
    count = lax.axis_size(axis)
    if direct(axis):
        return [blocks[0]] + [hop(blocks[step], axis, step) for step in range(1, count)]
    swapped = lax.all_to_all(jnp.stack(blocks), axis, 0, 0, tiled=True)
    return [swapped[i] for i in range(count)]


def scatter_rows(whole):
    for axis in ("expert", "shard"):
        count = lax.axis_size(axis)
        rows = whole.shape[0] // count
        ids = peer_ids(axis)
        blocks = [
            lax.dynamic_slice_in_dim(whole, ids[i] * rows, rows, axis=0).astype(BF)
            for i in range(count)
        ]
        whole = sum(block.astype(F32) for block in exchange(blocks, axis))
    return whole


def call(kernel, outs, ins, specs, scratch=(), flops=0):
    moved = sum(math.prod(a.shape) * a.dtype.itemsize for a in (*ins, *outs))
    return pl.pallas_call(
        kernel,
        out_shape=list(outs),
        in_specs=list(specs),
        out_specs=[VM] * len(outs),
        scratch_shapes=list(scratch),
        compiler_params=pltpu.CompilerParams(vmem_limit_bytes=48 * 1024 * 1024),
        cost_estimate=pl.CostEstimate(flops=flops, bytes_accessed=moved, transcendentals=0),
    )(*ins)


def out(shape, kind=BF):
    return jax.ShapeDtypeStruct(shape, kind)


def start_weights(place, pieces, held, sems):
    count = len(pieces) // 2
    rows = pieces[0].shape[0]
    copies = []
    for part in range(2):
        for i in range(count):
            target = place[0] if part == 0 else 1 - place[0]
            first = pl.multiple_of(place[2 + i] * rows, rows) if count > 1 else 0
            copies.append(
                pltpu.make_async_copy(
                    pieces[part * count + i],
                    held.at[target, pl.ds(first, rows), :],
                    sems.at[part * count + i],
                )
            )
    for copy in copies:
        copy.start()
    return copies


def inverse_rms(value):
    return lax.rsqrt(jnp.mean(value * value, axis=-1, keepdims=True) + EPSILON)


def norm_back(value, gain, grad):
    scale = inverse_rms(value)
    scaled = value * scale
    gained = grad * gain
    back = scale * (gained - scaled * jnp.mean(gained * scaled, axis=-1, keepdims=True))
    return back, jnp.sum(grad * scaled, axis=0, keepdims=True)


def gain_rows(side):
    pick = (
        lax.broadcasted_iota(jnp.int32, (16, EXT), 0)
        == lax.broadcasted_iota(jnp.int32, (16, EXT), 1)
    ).astype(BF)
    rows = dot_t(pick, side)
    return rows[0:1], rows[1:2]


def gelu_parts(value):
    c = math.sqrt(2.0 / math.pi)
    square = value * value
    inner = jnp.tanh(c * (value + 0.044715 * square * value))
    grad = 0.5 * (1.0 + inner) + 0.5 * value * (1.0 - inner * inner) * (
        c + (3.0 * 0.044715 * c) * square
    )
    return 0.5 * value * (1.0 + inner), grad


def softmax_lanes(logits, experts):
    lane = lax.broadcasted_iota(jnp.int32, logits.shape, 1)
    valid = (lane >= LEAD) & (lane < LEAD + experts)
    logits = jnp.where(valid, logits, MASK_FILL)
    power = jnp.exp(logits - jnp.max(logits, axis=-1, keepdims=True))
    power = jnp.where(valid, power, 0.0)
    return power / jnp.sum(power, axis=-1, keepdims=True), lane


def pair_rows(value):
    low_lanes = lax.broadcasted_iota(jnp.int32, value.shape, 1) < HEAD_DIM
    zero = jnp.zeros_like(value)
    return jnp.concatenate(
        [jnp.where(low_lanes, value, zero), jnp.where(low_lanes, zero, value)], axis=0
    )


def pair_lanes(value):
    half = value.shape[0] // 2
    low_lanes = lax.broadcasted_iota(jnp.int32, (half, value.shape[1]), 1) < HEAD_DIM
    return jnp.where(low_lanes, value[:half], value[half:])


def attn_forward(layer, seq, width, experts, count, *refs):
    place, route, seg_col, seg_row, bucket, bucket_of, head_sel = refs[:7]
    refs = refs[7:]
    pieces, refs = refs[: 2 * count], refs[2 * count :]
    if layer == 0:
        (x_ref,), refs = refs[:1], refs[1:]
    else:
        (hid_ref, gate_ref), toks, refs = refs[:2], refs[2:-12], refs[-12:]
        (out_ref, tok_ref), refs = refs[:2], refs[2:]
    n2_ref, state, probs_ref, hidden_ref, gates_ref, gv_ref, ext_ref, held, sems, qkv = refs
    copies = start_weights(place, pieces, held, sems)
    if layer == 0:
        x = x_ref[...].astype(F32)
    else:
        tok = sum(t[...].astype(F32) for t in toks).astype(BF)
        tok_ref[...] = tok
        low = (hid_ref[...] + gate_ref[:, 0:1] * tok.astype(F32)).astype(BF)
        out_ref[...] = low
        x = low.astype(F32)
    scaled = x * inverse_rms(x)
    same = seg_col[...] == seg_row[...]
    for copy in copies:
        copy.wait()
    side = held[0, :, 2 * width : 2 * width + EXT]
    ext_ref[...] = side
    gain_one, gain_two = gain_rows(side)
    values = jnp.where(
        bucket_of[...] == bucket[...], side[:, 2:3].astype(F32), 0.0
    ).astype(BF)
    table = dot(head_sel[...], values)
    normed = (scaled * gain_one).astype(BF)
    state[:, :width] = normed
    qkv[:, : 2 * width] = dot(normed, held[0, :, : 2 * width]).astype(BF)
    qkv[:, 2 * width :] = dot(normed, held[1, :, :width]).astype(BF)
    state[:, width : 4 * width] = qkv[...]
    scale = 1.0 / math.sqrt(HEAD_DIM)
    contexts = []
    for p in range(HEADS // 2):
        lanes = slice(128 * p, 128 * p + 128)
        q2 = pair_rows(qkv[:, lanes])
        scores = dot_t(q2, qkv[:, width + 128 * p : width + 128 * p + 128]) * scale
        parts = []
        for h in (2 * p, 2 * p + 1):
            line = jnp.broadcast_to(table[h : h + 1], (seq, 2 * seq))
            bias = pltpu.roll(line, seq + 1, axis=1, stride=1, stride_axis=0)[:, :seq]
            part = scores[seq * (h - 2 * p) : seq * (h - 2 * p) + seq] + bias
            parts.append(jnp.where(same, part, MASK_FILL))
        scores = jnp.concatenate(parts, axis=0)
        power = jnp.exp(scores - jnp.max(scores, axis=-1, keepdims=True))
        probs = power / jnp.sum(power, axis=-1, keepdims=True)
        probs_ref[p] = probs
        vals = qkv[:, 2 * width + 128 * p : 2 * width + 128 * p + 128]
        contexts.append(pair_lanes(dot(probs.astype(BF), vals)))
    context = jnp.concatenate(contexts, axis=1).astype(BF)
    state[:, 4 * width :] = context
    hidden = x + dot(context, held[1, :, width : 2 * width])
    hidden_ref[...] = hidden
    normed_two = (hidden * inverse_rms(hidden) * gain_two).astype(BF)
    n2_ref[...] = normed_two
    gates, lane = softmax_lanes(dot(normed_two, side), experts)
    gates_ref[...] = gates
    value = jnp.sum(jnp.where(lane == route[...] + LEAD, gates, 0.0), axis=-1, keepdims=True)
    gv_ref[...] = jnp.broadcast_to(value, gv_ref.shape)


def dispatch_rows(count, shards, cap, *refs):
    hot = refs[0]
    toks = refs[1 : 1 + shards]
    blocks = refs[1 + shards :]
    for z in range(shards):
        rows = dot(hot[z], toks[z][...]).astype(BF)
        for i in range(count):
            blocks[i][z * cap : (z + 1) * cap, :] = rows[i * cap : (i + 1) * cap]


def combine_rows(count, shards, cap, *refs):
    hot = refs[0]
    blocks = refs[1 : 1 + count]
    toks = refs[1 + count :]
    for z in range(shards):
        rows = jnp.concatenate([b[z * cap : (z + 1) * cap, :] for b in blocks], axis=0)
        toks[z][...] = dot(hot[z], rows).astype(BF)


def start_expert(layer, place, own, came, held, sems):
    def begin(pair):
        for i in range(2):
            pltpu.make_async_copy(pair[i], held.at[i], sems.at[i]).start()

    @pl.when(place[0] == layer)
    def _():
        begin(own)

    @pl.when(place[0] != layer)
    def _():
        begin(came)

    return [pltpu.make_async_copy(own[i], held.at[i], sems.at[i]) for i in range(2)]


def expert_forward(layer, count, *refs):
    place, own, came = refs[0], refs[1:3], refs[3:5]
    blocks = refs[5 : 5 + count]
    results = refs[5 + count : 5 + 2 * count]
    held, sems = refs[5 + 2 * count :]
    copies = start_expert(layer, place, own, came, held, sems)
    for copy in copies:
        copy.wait()
    for i in range(count):
        pre_act = dot(blocks[i][...], held[0])
        activated = gelu_parts(pre_act)[0].astype(BF)
        results[i][...] = dot(activated, held[1]).astype(BF)


def expert_backward(layer, count, experts, with_out, *refs):
    place, own, came, ext = refs[0], refs[1:3], refs[3:5], refs[5]
    blocks = refs[6 : 6 + count]
    dys = refs[6 + count : 6 + 2 * count]
    refs = refs[6 + 2 * count :]
    grads, refs = refs[:count], refs[count:]
    if with_out:
        results, refs = refs[:count], refs[count:]
    keep, held, sems = refs
    copies = start_expert(layer, place, own, came, held, sems)
    rows_each = blocks[0].shape[0]
    for copy in copies:
        copy.wait()
    for i in range(count):
        at = slice(i * rows_each, (i + 1) * rows_each)
        rows = blocks[i][...]
        gates, lane = softmax_lanes(dot(rows, ext[...]), experts)
        mine = (lane == place[1] + LEAD).astype(F32)
        value = jnp.sum(gates * mine, axis=-1, keepdims=True)
        dy = dys[i][...].astype(F32)
        grad_expert = (value * dy).astype(BF)
        act, slope = gelu_parts(dot(rows, held[0]))
        act = act.astype(BF)
        grad_pre = (dot_t(grad_expert, held[1]) * slope).astype(BF)
        grad = dot_t(grad_pre, held[0])
        if with_out:
            result = dot(act, held[1])
            results[i][...] = result.astype(BF)
            grad_gate = jnp.sum(dy * result, axis=-1, keepdims=True)
            grad_logits = (grad_gate * value * (mine - gates)).astype(BF)
            grad = grad + dot_t(grad_logits, ext[...])
        grads[i][...] = grad.astype(BF)
        keep[0, at, :] = rows
        keep[1, at, :] = grad_pre
        keep[2, at, :] = act
        keep[3, at, :] = grad_expert


def attn_backward(layer, seq, width, experts, count, shards, *refs):
    place, route, bucket_back, bucket_of, head_sel = refs[:5]
    pieces, refs = refs[5 : 5 + 2 * count], refs[5 + 2 * count :]
    dy_ref, x_ref, state, probs_ref, hidden_ref, n2_ref, gates_ref, gv_ref, tok_ref = refs[:9]
    parts, refs = refs[9 : 9 + shards], refs[9 + shards :]
    dx_ref, ship, stay, side_grad, held, sems, gj, g_rel = refs
    copies = start_weights(place, pieces, held, sems)
    dy = dy_ref[...].astype(F32)
    grad_norm_two = sum(p[...].astype(F32) for p in parts)
    hidden = hidden_ref[...]
    x = x_ref[...].astype(F32)
    for copy in copies:
        copy.wait()
    side = held[0, :, 2 * width : 2 * width + EXT]
    gain_one, gain_two = gain_rows(side)
    side_grad[...] = jnp.zeros_like(side_grad)
    if layer == 0:
        gates = gates_ref[...]
        lane = lax.broadcasted_iota(jnp.int32, gates.shape, 1)
        hot = (lane == route[...] + LEAD).astype(F32)
        grad_gate = jnp.sum(dy * tok_ref[...].astype(F32), axis=-1, keepdims=True)
        grad_logits = (grad_gate * gv_ref[:, 0:1] * (hot - gates)).astype(BF)
        grad_norm_two = grad_norm_two + dot_t(grad_logits, side)
        router_rows = t_dot(grad_logits, n2_ref[...])
        side_grad[...] = router_rows[: side_grad.shape[0]]
    back, gain_two_grad = norm_back(hidden, gain_two, grad_norm_two)
    grad_hidden = dy + back
    grad_hidden_low = grad_hidden.astype(BF)
    grad_context = dot_t(grad_hidden_low, held[1, :, width : 2 * width]).astype(BF)
    scale = 1.0 / math.sqrt(HEAD_DIM)
    mirror = (
        lax.broadcasted_iota(jnp.int32, (seq, 2 * seq), 0)
        + lax.broadcasted_iota(jnp.int32, (seq, 2 * seq), 1)
        == seq - 1
    ).astype(BF)
    for p in range(HEADS // 2):
        lanes = slice(128 * p, 128 * p + 128)
        q2 = pair_rows(state[:, width + 128 * p : width + 128 * p + 128])
        keys = state[:, 2 * width + 128 * p : 2 * width + 128 * p + 128]
        vals = state[:, 3 * width + 128 * p : 3 * width + 128 * p + 128]
        g2 = pair_rows(grad_context[:, lanes])
        probs = probs_ref[p]
        grad_probs = dot_t(g2, vals)
        grad_scores = probs * (
            grad_probs - jnp.sum(probs * grad_probs, axis=-1, keepdims=True)
        )
        grad_scores = grad_scores.astype(BF)
        gj[:, lanes] = (pair_lanes(dot(grad_scores, keys)) * scale).astype(BF)
        gj[:, width + 128 * p : width + 128 * p + 128] = (t_dot(grad_scores, q2) * scale).astype(BF)
        gj[:, 2 * width + 128 * p : 2 * width + 128 * p + 128] = t_dot(
            probs.astype(BF), g2
        ).astype(BF)
        turned = dot(grad_scores, mirror)
        for h in range(2):
            shifted = pltpu.roll(turned[h * seq : (h + 1) * seq], 0, axis=1, stride=1, stride_axis=0)
            g_rel[2 * p + h : 2 * p + h + 1, :] = jnp.sum(shifted, axis=0, keepdims=True)
    g_rel[HEADS:, :] = jnp.zeros_like(g_rel[HEADS:, :])
    buckets = (bucket_of[...] == bucket_back[...]).astype(BF)
    offsets = g_rel[...]
    high = offsets.astype(BF)
    low = (offsets - high.astype(F32)).astype(BF)
    by_row = dot_t(high, buckets) + dot_t(low, buckets)
    side_grad[2:3, :] = jnp.sum(by_row * head_sel[...].astype(F32), axis=0, keepdims=True)
    side_grad[1:2, :] = gain_two_grad
    grad_normed = dot_t(gj[:, : 2 * width], held[0, :, : 2 * width]) + dot_t(
        gj[:, 2 * width :], held[1, :, :width]
    )
    back, gain_one_grad = norm_back(x, gain_one, grad_normed)
    side_grad[0:1, :] = gain_one_grad
    dx_ref[...] = (grad_hidden + back).astype(BF)
    normed = state[:, :width]
    halves = (ship, stay)
    for core in range(2):

        @pl.when(place[0] == core)
        def _(core=core):
            halves[1 - core][:, :width] = normed
            halves[1 - core][:, width : 3 * width] = gj[:, : 2 * width]
            halves[1 - core][:, 3 * width :] = jnp.zeros_like(normed)
            halves[core][:, :width] = normed
            halves[core][:, width : 2 * width] = gj[:, 2 * width :]
            halves[core][:, 2 * width : 3 * width] = state[:, 4 * width :]
            halves[core][:, 3 * width :] = grad_hidden_low


def last_output(experts, shards, *refs):
    route, dy_ref, hidden_ref, n2_ref, gates_ref, gv_ref, side_in = refs[:7]
    parts, refs = refs[7 : 7 + shards], refs[7 + shards :]
    out_ref, side_grad = refs
    tok = sum(p[...].astype(F32) for p in parts).astype(BF).astype(F32)
    value = gv_ref[:, 0:1]
    out_ref[...] = (hidden_ref[...] + value * tok).astype(BF)
    gates = gates_ref[...]
    lane = lax.broadcasted_iota(jnp.int32, gates.shape, 1)
    hot = (lane == route[...] + LEAD).astype(F32)
    grad_gate = jnp.sum(dy_ref[...].astype(F32) * tok, axis=-1, keepdims=True)
    grad_logits = (grad_gate * value * (hot - gates)).astype(BF)
    side_grad[...] = side_in[...] + t_dot(grad_logits, n2_ref[...])[: side_grad.shape[0]]


def attn_weights(width, count, *refs):
    place, stay, came, side_a, side_b = refs[:5]
    blocks, total = refs[5 : 5 + count], refs[-1]

    def both(first, last):
        return jnp.concatenate([stay[:, first:last], came[:, first:last]], axis=0)

    @pl.when(place[0] == 0)
    def _():
        total[:, : 2 * width] = t_dot(both(0, width), both(width, 3 * width)).astype(BF)
        side = side_a[...] + side_b[...]
        pick = (
            lax.broadcasted_iota(jnp.int32, (side.shape[0], EXT), 0)
            == lax.broadcasted_iota(jnp.int32, (side.shape[0], EXT), 1)
        ).astype(BF)
        total[:, 2 * width :] = t_dot(side.astype(BF), pick).astype(BF)

    @pl.when(place[0] != 0)
    def _():
        total[:, :width] = t_dot(both(0, width), both(width, 2 * width)).astype(BF)
        total[:, width : 2 * width] = t_dot(
            both(2 * width, 3 * width), both(3 * width, 4 * width)
        ).astype(BF)
        total[:, 2 * width :] = jnp.zeros_like(total[:, 2 * width :])

    rows = blocks[0].shape[0]
    for i in range(count):
        first = pl.multiple_of(place[2 + i] * rows, rows) if count > 1 else 0
        blocks[i][...] = total[pl.ds(first, rows), :]


def sum_blocks(count, at, *refs):
    place, parts = refs[0], refs[1 : 1 + count]
    blocks, total = refs[1 + count : -1], refs[-1]
    total[...] = sum(p[...].astype(F32) for p in parts)
    rows = blocks[0].shape[0]
    for i, block in enumerate(blocks):
        first = pl.multiple_of(place[at + i] * rows, rows) if len(blocks) > 1 else 0
        block[...] = total[pl.ds(first, rows), :].astype(block.dtype)


def join_rows(count, first_id, *refs):
    place, parts, whole, sems = refs[0], refs[1 : 1 + count], refs[1 + count], refs[2 + count]
    rows = parts[0].shape[0]
    copies = []
    for i in range(count):
        first = pl.multiple_of(place[first_id + i] * rows, rows)
        copies.append(pltpu.make_async_copy(parts[i], whole.at[pl.ds(first, rows), :], sems.at[i]))
    for copy in copies:
        copy.start()
    for copy in copies:
        copy.wait()


def expert_weights(other, *refs):
    place, keeps, refs = refs[0], refs[1:3], refs[3:]
    if other:
        in_ref, out_ref, held, sem = refs
    else:
        came_in, came_out, in_ref, out_ref, held, sem = refs
    for layer in range(2):

        @pl.when((place[0] == layer) != other)
        def _(layer=layer):
            pltpu.make_async_copy(keeps[layer], held, sem).start()

    pltpu.make_async_copy(keeps[0], held, sem).wait()
    grad_in = t_dot(held[0], held[1])
    grad_out = t_dot(held[2], held[3])
    if not other:
        grad_in = grad_in + came_in[...].astype(F32)
        grad_out = grad_out + came_out[...].astype(F32)
    in_ref[...] = grad_in.astype(in_ref.dtype)
    out_ref[...] = grad_out.astype(out_ref.dtype)


def body(
    feed, segments, routes, rel_bucket, gain_attn, gain_ffn, w_query, w_key, w_value, w_out_attn,
    rel_table, router, expert_in, expert_out,
):
    seq = feed.shape[2]
    width = feed.shape[3]
    experts = lax.axis_size("expert")
    shards = lax.axis_size("shard")
    cap = max(2, 2 * seq // experts)
    own_rows = w_query.shape[1]
    table_rows = rel_table.shape[1]
    quick = direct("expert") and direct("shard")
    blocks_count = experts if quick else 1
    wide = 2 * width + EXT
    side_rows = -(-(LEAD + experts) // 16) * 16
    sec = lax.axis_index("section")
    first = sec == 0
    place = jnp.concatenate(
        [
            jnp.stack([sec, lax.axis_index("expert")]).astype(jnp.int32),
            peer_ids("expert"),
            peer_ids("shard"),
        ]
    )
    spots = np.arange(width)
    flat = spots // own_rows * table_rows + spots % own_rows
    real = spots % own_rows < table_rows
    bucket_of = jnp.asarray(np.where(real, flat // HEADS, -1)[:, None].astype(np.int32))
    head_sel = jnp.asarray(
        (real[None, :] & (flat % HEADS == np.arange(16)[:, None])).astype(np.float32)
    ).astype(BF)
    spare = jnp.full((1,), -2, jnp.int32)
    bucket = jnp.concatenate([rel_bucket, spare])[None, :]
    bucket_back = jnp.concatenate([rel_bucket[::-1], spare])[None, :]

    ext = jnp.concatenate(
        [
            gain_attn[0][:, None],
            gain_ffn[0][:, None],
            jnp.pad(rel_table[0], (0, own_rows - table_rows))[:, None],
            router[0],
            jnp.zeros((own_rows, EXT - LEAD - experts), BF),
        ],
        axis=1,
    )
    half_a = jnp.concatenate([w_query[0], w_key[0], ext], axis=1)
    half_b = jnp.concatenate([w_value[0], w_out_attn[0], ext], axis=1)
    came = swap(jnp.where(first, half_b, half_a))
    parts = [jnp.where(first, half_a, came), jnp.where(first, came, half_b)]

    def gather(part):
        if not quick:
            mine = [lax.all_gather(part, ("expert", "shard"), axis=0, tiled=True)]
        else:
            plane = pl.pallas_call(
                functools.partial(join_rows, shards, 2 + experts),
                out_shape=out((shards * own_rows, wide)),
                in_specs=[SM] + [HB] * shards,
                out_specs=HB,
                scratch_shapes=[pltpu.SemaphoreType.DMA((shards,))],
            )(place, *spread(part, "shard"))
            mine = spread(plane, "expert")
        return mine + [swap(piece) for piece in mine]

    weights = [gather(parts[0]), None]

    came = swap(jnp.where(first, feed[0, 1], feed[0, 0]))
    layer_x = jnp.where(first, feed[0, 0], came)
    layer_dy = jnp.where(first, came, feed[0, 1])
    came = swap(jnp.where(first, routes[0, 1, 0], routes[0, 0, 0]))
    kept = jnp.where(first, routes[0, 0, 0], routes[0, 1, 0])
    my_routes = jnp.stack([jnp.where(first, kept, came), jnp.where(first, came, kept)])
    seg_ids = jnp.where(first, segments[0, 0], segments[1, 0])
    own_experts = [expert_in[0, 0], expert_out[0, 0]]
    came_experts = [swap(expert_in[0, 0]), swap(expert_out[0, 0])]

    all_routes = jnp.stack(spread(my_routes, "shard"), axis=1)
    hot = (all_routes[..., None] == peer_ids("expert")).astype(BF)
    positions = jnp.arange(seq, dtype=jnp.int32)
    before = (positions[:, None] > positions[None, :]).astype(BF)
    rank = jnp.einsum("ij,lzje->lzie", before, hot, preferred_element_type=F32)
    slot_in = jnp.arange(cap, dtype=jnp.int32).astype(F32)
    back_hot = (hot[..., None] * (rank[..., None] == slot_in).astype(BF)).reshape(
        2, shards, seq, experts * cap
    )
    to_hot = jnp.swapaxes(back_hot, 2, 3)
    route_cols = my_routes[:, :, None]
    seg_col, seg_row = seg_ids[:, None], seg_ids[None, :]

    row = out((seq, width))
    block = out((shards * cap * experts // blocks_count, width))
    sems = pltpu.SemaphoreType.DMA
    weight_count = experts if quick else 1
    weight_scratch = [pltpu.VMEM((2, width, wide), BF), sems((2 * weight_count,))]
    expert_scratch = [pltpu.VMEM((2, expert_in.shape[2], expert_in.shape[3]), BF), sems((2,))]
    expert_specs = [SM] + [HB] * 4

    def to_experts(layer, tokens):
        every = spread(tokens, "shard")
        if not quick:
            slots = jnp.einsum(
                "zcs,zsd->czd", to_hot[layer], jnp.stack(every), preferred_element_type=F32
            )
            slots = slots.astype(BF).reshape(experts, cap * shards, width)
            moved = exchange([slots[i] for i in range(experts)], "expert")
            return [jnp.concatenate(moved, axis=0)]
        blocks = call(
            functools.partial(dispatch_rows, experts, shards, cap),
            [block] * experts,
            [to_hot[layer], *every],
            [VM] * (1 + shards),
        )
        return exchange(blocks, "expert")

    def to_tokens(layer, blocks):
        if not quick:
            rows = blocks[0].reshape(experts, cap * shards, width)
            back = jnp.stack(exchange([rows[i] for i in range(experts)], "expert"))
            back = back.reshape(experts * cap, shards, width)
            tokens = jnp.einsum(
                "zsc,czd->zsd", back_hot[layer], back, preferred_element_type=F32
            ).astype(BF)
            return exchange([tokens[i] for i in range(shards)], "shard")
        back = exchange(blocks, "expert")
        tokens = call(
            functools.partial(combine_rows, experts, shards, cap),
            [row] * shards,
            [back_hot[layer], *back],
            [VM] * (1 + experts),
        )
        return exchange(tokens, "shard")

    def attention(layer, ins, in_specs):
        state_outs = [
            row,
            out((seq, 5 * width)),
            out((HEADS // 2, 2 * seq, seq), F32),
            out((seq, width), F32),
            out((seq, EXT), F32),
            out((seq, EXT), F32),
            out((width, EXT)),
        ]
        return call(
            functools.partial(attn_forward, layer, seq, width, experts, weight_count),
            ([row, row] if layer else []) + state_outs,
            [
                place, route_cols[layer], seg_col, seg_row, bucket, bucket_of, head_sel,
                *weights[layer], *ins,
            ],
            [SM] + [VM] * 6 + [HB] * (2 * weight_count) + in_specs,
            weight_scratch + [pltpu.VMEM((seq, 3 * width), BF)],
        )

    def attention_back(layer, dy, x, state, tok, parts):
        n2, acts, probs, hidden, gates, gv, _ = state
        return call(
            functools.partial(attn_backward, layer, seq, width, experts, weight_count, shards),
            [
                row,
                out((seq, 4 * width)),
                out((seq, 4 * width)),
                out((side_rows, width), F32),
            ],
            [
                place, route_cols[layer], bucket_back, bucket_of, head_sel, *weights[layer],
                dy, x, acts, probs, hidden, n2, gates, gv, tok, *parts,
            ],
            [SM] + [VM] * 4 + [HB] * (2 * weight_count) + [VM] * (9 + shards),
            weight_scratch + [pltpu.VMEM((seq, 3 * width), BF), pltpu.VMEM((16, 2 * seq), F32)],
        )

    def back_expert(layer, rows, dys, ext_side, with_out):
        results = call(
            functools.partial(expert_backward, layer, blocks_count, experts, with_out),
            [block] * (blocks_count * (2 if with_out else 1))
            + [out((4, shards * cap * experts, width))],
            [place, *own_experts, *came_experts, ext_side, *rows, *dys],
            expert_specs + [VM] * (1 + 2 * blocks_count),
            expert_scratch,
        )
        return results[:blocks_count], results[blocks_count:-1], results[-1]

    def reduce_weights(ship, stay, side):
        came = swap(ship)
        side_came = swap(side)
        blocks = call(
            functools.partial(attn_weights, width, weight_count),
            [out((width // weight_count, wide))] * weight_count,
            [place, stay, came, side, side_came],
            [SM] + [VM] * 4,
            [pltpu.VMEM((width, wide), BF)],
        )
        if not quick:
            return scatter_rows(blocks[0])
        blocks = call(
            functools.partial(sum_blocks, experts, 2 + experts),
            [out((own_rows, wide))] * shards,
            [place, *exchange(blocks, "expert")],
            [SM] + [VM] * experts,
            [pltpu.VMEM((shards * own_rows, wide), F32)],
        )
        (total,) = call(
            functools.partial(sum_blocks, shards, 0),
            [out((own_rows, wide), F32)],
            [place, *exchange(blocks, "shard")],
            [SM] + [VM] * shards,
            [pltpu.VMEM((own_rows, wide), F32)],
        )
        return total

    state_zero = attention(0, [layer_x], [VM])
    rows_zero = to_experts(0, state_zero[0])
    weights[1] = gather(parts[1])
    dys_one = to_experts(1, layer_dy)
    results = call(
        functools.partial(expert_forward, 0, blocks_count),
        [block] * blocks_count,
        [place, *own_experts, *came_experts, *rows_zero],
        expert_specs + [VM] * blocks_count,
        expert_scratch,
    )
    toks = to_tokens(0, results)
    results = attention(1, [state_zero[3], state_zero[5], *toks], [VM] * (2 + shards))
    (out_zero, tok_zero), state_one = results[:2], results[2:]
    rows_one = to_experts(1, state_one[0])
    grads, results, keep_one = back_expert(1, rows_one, dys_one, state_one[6], True)
    parts_one = to_tokens(1, grads)
    dx_one, ship_one, stay_one, side_one = attention_back(
        1, layer_dy, out_zero, state_one, out_zero, parts_one
    )
    dys_zero = to_experts(0, dx_one)
    toks_one = to_tokens(1, results)
    grads, _, keep_zero = back_expert(0, rows_zero, dys_zero, state_zero[6], False)
    out_one, side_one = call(
        functools.partial(last_output, experts, shards),
        [row, out((side_rows, width), F32)],
        [
            route_cols[1], layer_dy, state_one[3], state_one[0], state_one[4], state_one[5],
            side_one, *toks_one,
        ],
        [VM] * (7 + shards),
    )
    sum_one = reduce_weights(ship_one, stay_one, side_one)
    matrix = (expert_in.shape[2], expert_in.shape[3])
    keep_scratch = [pltpu.VMEM(keep_one.shape, BF), sems(())]
    sent = call(
        functools.partial(expert_weights, True),
        [out(matrix)] * 2,
        [place, keep_zero, keep_one],
        [SM, HB, HB],
        keep_scratch,
    )
    came_grads = [swap(grad) for grad in sent]
    parts_zero = to_tokens(0, grads)
    dx_zero, ship_zero, stay_zero, side_zero = attention_back(
        0, dx_one, layer_x, state_zero, tok_zero, parts_zero
    )
    sum_zero = reduce_weights(ship_zero, stay_zero, side_zero)
    own_grads = call(
        functools.partial(expert_weights, False),
        [out(matrix, F32)] * 2,
        [place, keep_zero, keep_one, *came_grads],
        [SM, HB, HB, VM, VM],
        keep_scratch,
    )

    came = swap(jnp.where(first, sum_one, sum_zero))
    kept = jnp.where(first, sum_zero, sum_one)
    final_a = jnp.where(first, kept, came)
    final_b = jnp.where(first, came, kept)

    def by_batch(zero, one):
        came = swap(jnp.where(first, one, zero))
        kept = jnp.where(first, zero, one)
        return jnp.stack([jnp.where(first, kept, came), jnp.where(first, came, kept)])

    side = final_a[:, 2 * width :]
    return (
        by_batch(out_zero, out_one)[None],
        by_batch(dx_zero, dx_one)[None],
        side[:, 0][None],
        side[:, 1][None],
        final_a[:, :width][None],
        final_a[:, width : 2 * width][None],
        final_b[:, :width][None],
        final_b[:, width : 2 * width][None],
        side[:table_rows, 2][None],
        side[:, LEAD : LEAD + experts][None],
        own_grads[0][None, None],
        own_grads[1][None, None],
    )


def solution(mesh):
    rows = ("expert", "shard")
    tokens = P("section", None, rows, None)
    matrix = P("section", rows, None)
    vector = P("section", rows)
    expert_specs = (P("section", "expert", None, "shard"), P("section", "expert", "shard", None))
    in_specs = (
        tokens, P(None, rows, None), tokens, P(), vector, vector, matrix, matrix, matrix, matrix,
        vector, matrix, *expert_specs,
    )
    out_specs = (
        tokens, tokens, vector, vector, matrix, matrix, matrix, matrix, vector, matrix,
        *expert_specs,
    )
    return jax.shard_map(body, mesh=mesh, in_specs=in_specs, out_specs=out_specs, check_vma=False)
```

time: 580 us -> 456 us (0.79)
  Pallas kernels: 0 us -> 113 us
  local copies, waits for them, and re-layouts: 153 us -> 57.9 us
  matrix products: 87.2 us -> 0.87 us
  other arithmetic: 34.8 us -> 7.59 us
  waiting for transfers between devices: 155 us -> 145 us
  between operations: 8.56 us -> 2.07 us
  starting transfers between devices: 129 us -> 123 us
    pallas_call x0 -> x26, Pallas kernels: none -> 113 us  [the longest x24 70.4 us: call(): pl.pallas_call(kernel, out_shape=list(outs), in_specs=list(specs), out_sp...]
    dot_general x54 -> x0, matrix products: 87.1 us -> none  [the longest x12 26.9 us: dot_t(): lax.dot_general(a, b, (((1,), (1,)), ((), ())), preferred_element_type=F32)]
    slice x39 -> x1, local copies, waits for them, and re-layouts: 42.8 us -> 0.71 us  [to_tokens(): back_hot[layer]]
    reshape x26 -> x0, local copies, waits for them, and re-layouts: 24.5 us -> none  [the longest x4 8.43 us: to_tokens(): back = back.reshape(experts * cap, shards, width)]
    unnamed x260 -> x254, local copies, waits for them, and re-layouts: 21 us -> 42.1 us
    squeeze x20 -> x5, local copies, waits for them, and re-layouts: 23.9 us -> 6.36 us  [the longest x2 2.62 us: to_tokens(): back_hot[layer]]
    ppermute x75, starting transfers between devices: 95.8 us -> 81.6 us  [hop(): return lax.ppermute(value, axis, [(i, i ^ step) for i in range(count)])]
    concatenate x7 -> x0, local copies, waits for them, and re-layouts: 10.7 us -> none  [the longest x2 9.1 us: backward(): grad_a = jnp.concatenate([grad_qkv[:, :2 * width], side], axis=1)]
  transfers between devices with their start and end apart: 89 -> 97, of which waited for: 28 -> 32; matrix products, arithmetic and copies ran while one was open for 29% -> 4% of each run, Pallas kernels for 0% -> 21%
where the time goes in v2:
time: 456 us; the launch traced here: 449 us
  waiting for transfers between devices  145 us (32%)
  starting transfers between devices  123 us (27%)
  Pallas kernels  113 us (25%)
  local copies, waits for them, and re-layouts  57.9 us (13%)
  other arithmetic  7.59 us (2%)
    ppermute x75, waiting for transfers between devices, hop(): return lax.ppermute(value, axis, [(i, i ^ step) for i in range(count)])  143 us
    ppermute x75, starting transfers between devices, hop(): return lax.ppermute(value, axis, [(i, i ^ step) for i in range(count)])  81.6 us
    pallas_call x24, Pallas kernels, call(): pl.pallas_call(kernel, out_shape=list(outs), in_specs=list(specs), out_sp...  70.4 us
    pallas_call x2, Pallas kernels, gather(): pl.pallas_call(functools.partial(join_rows, shards, 2 + experts), out_sha...  42.5 us
    unnamed x254, local copies, waits for them, and re-layouts  42.1 us
    ppermute x22, starting transfers between devices, swap(): return lax.ppermute(value, 'section', [(0, 1), (1, 0)])  41.2 us
  transfers between devices with their start and end apart: 97, of which 32 were waited for; matrix products, arithmetic and copies ran while one was open for 4% of the time, Pallas kernels for 21%

profile of v2, /device:TPU:1, one launch (start us, length us, event | category | flops | bytes accessed | tf_op | source)
XLA Modules:
  0.0 448.9 jit_solution(4204279641856727952)
XLA Ops:
  8.0 4.5 collective-permute-start.14
  13.3 3.3 collective-permute-done.14.refs_4_
  16.7 9.1 %collective-permute-done.13.refs_3_ = bf16[48,1664]{1,0:T(8,128)(2,1)S(1)} collective-permute-done((bf16[48,1664]{1,0:T(8,128)(2,1)S(1)}, bf16[48,1664]{1,0:T(8,128)(2,1)S(1)}, u32[]{:S(2)}, u32[]{:S(2)}) %collective-permute-start.13) | collective-permute-done | bytes 159776 | tf_op jit(solution)/shard_map/ppermute | solution.py:55
  27.1 21.2 %shard_map.248.refs_7_.refs_5_ = bf16[192,1664]{1,0:T(8,128)(2,1)} custom-call(s32[10]{0:T(128)} %pad_add_fusion.4.refs_0_, bf16[48,1664]{1,0:T(8,128)(2,1)} %copy-done.101, bf16[48,1664]{1,0:T(8,128)(2,1)} %copy-done.107, bf16[48,1664]{1,0:T(8,128)(2,1)} %copy-done.106, bf16[48,1664]{1,0:T(8,128)(2,1)} %copy-done.105), custom_call_target="tpu_custom_call" | custom-call | tf_op jit(solution)/shard_map/pallas_call | solution.py:560
  48.2 2.2 collective-permute-start.17
  51.6 2.5 collective-permute-start.23
  55.3 2.8 collective-permute-start.18
  58.1 2.3 collective-permute-start.25
  64.2 3.8 collective-permute-start.21
  68.1 11.4 %collective-permute-done.16.refs_9_.refs_7_ = bf16[192,1664]{1,0:T(8,128)(2,1)} collective-permute-done((bf16[192,1664]{1,0:T(8,128)(2,1)}, bf16[192,1664]{1,0:T(8,128)(2,1)}, u32[]{:S(2)}, u32[]{:S(2)}) %collective-permute-start.16) | collective-permute-done | bytes 639008 | tf_op jit(solution)/shard_map/ppermute | solution.py:55
  87.6 2.3 collective-permute-start.4
  98.4 5.8 %shard_map.249 = (bf16[64,768]{1,0:T(8,128)(2,1)}, bf16[64,3840]{1,0:T(8,128)(2,1)S(1)}, f32[6,128,64]{2,1,0:T(8,128)S(1)}, f32[64,768]{1,0:T(8,128)S(1)}, f32[6...) custom-call(s32[10]{0:T(128)S(1)} %copy-done.68, s32[64,1]{1,0:T(8,128)S(1)} %copy-done.50, ...), custom_call_target="tpu_custom_call" | custom-call | bytes 6484264 | tf_op jit(solution)/shard_map/pallas_call | solution.py:89
  108.3 2.2 collective-permute-start.30
  112.8 21.3 %shard_map.247.refs_7_.refs_5_ = bf16[192,1664]{1,0:T(8,128)(2,1)} custom-call(s32[10]{0:T(128)} %pad_add_fusion.4.refs_0_, bf16[48,1664]{1,0:T(8,128)(2,1)} %get-tuple-element.247.refs_1_, bf16[48,1664]{1,0:T(8,128)(2,1)} %copy-done.104, bf16[48,1664]{1,0:T(8,128)(2,1)} %copy-done.103, bf16[48,1664]{1,0:T(8,128)(2,1)} %copy-done.102), custom_call_target="tpu_custom_call" | custom-call | tf_op jit(solution)/shard_map/pallas_call | solution.py:560
  141.7 25.4 %collective-permute-done.31.refs_6_.refs_7_ = bf16[128,768]{1,0:T(8,128)(2,1)S(1)} collective-permute-done((bf16[128,768]{1,0:T(8,128)(2,1)S(1)}, bf16[128,768]{1,0:T(8,128)(2,1)S(1)}, u32[]{:S(2)}, u32[]{:S(2)}) %collective-permute-start.31) | collective-permute-done | bytes 196640 | tf_op jit(solution)/shard_map/ppermute | solution.py:55
  169.5 2.2 collective-permute-start.48
  174.4 4.0 shard_map.251
  182.0 4.1 collective-permute-start.8
  187.3 2.4 collective-permute-start.9
  191.8 5.2 %collective-permute-done.36.refs_4_ = bf16[128,768]{1,0:T(8,128)(2,1)S(1)} collective-permute-done((bf16[128,768]{1,0:T(8,128)(2,1)S(1)}, bf16[128,768]{1,0:T(8,128)(2,1)S(1)}, u32[]{:S(2)}, u32[]{:S(2)}) %collective-permute-start.36) | collective-permute-done | bytes 196640 | tf_op jit(solution)/shard_map/ppermute | solution.py:55
  208.5 2.2 collective-permute-start.39
  221.2 6.2 %shard_map.253 = (bf16[64,768]{1,0:T(8,128)(2,1)S(1)}, bf16[64,768]{1,0:T(8,128)(2,1)S(1)}, bf16[64,768]{1,0:T(8,128)(2,1)S(1)}, bf16[64,3840]{1,0:T(8,128)(2,1)...) custom-call(s32[10]{0:T(128)S(1)} %copy-done.69, ...), custom_call_target="tpu_custom_call" | custom-call | bytes 7205160 | tf_op jit(solution)/shard_map/pallas_call | solution.py:89
  235.9 4.1 collective-permute-done.41.refs_3_
  243.1 4.3 collective-permute-done.43.refs_7_
  248.3 4.2 collective-permute-done.45.refs_9_
  252.5 8.7 %shard_map.256 = (bf16[128,768]{1,0:T(8,128)(2,1)S(1)}, bf16[128,768]{1,0:T(8,128)(2,1)}, bf16[128,768]{1,0:T(8,128)(2,1)}, bf16[128,768]{1,0:T(8,128)(2,1)}, bf...) custom-call(s32[10]{0:T(128)S(1)} %copy-done.69, ...), custom_call_target="tpu_custom_call" | custom-call | bytes 11206696 | tf_op jit(solution)/shard_map/pallas_call | solution.py:89
  268.8 3.7 collective-permute-done.53.refs_3_
  273.7 2.2 collective-permute-start.55
  275.8 2.2 collective-permute-start.57
  278.1 4.1 collective-permute-done.56.refs_24_
  289.1 7.4 %shard_map.258 = (bf16[64,768]{1,0:T(8,128)(2,1)S(1)}, bf16[64,3072]{1,0:T(8,128)(2,1)S(1)}, bf16[64,3072]{1,0:T(8,128)(2,1)S(1)}, f32[16,768]{1,0:T(8,128)S(1)}) custom-call(s32[10]{0:T(128)S(1)} %copy-done.70, s32[64,1]{1,0:T(8,128)S(1)} %copy-done.37, s32[1,128]{1,0:T(1,128)S(1)} %fusion.7.refs_2_, s32[768,1]{1,0:T(8,128)S(1)} %copy-done.6, ...), custom_call_target="tpu_custom_call" | custom-call | bytes 7810856 | tf_op jit(solution)/shard_map/pallas_call | solution.py:89
  297.8 3.8 collective-permute-start.66
  301.9 4.2 collective-permute-done.66.refs_3_
  307.0 2.6 collective-permute-start.70
  311.4 7.1 %collective-permute-start.86 = (bf16[64,3072]{1,0:T(8,128)(2,1)S(1)}, bf16[64,3072]{1,0:T(8,128)(2,1)S(1)}, u32[]{:S(2)}, u32[]{:S(2)}) collective-permute-start(bf16[64,3072]{1,0:T(8,128)(2,1)S(1)} %get-tuple-element.188), channel_id=1, source_target_pairs={{0,16},{16,0},{1,17},{17,1},{2,18},{18,2},{3,19},{19,3},{4,20},{20... | collective-permute-start | bytes 1179656 | tf_op jit(solution)/shard_map/ppermute | solution.py:39
  318.7 8.2 %shard_map.262 = (bf16[128,768]{1,0:T(8,128)(2,1)S(1)}, bf16[128,768]{1,0:T(8,128)(2,1)S(1)}, bf16[128,768]{1,0:T(8,128)(2,1)S(1)}, bf16[128,768]{1,0:T(8,128)(2,1)S(1)}, bf16[4,512,768]{2,1,0:T(8,128)(2,1)}) custom-call(s32[10]{0:T(128)S(1)} %copy-done.70, bf16[768,768]{1,0:T(8,128)(2,1)S(1)} %bitcast.95, bf16[768,768]{1,0:T(8,128)(2,1)S(1)} %bitcast.99, ...), custom_call_target="tpu_custom_call" | custom-call | bytes 10420264 | tf_op jit(solution)/shard_map/pallas_call | solution.py:89
  327.4 2.1 collective-permute-start.72
  337.5 2.6 collective-permute-start.76
  341.5 8.3 %collective-permute-start.87 = (f32[16,768]{1,0:T(8,128)S(1)}, f32[16,768]{1,0:T(8,128)S(1)}, u32[]{:S(2)}, u32[]{:S(2)}) collective-permute-start(f32[16,768]{1,0:T(8,128)S(1)} %get-tuple-element.189.refs_3_), channel_id=1, source_target_pairs={{0,16},{16,0},{1,17},{17,1},{2,18},{18,2},{3,19},{19,3},{4,20},{20... | collective-permute-start | bytes 147464 | tf_op jit(solution)/shard_map/ppermute | solution.py:39
  352.4 7.4 %shard_map.264 = (bf16[64,768]{1,0:T(8,128)(2,1)S(1)}, bf16[64,3072]{1,0:T(8,128)(2,1)S(1)}, bf16[64,3072]{1,0:T(8,128)(2,1)S(1)}, f32[16,768]{1,0:T(8,128)S(1)}) custom-call(s32[10]{0:T(128)S(1)} %copy-done.70, s32[64,1]{1,0:T(8,128)S(1)} %copy-done.51, s32[1,128]{1,0:T(1,128)S(1)} %fusion.7.refs_2_, s32[768,1]{1,0:T(8,128)S(1)} %copy-done.6, ...), custom_call_target="tpu_custom_call" | custom-call | bytes 7810856 | tf_op jit(solution)/shard_map/pallas_call | solution.py:89
  359.9 2.5 collective-permute-start.78
  369.8 22.1 %collective-permute-done.89.refs_3_ = bf16[192,1664]{1,0:T(8,128)(2,1)S(1)} collective-permute-done((bf16[192,1664]{1,0:T(8,128)(2,1)S(1)}, bf16[192,1664]{1,0:T(8,128)(2,1)S(1)}, u32[]{:S(2)}, u32[]{:S(2)}) %collective-permute-start.89) | collective-permute-done | bytes 639008 | tf_op jit(solution)/shard_map/ppermute | solution.py:55
  398.8 2.2 shard_map.271
  401.0 18.3 %collective-permute-done.81.refs_3_ = bf16[192,1664]{1,0:T(8,128)(2,1)S(1)} collective-permute-done((bf16[192,1664]{1,0:T(8,128)(2,1)S(1)}, bf16[192,1664]{1,0:T(8,128)(2,1)S(1)}, u32[]{:S(2)}, u32[]{:S(2)}) %collective-permute-start.81) | collective-permute-done | bytes 639008 | tf_op jit(solution)/shard_map/ppermute | solution.py:55
  426.4 3.4 collective-permute-done.83.refs_2_
  431.2 4.4 collective-permute-done.85.refs_4_
  436.3 2.9 collective-permute-start.94
  439.9 5.6 %shard_map.272 = (f32[768,768]{1,0:T(8,128)}, f32[768,768]{1,0:T(8,128)}) custom-call(s32[10]{0:T(128)S(1)} %copy-done.70, bf16[4,512,768]{2,1,0:T(8,128)(2,1)S(1)} %copy-done, bf16[4,512,768]{2,1,0:T(8,128)(2,1)} %get-tuple-element.199.refs_2_, bf16[768,768]{1,0:T(8,128)(2,1)S(1)} %collective-permute-done.95.refs_3_, ...), custom_call_target="tpu_custom_call" | custom-call | bytes 13369384 | tf_op jit(solution)/shard_map/pallas_call | solution.py:89
  (476 shorter events, 151.8 us)
Async XLA Ops:
  5.9 45.0 %collective-permute-start = (s32[64]{0:T(128)S(1)}, s32[64]{0:T(128)S(1)}, u32[]{:S(2)}, u32[]{:S(2)}) collective-permute-start(s32[64]{0:T(128)S(1)} %fusion.8), channel_id=1, source_target_pairs={{0,16},{16,0},{1,17},{17,1},{2,18},{18,2},{3,19},{19,3},{4,20},{20... | collective-permute-start | bytes 776 | tf_op jit(solution)/shard_map/ppermute | solution.py:39
  12.4 13.3 %collective-permute-start.13 = (bf16[48,1664]{1,0:T(8,128)(2,1)S(1)}, bf16[48,1664]{1,0:T(8,128)(2,1)S(1)}, u32[]{:S(2)}, u32[]{:S(2)}) collective-permute-start(bf16[48,1664]{1,0:T(8,128)(2,1)S(1)} %get-tuple-element.246.refs_1_), channel_id=1, source_target_pairs={{0,2},{1,3},{2,0},{3,1},{4,6},{5,7},{6,4},{7,5},{8,10},{9,11},{10,... | collective-permute-start | bytes 479240 | tf_op jit(solution)/shard_map/ppermute | solution.py:55
  12.4 13.3 %collective-permute-start.12 = (bf16[48,1664]{1,0:T(8,128)(2,1)S(1)}, bf16[48,1664]{1,0:T(8,128)(2,1)S(1)}, u32[]{:S(2)}, u32[]{:S(2)}) collective-permute-start(bf16[48,1664]{1,0:T(8,128)(2,1)S(1)} %get-tuple-element.246.refs_1_), channel_id=1, source_target_pairs={{0,1},{1,0},{2,3},{3,2},{4,5},{5,4},{6,7},{7,6},{8,9},{9,8},{10,11... | collective-permute-start | bytes 479240 | tf_op jit(solution)/shard_map/ppermute | solution.py:55
  48.2 16.0 %collective-permute-start.17 = (bf16[192,1664]{1,0:T(8,128)(2,1)}, bf16[192,1664]{1,0:T(8,128)(2,1)}, u32[]{:S(2)}, u32[]{:S(2)}) collective-permute-start(bf16[192,1664]{1,0:T(8,128)(2,1)} %shard_map.248.refs_7_.refs_5_), channel_id=1, source_target_pairs={{0,12},{4,8},{8,4},{12,0},{1,13},{5,9},{9,5},{13,1},{2,14},{6,10},... | collective-permute-start | bytes 1916936 | tf_op jit(solution)/shard_map/ppermute | solution.py:55
  50.5 29.0 %collective-permute-start.16 = (bf16[192,1664]{1,0:T(8,128)(2,1)}, bf16[192,1664]{1,0:T(8,128)(2,1)}, u32[]{:S(2)}, u32[]{:S(2)}) collective-permute-start(bf16[192,1664]{1,0:T(8,128)(2,1)} %shard_map.248.refs_7_.refs_5_), channel_id=1, source_target_pairs={{0,8},{4,12},{8,0},{12,4},{1,9},{5,13},{9,1},{13,5},{2,10},{6,14},... | collective-permute-start | bytes 1916936 | tf_op jit(solution)/shard_map/ppermute | solution.py:55
  50.7 29.3 %collective-permute-start.15 = (bf16[192,1664]{1,0:T(8,128)(2,1)}, bf16[192,1664]{1,0:T(8,128)(2,1)}, u32[]{:S(2)}, u32[]{:S(2)}) collective-permute-start(bf16[192,1664]{1,0:T(8,128)(2,1)} %shard_map.248.refs_7_.refs_5_), channel_id=1, source_target_pairs={{0,4},{4,0},{8,12},{12,8},{1,5},{5,1},{9,13},{13,9},{2,6},{6,2},{1... | collective-permute-start | bytes 1916936 | tf_op jit(solution)/shard_map/ppermute | solution.py:55
  55.3 26.4 %collective-permute-start.18 = (bf16[192,1664]{1,0:T(8,128)(2,1)}, bf16[192,1664]{1,0:T(8,128)(2,1)S(1)}, u32[]{:S(2)}, u32[]{:S(2)}) collective-permute-start(bf16[192,1664]{1,0:T(8,128)(2,1)} %shard_map.248.refs_7_.refs_5_), channel_id=1, source_target_pairs={{0,16},{16,0},{1,17},{17,1},{2,18},{18,2},{3,19},{19,3},{4,20},{20... | collective-permute-start | bytes 1916936 | tf_op jit(solution)/shard_map/ppermute | solution.py:39
  62.5 18.1 %collective-permute-start.22 = (bf16[64,768]{1,0:T(8,128)(2,1)S(1)}, bf16[64,768]{1,0:T(8,128)(2,1)S(1)}, u32[]{:S(2)}, u32[]{:S(2)}) collective-permute-start(bf16[64,768]{1,0:T(8,128)(2,1)S(1)} %bitcast_select_fusion.1), channel_id=1, source_target_pairs={{0,16},{16,0},{1,17},{17,1},{2,18},{18,2},{3,19},{19,3},{4,20},{20... | collective-permute-start | bytes 294920 | tf_op jit(solution)/shard_map/ppermute | solution.py:39
  64.2 23.4 %collective-permute-start.21 = (bf16[192,1664]{1,0:T(8,128)(2,1)}, bf16[192,1664]{1,0:T(8,128)(2,1)}, u32[]{:S(2)}, u32[]{:S(2)}) collective-permute-start(bf16[192,1664]{1,0:T(8,128)(2,1)} %collective-permute-done.17.refs_10_.refs_8_), channel_id=1, source_target_pairs={{0,16},{16,0},{1,17},{17,1},{2,18},{18,2},{3,19},{19,3},{4,20},{20... | collective-permute-start | bytes 1916936 | tf_op jit(solution)/shard_map/ppermute | solution.py:39
  81.3 58.7 %collective-permute-start.26 = (bf16[768,768]{1,0:T(8,128)(2,1)S(1)}, bf16[768,768]{1,0:T(8,128)(2,1)S(1)}, u32[]{:S(2)}, u32[]{:S(2)}) collective-permute-start(bf16[768,768]{1,0:T(8,128)(2,1)S(1)} %bitcast.92), channel_id=1, source_target_pairs={{0,16},{16,0},{1,17},{17,1},{2,18},{18,2},{3,19},{19,3},{4,20},{20... | collective-permute-start | bytes 3538952 | tf_op jit(solution)/shard_map/ppermute | solution.py:39
  82.5 58.7 %collective-permute-start.27 = (bf16[768,768]{1,0:T(8,128)(2,1)S(1)}, bf16[768,768]{1,0:T(8,128)(2,1)}, u32[]{:S(2)}, u32[]{:S(2)}) collective-permute-start(bf16[768,768]{1,0:T(8,128)(2,1)S(1)} %bitcast.96), channel_id=1, source_target_pairs={{0,16},{16,0},{1,17},{17,1},{2,18},{18,2},{3,19},{19,3},{4,20},{20... | collective-permute-start | bytes 3538952 | tf_op jit(solution)/shard_map/ppermute | solution.py:39
  87.6 20.7 %collective-permute-start.4 = (bf16[48,1664]{1,0:T(8,128)(2,1)}, bf16[48,1664]{1,0:T(8,128)(2,1)S(1)}, u32[]{:S(2)}, u32[]{:S(2)}) collective-permute-start(bf16[48,1664]{1,0:T(8,128)(2,1)} %get-tuple-element.247.refs_1_), channel_id=1, source_target_pairs={{0,3},{1,2},{2,1},{3,0},{4,7},{5,6},{6,5},{7,4},{8,11},{9,10},{10,... | collective-permute-start | bytes 479240 | tf_op jit(solution)/shard_map/ppermute | solution.py:55
  89.9 20.6 %collective-permute-start.3 = (bf16[48,1664]{1,0:T(8,128)(2,1)}, bf16[48,1664]{1,0:T(8,128)(2,1)S(1)}, u32[]{:S(2)}, u32[]{:S(2)}) collective-permute-start(bf16[48,1664]{1,0:T(8,128)(2,1)} %get-tuple-element.247.refs_1_), channel_id=1, source_target_pairs={{0,2},{1,3},{2,0},{3,1},{4,6},{5,7},{6,4},{7,5},{8,10},{9,11},{10,... | collective-permute-start | bytes 479240 | tf_op jit(solution)/shard_map/ppermute | solution.py:55
  89.9 20.6 %collective-permute-start.2 = (bf16[48,1664]{1,0:T(8,128)(2,1)}, bf16[48,1664]{1,0:T(8,128)(2,1)S(1)}, u32[]{:S(2)}, u32[]{:S(2)}) collective-permute-start(bf16[48,1664]{1,0:T(8,128)(2,1)} %get-tuple-element.247.refs_1_), channel_id=1, source_target_pairs={{0,1},{1,0},{2,3},{3,2},{4,5},{5,4},{6,7},{7,6},{8,9},{9,8},{10,11... | collective-permute-start | bytes 479240 | tf_op jit(solution)/shard_map/ppermute | solution.py:55
  108.3 25.8 %collective-permute-start.30 = (bf16[64,768]{1,0:T(8,128)(2,1)}, bf16[64,768]{1,0:T(8,128)(2,1)}, u32[]{:S(2)}, u32[]{:S(2)}) collective-permute-start(bf16[64,768]{1,0:T(8,128)(2,1)} %get-tuple-element.110.refs_1_.refs_18_), channel_id=1, source_target_pairs={{0,3},{1,2},{2,1},{3,0},{4,7},{5,6},{6,5},{7,4},{8,11},{9,10},{10,... | collective-permute-start | bytes 294920 | tf_op jit(solution)/shard_map/ppermute | solution.py:55
  110.5 25.1 %collective-permute-start.29 = (bf16[64,768]{1,0:T(8,128)(2,1)}, bf16[64,768]{1,0:T(8,128)(2,1)}, u32[]{:S(2)}, u32[]{:S(2)}) collective-permute-start(bf16[64,768]{1,0:T(8,128)(2,1)} %get-tuple-element.110.refs_1_.refs_18_), channel_id=1, source_target_pairs={{0,2},{1,3},{2,0},{3,1},{4,6},{5,7},{6,4},{7,5},{8,10},{9,11},{10,... | collective-permute-start | bytes 294920 | tf_op jit(solution)/shard_map/ppermute | solution.py:55
  110.6 26.1 %collective-permute-start.28 = (bf16[64,768]{1,0:T(8,128)(2,1)}, bf16[64,768]{1,0:T(8,128)(2,1)}, u32[]{:S(2)}, u32[]{:S(2)}) collective-permute-start(bf16[64,768]{1,0:T(8,128)(2,1)} %get-tuple-element.110.refs_1_.refs_18_), channel_id=1, source_target_pairs={{0,1},{1,0},{2,3},{3,2},{4,5},{5,4},{6,7},{7,6},{8,9},{9,8},{10,11... | collective-permute-start | bytes 294920 | tf_op jit(solution)/shard_map/ppermute | solution.py:55
  134.2 47.8 %collective-permute-start.7 = (bf16[192,1664]{1,0:T(8,128)(2,1)}, bf16[192,1664]{1,0:T(8,128)(2,1)}, u32[]{:S(2)}, u32[]{:S(2)}) collective-permute-start(bf16[192,1664]{1,0:T(8,128)(2,1)} %shard_map.247.refs_7_.refs_5_), channel_id=1, source_target_pairs={{0,12},{4,8},{8,4},{12,0},{1,13},{5,9},{9,5},{13,1},{2,14},{6,10},... | collective-permute-start | bytes 1916936 | tf_op jit(solution)/shard_map/ppermute | solution.py:55
  135.6 50.5 %collective-permute-start.6 = (bf16[192,1664]{1,0:T(8,128)(2,1)}, bf16[192,1664]{1,0:T(8,128)(2,1)}, u32[]{:S(2)}, u32[]{:S(2)}) collective-permute-start(bf16[192,1664]{1,0:T(8,128)(2,1)} %shard_map.247.refs_7_.refs_5_), channel_id=1, source_target_pairs={{0,8},{4,12},{8,0},{12,4},{1,9},{5,13},{9,1},{13,5},{2,10},{6,14},... | collective-permute-start | bytes 1916936 | tf_op jit(solution)/shard_map/ppermute | solution.py:55
  136.6 49.5 %collective-permute-start.5 = (bf16[192,1664]{1,0:T(8,128)(2,1)}, bf16[192,1664]{1,0:T(8,128)(2,1)}, u32[]{:S(2)}, u32[]{:S(2)}) collective-permute-start(bf16[192,1664]{1,0:T(8,128)(2,1)} %shard_map.247.refs_7_.refs_5_), channel_id=1, source_target_pairs={{0,4},{4,0},{8,12},{12,8},{1,5},{5,1},{9,13},{13,9},{2,6},{6,2},{1... | collective-permute-start | bytes 1916936 | tf_op jit(solution)/shard_map/ppermute | solution.py:55
  140.0 27.1 %collective-permute-start.31 = (bf16[128,768]{1,0:T(8,128)(2,1)S(1)}, bf16[128,768]{1,0:T(8,128)(2,1)S(1)}, u32[]{:S(2)}, u32[]{:S(2)}) collective-permute-start(bf16[128,768]{1,0:T(8,128)(2,1)S(1)} %get-tuple-element.112), channel_id=1, source_target_pairs={{0,4},{4,0},{8,12},{12,8},{1,5},{5,1},{9,13},{13,9},{2,6},{6,2},{1... | collective-permute-start | bytes 589832 | tf_op jit(solution)/shard_map/ppermute | solution.py:55
  141.3 28.3 %collective-permute-start.32 = (bf16[128,768]{1,0:T(8,128)(2,1)S(1)}, bf16[128,768]{1,0:T(8,128)(2,1)S(1)}, u32[]{:S(2)}, u32[]{:S(2)}) collective-permute-start(bf16[128,768]{1,0:T(8,128)(2,1)S(1)} %get-tuple-element.113), channel_id=1, source_target_pairs={{0,8},{4,12},{8,0},{12,4},{1,9},{5,13},{9,1},{13,5},{2,10},{6,14},... | collective-permute-start | bytes 589832 | tf_op jit(solution)/shard_map/ppermute | solution.py:55
  182.0 25.7 %collective-permute-start.8 = (bf16[192,1664]{1,0:T(8,128)(2,1)}, bf16[192,1664]{1,0:T(8,128)(2,1)S(1)}, u32[]{:S(2)}, u32[]{:S(2)}) collective-permute-start(bf16[192,1664]{1,0:T(8,128)(2,1)} %shard_map.247.refs_7_.refs_5_), channel_id=1, source_target_pairs={{0,16},{16,0},{1,17},{17,1},{2,18},{18,2},{3,19},{19,3},{4,20},{20... | collective-permute-start | bytes 1916936 | tf_op jit(solution)/shard_map/ppermute | solution.py:39
  186.1 22.4 %collective-permute-start.11 = (bf16[192,1664]{1,0:T(8,128)(2,1)}, bf16[192,1664]{1,0:T(8,128)(2,1)}, u32[]{:S(2)}, u32[]{:S(2)}) collective-permute-start(bf16[192,1664]{1,0:T(8,128)(2,1)} %collective-permute-done.7.refs_10_.refs_8_), channel_id=1, source_target_pairs={{0,16},{16,0},{1,17},{17,1},{2,18},{18,2},{3,19},{19,3},{4,20},{20... | collective-permute-start | bytes 1916936 | tf_op jit(solution)/shard_map/ppermute | solution.py:39
  186.1 30.3 %collective-permute-start.10 = (bf16[192,1664]{1,0:T(8,128)(2,1)}, bf16[192,1664]{1,0:T(8,128)(2,1)}, u32[]{:S(2)}, u32[]{:S(2)}) collective-permute-start(bf16[192,1664]{1,0:T(8,128)(2,1)} %collective-permute-done.6.refs_9_.refs_7_), channel_id=1, source_target_pairs={{0,16},{16,0},{1,17},{17,1},{2,18},{18,2},{3,19},{19,3},{4,20},{20... | collective-permute-start | bytes 1916936 | tf_op jit(solution)/shard_map/ppermute | solution.py:39
  187.3 29.9 %collective-permute-start.9 = (bf16[192,1664]{1,0:T(8,128)(2,1)}, bf16[192,1664]{1,0:T(8,128)(2,1)}, u32[]{:S(2)}, u32[]{:S(2)}) collective-permute-start(bf16[192,1664]{1,0:T(8,128)(2,1)} %collective-permute-done.5.refs_8_.refs_6_), channel_id=1, source_target_pairs={{0,16},{16,0},{1,17},{17,1},{2,18},{18,2},{3,19},{19,3},{4,20},{20... | collective-permute-start | bytes 1916936 | tf_op jit(solution)/shard_map/ppermute | solution.py:39
  216.4 26.0 %collective-permute-start.49 = (bf16[128,768]{1,0:T(8,128)(2,1)}, bf16[128,768]{1,0:T(8,128)(2,1)}, u32[]{:S(2)}, u32[]{:S(2)}) collective-permute-start(bf16[128,768]{1,0:T(8,128)(2,1)} %get-tuple-element.136), channel_id=1, source_target_pairs={{0,4},{4,0},{8,12},{12,8},{1,5},{5,1},{9,13},{13,9},{2,6},{6,2},{1... | collective-permute-start | bytes 589832 | tf_op jit(solution)/shard_map/ppermute | solution.py:55
  306.9 11.6 %collective-permute-start.69 = (bf16[128,768]{1,0:T(8,128)(2,1)S(1)}, bf16[128,768]{1,0:T(8,128)(2,1)S(1)}, u32[]{:S(2)}, u32[]{:S(2)}) collective-permute-start(bf16[128,768]{1,0:T(8,128)(2,1)S(1)} %get-tuple-element.165), channel_id=1, source_target_pairs={{0,8},{4,12},{8,0},{12,4},{1,9},{5,13},{9,1},{13,5},{2,10},{6,14},... | collective-permute-start | bytes 589832 | tf_op jit(solution)/shard_map/ppermute | solution.py:55
  307.0 11.6 %collective-permute-start.70 = (bf16[128,768]{1,0:T(8,128)(2,1)S(1)}, bf16[128,768]{1,0:T(8,128)(2,1)S(1)}, u32[]{:S(2)}, u32[]{:S(2)}) collective-permute-start(bf16[128,768]{1,0:T(8,128)(2,1)S(1)} %get-tuple-element.166), channel_id=1, source_target_pairs={{0,12},{4,8},{8,4},{12,0},{1,13},{5,9},{9,5},{13,1},{2,14},{6,10},... | collective-permute-start | bytes 589832 | tf_op jit(solution)/shard_map/ppermute | solution.py:55
  309.5 17.8 %collective-permute-start.58 = (bf16[128,768]{1,0:T(8,128)(2,1)S(1)}, bf16[128,768]{1,0:T(8,128)(2,1)S(1)}, u32[]{:S(2)}, u32[]{:S(2)}) collective-permute-start(bf16[128,768]{1,0:T(8,128)(2,1)S(1)} %copy-done.95), channel_id=1, source_target_pairs={{0,4},{4,0},{8,12},{12,8},{1,5},{5,1},{9,13},{13,9},{2,6},{6,2},{1... | collective-permute-start | bytes 589832 | tf_op jit(solution)/shard_map/ppermute | solution.py:55
  309.6 19.9 %collective-permute-start.59 = (bf16[128,768]{1,0:T(8,128)(2,1)S(1)}, bf16[128,768]{1,0:T(8,128)(2,1)S(1)}, u32[]{:S(2)}, u32[]{:S(2)}) collective-permute-start(bf16[128,768]{1,0:T(8,128)(2,1)S(1)} %copy-done.93), channel_id=1, source_target_pairs={{0,8},{4,12},{8,0},{12,4},{1,9},{5,13},{9,1},{13,5},{2,10},{6,14},... | collective-permute-start | bytes 589832 | tf_op jit(solution)/shard_map/ppermute | solution.py:55
  311.4 39.3 %collective-permute-start.86 = (bf16[64,3072]{1,0:T(8,128)(2,1)S(1)}, bf16[64,3072]{1,0:T(8,128)(2,1)S(1)}, u32[]{:S(2)}, u32[]{:S(2)}) collective-permute-start(bf16[64,3072]{1,0:T(8,128)(2,1)S(1)} %get-tuple-element.188), channel_id=1, source_target_pairs={{0,16},{16,0},{1,17},{17,1},{2,18},{18,2},{3,19},{19,3},{4,20},{20... | collective-permute-start | bytes 1179656 | tf_op jit(solution)/shard_map/ppermute | solution.py:39
  318.4 11.3 %collective-permute-start.60 = (bf16[128,768]{1,0:T(8,128)(2,1)S(1)}, bf16[128,768]{1,0:T(8,128)(2,1)S(1)}, u32[]{:S(2)}, u32[]{:S(2)}) collective-permute-start(bf16[128,768]{1,0:T(8,128)(2,1)S(1)} %copy-done.91), channel_id=1, source_target_pairs={{0,12},{4,8},{8,4},{12,0},{1,13},{5,9},{9,5},{13,1},{2,14},{6,10},... | collective-permute-start | bytes 589832 | tf_op jit(solution)/shard_map/ppermute | solution.py:55
  336.5 15.8 %collective-permute-start.74 = (bf16[64,768]{1,0:T(8,128)(2,1)S(1)}, bf16[64,768]{1,0:T(8,128)(2,1)S(1)}, u32[]{:S(2)}, u32[]{:S(2)}) collective-permute-start(bf16[64,768]{1,0:T(8,128)(2,1)S(1)} %get-tuple-element.172), channel_id=1, source_target_pairs={{0,1},{1,0},{2,3},{3,2},{4,5},{5,4},{6,7},{7,6},{8,9},{9,8},{10,11... | collective-permute-start | bytes 294920 | tf_op jit(solution)/shard_map/ppermute | solution.py:55
  336.6 15.7 %collective-permute-start.75 = (bf16[64,768]{1,0:T(8,128)(2,1)S(1)}, bf16[64,768]{1,0:T(8,128)(2,1)S(1)}, u32[]{:S(2)}, u32[]{:S(2)}) collective-permute-start(bf16[64,768]{1,0:T(8,128)(2,1)S(1)} %get-tuple-element.173), channel_id=1, source_target_pairs={{0,2},{1,3},{2,0},{3,1},{4,6},{5,7},{6,4},{7,5},{8,10},{9,11},{10,... | collective-permute-start | bytes 294920 | tf_op jit(solution)/shard_map/ppermute | solution.py:55
  337.5 14.8 %collective-permute-start.76 = (bf16[64,768]{1,0:T(8,128)(2,1)S(1)}, bf16[64,768]{1,0:T(8,128)(2,1)S(1)}, u32[]{:S(2)}, u32[]{:S(2)}) collective-permute-start(bf16[64,768]{1,0:T(8,128)(2,1)S(1)} %get-tuple-element.174), channel_id=1, source_target_pairs={{0,3},{1,2},{2,1},{3,0},{4,7},{5,6},{6,5},{7,4},{8,11},{9,10},{10,... | collective-permute-start | bytes 294920 | tf_op jit(solution)/shard_map/ppermute | solution.py:55
  352.2 16.3 %collective-permute-start.88 = (bf16[192,1664]{1,0:T(8,128)(2,1)S(1)}, bf16[192,1664]{1,0:T(8,128)(2,1)S(1)}, u32[]{:S(2)}, u32[]{:S(2)}) collective-permute-start(bf16[192,1664]{1,0:T(8,128)(2,1)S(1)} %get-tuple-element.191), channel_id=1, source_target_pairs={{0,4},{4,0},{8,12},{12,8},{1,5},{5,1},{9,13},{13,9},{2,6},{6,2},{1... | collective-permute-start | bytes 1916936 | tf_op jit(solution)/shard_map/ppermute | solution.py:55
  362.3 29.7 %collective-permute-start.89 = (bf16[192,1664]{1,0:T(8,128)(2,1)S(1)}, bf16[192,1664]{1,0:T(8,128)(2,1)S(1)}, u32[]{:S(2)}, u32[]{:S(2)}) collective-permute-start(bf16[192,1664]{1,0:T(8,128)(2,1)S(1)} %get-tuple-element.192), channel_id=1, source_target_pairs={{0,8},{4,12},{8,0},{12,4},{1,9},{5,13},{9,1},{13,5},{2,10},{6,14},... | collective-permute-start | bytes 1916936 | tf_op jit(solution)/shard_map/ppermute | solution.py:55
  364.0 29.3 %collective-permute-start.90 = (bf16[192,1664]{1,0:T(8,128)(2,1)S(1)}, bf16[192,1664]{1,0:T(8,128)(2,1)S(1)}, u32[]{:S(2)}, u32[]{:S(2)}) collective-permute-start(bf16[192,1664]{1,0:T(8,128)(2,1)S(1)} %get-tuple-element.193), channel_id=1, source_target_pairs={{0,12},{4,8},{8,4},{12,0},{1,13},{5,9},{9,5},{13,1},{2,14},{6,10},... | collective-permute-start | bytes 1916936 | tf_op jit(solution)/shard_map/ppermute | solution.py:55
  366.7 30.5 %collective-permute-start.80 = (bf16[192,1664]{1,0:T(8,128)(2,1)S(1)}, bf16[192,1664]{1,0:T(8,128)(2,1)S(1)}, u32[]{:S(2)}, u32[]{:S(2)}) collective-permute-start(bf16[192,1664]{1,0:T(8,128)(2,1)S(1)} %get-tuple-element.180), channel_id=1, source_target_pairs={{0,4},{4,0},{8,12},{12,8},{1,5},{5,1},{9,13},{13,9},{2,6},{6,2},{1... | collective-permute-start | bytes 1916936 | tf_op jit(solution)/shard_map/ppermute | solution.py:55
  367.7 51.7 %collective-permute-start.81 = (bf16[192,1664]{1,0:T(8,128)(2,1)S(1)}, bf16[192,1664]{1,0:T(8,128)(2,1)S(1)}, u32[]{:S(2)}, u32[]{:S(2)}) collective-permute-start(bf16[192,1664]{1,0:T(8,128)(2,1)S(1)} %get-tuple-element.181), channel_id=1, source_target_pairs={{0,8},{4,12},{8,0},{12,4},{1,9},{5,13},{9,1},{13,5},{2,10},{6,14},... | collective-permute-start | bytes 1916936 | tf_op jit(solution)/shard_map/ppermute | solution.py:55
  368.5 51.7 %collective-permute-start.82 = (bf16[192,1664]{1,0:T(8,128)(2,1)S(1)}, bf16[192,1664]{1,0:T(8,128)(2,1)S(1)}, u32[]{:S(2)}, u32[]{:S(2)}) collective-permute-start(bf16[192,1664]{1,0:T(8,128)(2,1)S(1)} %get-tuple-element.182), channel_id=1, source_target_pairs={{0,12},{4,8},{8,4},{12,0},{1,13},{5,9},{9,5},{13,1},{2,14},{6,10},... | collective-permute-start | bytes 1916936 | tf_op jit(solution)/shard_map/ppermute | solution.py:55
  394.4 27.6 %collective-permute-start.91 = (bf16[48,1664]{1,0:T(8,128)(2,1)S(1)}, bf16[48,1664]{1,0:T(8,128)(2,1)S(1)}, u32[]{:S(2)}, u32[]{:S(2)}) collective-permute-start(bf16[48,1664]{1,0:T(8,128)(2,1)S(1)} %get-tuple-element.195), channel_id=1, source_target_pairs={{0,1},{1,0},{2,3},{3,2},{4,5},{5,4},{6,7},{7,6},{8,9},{9,8},{10,11... | collective-permute-start | bytes 479240 | tf_op jit(solution)/shard_map/ppermute | solution.py:55
  395.3 27.6 %collective-permute-start.92 = (bf16[48,1664]{1,0:T(8,128)(2,1)S(1)}, bf16[48,1664]{1,0:T(8,128)(2,1)S(1)}, u32[]{:S(2)}, u32[]{:S(2)}) collective-permute-start(bf16[48,1664]{1,0:T(8,128)(2,1)S(1)} %get-tuple-element.196), channel_id=1, source_target_pairs={{0,2},{1,3},{2,0},{3,1},{4,6},{5,7},{6,4},{7,5},{8,10},{9,11},{10,... | collective-permute-start | bytes 479240 | tf_op jit(solution)/shard_map/ppermute | solution.py:55
  397.2 27.8 %collective-permute-start.93 = (bf16[48,1664]{1,0:T(8,128)(2,1)S(1)}, bf16[48,1664]{1,0:T(8,128)(2,1)S(1)}, u32[]{:S(2)}, u32[]{:S(2)}) collective-permute-start(bf16[48,1664]{1,0:T(8,128)(2,1)S(1)} %get-tuple-element.197), channel_id=1, source_target_pairs={{0,3},{1,2},{2,1},{3,0},{4,7},{5,6},{6,5},{7,4},{8,11},{9,10},{10,... | collective-permute-start | bytes 479240 | tf_op jit(solution)/shard_map/ppermute | solution.py:55
  419.4 20.6 %collective-permute-start.95 = (bf16[768,768]{1,0:T(8,128)(2,1)S(1)}, bf16[768,768]{1,0:T(8,128)(2,1)S(1)}, u32[]{:S(2)}, u32[]{:S(2)}) collective-permute-start(bf16[768,768]{1,0:T(8,128)(2,1)S(1)} %get-tuple-element.200), channel_id=1, source_target_pairs={{0,16},{16,0},{1,17},{17,1},{2,18},{18,2},{3,19},{19,3},{4,20},{20... | collective-permute-start | bytes 3538952 | tf_op jit(solution)/shard_map/ppermute | solution.py:39
  420.2 19.7 %collective-permute-start.96 = (bf16[768,768]{1,0:T(8,128)(2,1)S(1)}, bf16[768,768]{1,0:T(8,128)(2,1)S(1)}, u32[]{:S(2)}, u32[]{:S(2)}) collective-permute-start(bf16[768,768]{1,0:T(8,128)(2,1)S(1)} %get-tuple-element.201), channel_id=1, source_target_pairs={{0,16},{16,0},{1,17},{17,1},{2,18},{18,2},{3,19},{19,3},{4,20},{20... | collective-permute-start | bytes 3538952 | tf_op jit(solution)/shard_map/ppermute | solution.py:39
  425.0 10.6 %collective-permute-start.85 = (bf16[48,1664]{1,0:T(8,128)(2,1)S(1)}, bf16[48,1664]{1,0:T(8,128)(2,1)S(1)}, u32[]{:S(2)}, u32[]{:S(2)}) collective-permute-start(bf16[48,1664]{1,0:T(8,128)(2,1)S(1)} %get-tuple-element.186), channel_id=1, source_target_pairs={{0,3},{1,2},{2,1},{3,0},{4,7},{5,6},{6,5},{7,4},{8,11},{9,10},{10,... | collective-permute-start | bytes 479240 | tf_op jit(solution)/shard_map/ppermute | solution.py:55
  (175 other events, 2101.5 us)

commit v3 on v2

v3 whole, which is shorter than its diff:
```python
import functools
import math

import jax
import jax.numpy as jnp
import numpy as np
from jax import lax
from jax.experimental import pallas as pl
from jax.experimental.pallas import tpu as pltpu
from jax.sharding import PartitionSpec as P

HEADS = 12
HEAD_DIM = 64
NB = 32
EXT = 128
LEAD = 3
EPSILON = 1e-06
MASK_FILL = -1e30
BF = jnp.bfloat16
F32 = jnp.float32
VM = pl.BlockSpec()
SM = pl.BlockSpec(memory_space=pltpu.SMEM)
HB = pl.BlockSpec(memory_space=pltpu.HBM)
AN = pl.BlockSpec(memory_space=pl.ANY)


def dot(a, b):
    return jnp.dot(a, b, preferred_element_type=F32)


def dot_t(a, b):
    return lax.dot_general(a, b, (((1,), (1,)), ((), ())), preferred_element_type=F32)


def t_dot(a, b):
    return lax.dot_general(a, b, (((0,), (0,)), ((), ())), preferred_element_type=F32)


def swap(value):
    return lax.ppermute(value, "section", [(0, 1), (1, 0)])


def direct(axis):
    count = lax.axis_size(axis)
    return count <= 4 and count & (count - 1) == 0


def peer_ids(axis):
    count = lax.axis_size(axis)
    ids = jnp.arange(count, dtype=jnp.int32)
    return ids ^ lax.axis_index(axis) if direct(axis) else ids


def hop(value, axis, step):
    count = lax.axis_size(axis)
    return lax.ppermute(value, axis, [(i, i ^ step) for i in range(count)])


def spread(value, axis):
    count = lax.axis_size(axis)
    if direct(axis):
        return [value] + [hop(value, axis, step) for step in range(1, count)]
    every = lax.all_gather(value, axis, axis=0)
    return [every[i] for i in range(count)]


def exchange(blocks, axis):
    count = lax.axis_size(axis)
    if direct(axis):
        return [blocks[0]] + [hop(blocks[step], axis, step) for step in range(1, count)]
    swapped = lax.all_to_all(jnp.stack(blocks), axis, 0, 0, tiled=True)
    return [swapped[i] for i in range(count)]


def scatter_rows(whole):
    for axis in ("expert", "shard"):
        count = lax.axis_size(axis)
        rows = whole.shape[0] // count
        ids = peer_ids(axis)
        blocks = [
            lax.dynamic_slice_in_dim(whole, ids[i] * rows, rows, axis=0).astype(BF)
            for i in range(count)
        ]
        whole = sum(block.astype(F32) for block in exchange(blocks, axis))
    return whole


def call(kernel, outs, ins, specs, scratch=(), flops=0, out_specs=None, after=()):
    count = len(ins)
    moved = sum(math.prod(a.shape) * a.dtype.itemsize for a in (*ins, *outs))

    def run(*refs):
        kernel(*refs[:count], *refs[count + len(after) :])

    return pl.pallas_call(
        run,
        out_shape=list(outs),
        in_specs=list(specs) + [AN] * len(after),
        out_specs=list(out_specs or [VM] * len(outs)),
        scratch_shapes=list(scratch),
        compiler_params=pltpu.CompilerParams(vmem_limit_bytes=28 * 1024 * 1024),
        cost_estimate=pl.CostEstimate(flops=flops, bytes_accessed=moved, transcendentals=0),
    )(*ins, *after)


def out(shape, kind=BF):
    return jax.ShapeDtypeStruct(shape, kind)


def begin(copies):
    for copy in copies:
        copy.start()
    return copies


def finish(copies):
    for copy in copies:
        copy.wait()


def join_weights(place, pieces, held, layout, shards):
    peers = len(pieces) // (2 * len(layout))
    for part in range(2):
        target = place[0] if part == 0 else 1 - place[0]
        for i, (zs, column) in enumerate(layout):
            for e in range(peers):
                piece = pieces[(part * len(layout) + i) * peers + e]
                rows = piece.shape[0] // len(zs)
                for at, z in enumerate(zs):
                    first = (place[2 + e] * shards + place[2 + peers + z]) * rows
                    held[
                        target,
                        pl.ds(pl.multiple_of(first, rows), rows),
                        column : column + piece.shape[1],
                    ] = piece[at * rows : (at + 1) * rows, :]


def as_column(row, turned=None):
    n = row.shape[1]
    across = lax.broadcasted_iota(jnp.int32, (n, n), 1)
    down = lax.broadcasted_iota(jnp.int32, (n, n), 0)
    if turned is not None:
        down = turned - down
    return jnp.sum(jnp.where(across == down, row, jnp.zeros_like(row)), axis=1, keepdims=True)


def table_places(width, own_rows, table_rows):
    spot = lax.broadcasted_iota(jnp.int32, (16, width), 1).astype(F32)
    owner = jnp.floor((spot + 0.5) * (1.0 / own_rows))
    rest = spot - owner * own_rows
    flat = owner * table_rows + rest
    bucket = jnp.floor((flat + 0.5) * (1.0 / HEADS))
    head = flat - bucket * HEADS
    real = rest < table_rows
    row = lax.broadcasted_iota(jnp.int32, (16, width), 0).astype(F32)
    return jnp.where(real, bucket, -1.0)[0:1], (real & (head == row)).astype(F32)


def inverse_rms(value):
    return lax.rsqrt(jnp.mean(value * value, axis=-1, keepdims=True) + EPSILON)


def norm_back(value, gain, grad):
    scale = inverse_rms(value)
    scaled = value * scale
    gained = grad * gain
    back = scale * (gained - scaled * jnp.mean(gained * scaled, axis=-1, keepdims=True))
    return back, jnp.sum(grad * scaled, axis=0, keepdims=True)


def gain_rows(side):
    pick = (
        lax.broadcasted_iota(jnp.int32, (16, EXT), 0)
        == lax.broadcasted_iota(jnp.int32, (16, EXT), 1)
    ).astype(BF)
    rows = dot_t(pick, side)
    return rows[0:1], rows[1:2], rows[2:3]


def gelu_parts(value):
    c = math.sqrt(2.0 / math.pi)
    square = value * value
    inner = jnp.tanh(c * (value + 0.044715 * square * value))
    grad = 0.5 * (1.0 + inner) + 0.5 * value * (1.0 - inner * inner) * (
        c + (3.0 * 0.044715 * c) * square
    )
    return 0.5 * value * (1.0 + inner), grad


def softmax_lanes(logits, experts):
    lane = lax.broadcasted_iota(jnp.int32, logits.shape, 1)
    valid = (lane >= LEAD) & (lane < LEAD + experts)
    logits = jnp.where(valid, logits, MASK_FILL)
    power = jnp.exp(logits - jnp.max(logits, axis=-1, keepdims=True))
    power = jnp.where(valid, power, 0.0)
    return power / jnp.sum(power, axis=-1, keepdims=True), lane


def pair_rows(value):
    low_lanes = lax.broadcasted_iota(jnp.int32, value.shape, 1) < HEAD_DIM
    zero = jnp.zeros_like(value)
    return jnp.concatenate(
        [jnp.where(low_lanes, value, zero), jnp.where(low_lanes, zero, value)], axis=0
    )


def pair_lanes(value):
    half = value.shape[0] // 2
    low_lanes = lax.broadcasted_iota(jnp.int32, (half, value.shape[1]), 1) < HEAD_DIM
    return jnp.where(low_lanes, value[:half], value[half:])


def attn_forward(layer, seq, width, experts, layout, count, shards, own_rows, table_rows, *refs):
    place, info = refs[:2]
    refs = refs[2:]
    pieces, refs = refs[:count], refs[count:]
    if layer == 0:
        (x_ref,), refs = refs[:1], refs[1:]
        n2_ref, refs = refs[0], refs[1:]
        extra = []
    else:
        (hid_ref,), toks, refs = refs[:1], refs[1:-16], refs[-16:]
        out_ref, n2_ref, tok_out = refs[:3]
        refs = refs[3:]
    acts_out, probs_out, floats_out, ext_out, held_out = refs[:5]
    held, sem, acts, probs_keep, floats, ext_keep, low_keep, out_sems = refs[5:]
    if layer == 0:
        low = x_ref[...]
    else:
        coming = pltpu.make_async_copy(hid_ref, floats, out_sems.at[0])
        coming.start()
        tok = sum(t[...].astype(F32) for t in toks).astype(BF)
        low_keep[...] = tok
        coming.wait()
        gate = floats[:, width + EXT : width + EXT + 1]
        low = (floats[:, :width] + gate * tok.astype(F32)).astype(BF)
        out_ref[...] = low
        extra = begin([pltpu.make_async_copy(low_keep, tok_out, out_sems.at[0])])
    acts[:, 6 * width :] = low
    x = low.astype(F32)
    scaled = x * inverse_rms(x)
    seg_row = info[0:1, :seq]
    same = as_column(seg_row) == seg_row
    route = as_column(info[1 + layer : 2 + layer, :seq])
    bucket = as_column(info[3:4, :]).astype(F32)
    bucket_row, head_sel = table_places(width, own_rows, table_rows)
    buckets = (bucket == bucket_row).astype(BF)
    if layout:
        join_weights(place, pieces, held, layout, shards)
    else:
        held[place[0]] = pieces[0][...]
        held[1 - place[0]] = pieces[1][...]
    extra = extra + begin([pltpu.make_async_copy(held, held_out, sem)])
    side = held[0, :, 2 * width : 2 * width + EXT]
    ext_keep[...] = side
    extra = extra + begin([pltpu.make_async_copy(ext_keep, ext_out, out_sems.at[1])])
    gain_one, gain_two, table_row = gain_rows(side)
    table = dot_t((head_sel * table_row).astype(BF), buckets)
    normed = (scaled * gain_one).astype(BF)
    acts[:, :width] = normed
    acts[:, width : 3 * width] = dot(normed, held[0, :, : 2 * width]).astype(BF)
    acts[:, 3 * width : 4 * width] = dot(normed, held[1, :, :width]).astype(BF)
    scale = 1.0 / math.sqrt(HEAD_DIM)
    contexts = []
    for p in range(HEADS // 2):
        at = [(1 + i) * width + 128 * p for i in range(3)]
        q2 = pair_rows(acts[:, at[0] : at[0] + 128])
        scores = dot_t(q2, acts[:, at[1] : at[1] + 128]) * scale
        parts = []
        for h in (2 * p, 2 * p + 1):
            line = jnp.broadcast_to(table[h : h + 1], (seq, 2 * seq))
            bias = pltpu.roll(line, seq + 1, axis=1, stride=1, stride_axis=0)[:, :seq]
            part = scores[seq * (h - 2 * p) : seq * (h - 2 * p) + seq] + bias
            parts.append(jnp.where(same, part, MASK_FILL))
        scores = jnp.concatenate(parts, axis=0)
        power = jnp.exp(scores - jnp.max(scores, axis=-1, keepdims=True))
        probs = power / jnp.sum(power, axis=-1, keepdims=True)
        probs_keep[p] = probs
        contexts.append(pair_lanes(dot(probs.astype(BF), acts[:, at[2] : at[2] + 128])))
    extra = extra + begin([pltpu.make_async_copy(probs_keep, probs_out, out_sems.at[2])])
    context = jnp.concatenate(contexts, axis=1).astype(BF)
    acts[:, 4 * width : 5 * width] = context
    hidden = x + dot(context, held[1, :, width : 2 * width])
    floats[:, :width] = hidden
    normed_two = (hidden * inverse_rms(hidden) * gain_two).astype(BF)
    n2_ref[...] = normed_two
    acts[:, 5 * width : 6 * width] = normed_two
    extra = extra + begin([pltpu.make_async_copy(acts, acts_out, out_sems.at[3])])
    gates, lane = softmax_lanes(dot(normed_two, side), experts)
    floats[:, width : width + EXT] = gates
    value = jnp.sum(jnp.where(lane == route + LEAD, gates, 0.0), axis=-1, keepdims=True)
    floats[:, width + EXT :] = jnp.broadcast_to(value, gates.shape)
    finish(extra + begin([pltpu.make_async_copy(floats, floats_out, out_sems.at[4])]))


def pick_inputs(seq, *refs):
    place, own_feed, came_feed, segments, own_routes, came_routes, buckets = refs[:7]
    x_ref, dy_ref, info, sems = refs[7:]
    sec = place[0]
    for core in range(2):

        @pl.when(sec == core)
        def _(core=core):
            sources = (own_feed, came_feed) if core == 0 else (came_feed, own_feed)
            finish(
                begin(
                    [
                        pltpu.make_async_copy(sources[0].at[core], x_ref, sems.at[0]),
                        pltpu.make_async_copy(sources[1].at[core], dy_ref, sems.at[1]),
                    ]
                )
            )
            info[...] = jnp.full(info.shape, -2, jnp.int32)
            info[0:1, :seq] = segments[core : core + 1, :]
            info[1 + core : 2 + core, :seq] = own_routes[core : core + 1, :]
            info[2 - core : 3 - core, :seq] = came_routes[core : core + 1, :]
            info[3:4, : 2 * seq - 1] = buckets[...]


def routing_slots(shards, seq, experts, cap, *refs):
    place, infos, slots = refs[0], refs[1 : 1 + shards], refs[1 + shards]
    before = (
        lax.broadcasted_iota(jnp.int32, (seq, seq), 0)
        < lax.broadcasted_iota(jnp.int32, (seq, seq), 1)
    ).astype(BF)
    routes = jnp.concatenate(
        [info[1 + layer : 2 + layer, :seq] for layer in range(2) for info in infos], axis=0
    )
    rank = jnp.zeros(routes.shape, F32)
    for e in range(experts):
        mine = (routes == e).astype(F32)
        rank = rank + mine * dot(mine.astype(BF), before)
    slots[...] = (routes ^ place[1]) * cap + rank.astype(jnp.int32)


def slot_hot(slots, layer, shards, z, total):
    row = slots[layer * shards + z : layer * shards + z + 1, :]
    return (lax.broadcasted_iota(jnp.int32, (total, row.shape[1]), 0) == row).astype(BF)


def dispatch_rows(layer, count, shards, cap, *refs):
    slots = refs[0]
    toks = refs[1 : 1 + shards]
    blocks = refs[1 + shards :]
    for z in range(shards):
        rows = dot(slot_hot(slots, layer, shards, z, count * cap), toks[z][...]).astype(BF)
        for i in range(count):
            blocks[i][z * cap : (z + 1) * cap, :] = rows[i * cap : (i + 1) * cap]


def combine_rows(layer, count, shards, cap, *refs):
    slots = refs[0]
    blocks, refs = refs[1 : 1 + count], refs[1 + count :]
    more = (len(refs) - shards) // 2
    handed, toks, given = refs[:more], refs[more : more + shards], refs[more + shards :]
    for z in range(shards):
        rows = jnp.concatenate([b[z * cap : (z + 1) * cap, :] for b in blocks], axis=0)
        toks[z][...] = t_dot(slot_hot(slots, layer, shards, z, count * cap), rows).astype(BF)
    for source, target in zip(handed, given):
        target[...] = source[...]


def start_expert(layer, place, own, came, held, sems):
    def begin(pair):
        for i in range(2):
            pltpu.make_async_copy(pair[i], held.at[i], sems.at[i]).start()

    @pl.when(place[0] == layer)
    def _():
        begin(own)

    @pl.when(place[0] != layer)
    def _():
        begin(came)

    return [pltpu.make_async_copy(own[i], held.at[i], sems.at[i]) for i in range(2)]


def expert_forward(layer, count, *refs):
    place, own, came = refs[0], refs[1:3], refs[3:5]
    blocks = refs[5 : 5 + count]
    results, rows_out = refs[5 + count : 5 + 2 * count], refs[5 + 2 * count]
    held, sems, rows, out_sem = refs[6 + 2 * count :]
    copies = start_expert(layer, place, own, came, held, sems)
    each = blocks[0].shape[0]
    for i in range(count):
        rows[i * each : (i + 1) * each, :] = blocks[i][...]
    leaving = begin([pltpu.make_async_copy(rows, rows_out, out_sem)])
    finish(copies)
    for i in range(count):
        activated = gelu_parts(dot(blocks[i][...], held[0]))[0].astype(BF)
        results[i][...] = dot(activated, held[1]).astype(BF)
    finish(leaving)


def expert_backward(layer, count, experts, with_out, *refs):
    place, own, came, ext_in = refs[0], refs[1:3], refs[3:5], refs[5]
    if with_out:
        blocks, dy_in, refs = refs[6 : 6 + count], refs[6 + count : 6 + 2 * count], refs[6 + 2 * count :]
    else:
        rows_in, dys, refs = refs[6], refs[7 : 7 + count], refs[7 + count :]
    grads, refs = refs[:count], refs[count:]
    if with_out:
        results, refs = refs[:count], refs[count:]
    keep_out, held, sems, keep, ext, late, more_sems = refs
    copies = start_expert(layer, place, own, came, held, sems)
    each = grads[0].shape[0]
    loads = [pltpu.make_async_copy(ext_in, ext, more_sems.at[0])]
    if with_out:
        loads += [
            pltpu.make_async_copy(dy_in[i], late.at[pl.ds(i * each, each), :], more_sems.at[1 + i])
            for i in range(count)
        ]
    else:
        loads += [pltpu.make_async_copy(rows_in, late, more_sems.at[1])]
    begin(loads)
    finish(loads + copies)
    leaving = []
    for i in range(count):
        at = slice(i * each, (i + 1) * each)
        if with_out:
            rows, dy = blocks[i][...], late[at, :]
        else:
            rows, dy = late[at, :], dys[i][...]
        dy = dy.astype(F32)
        gates, lane = softmax_lanes(dot(rows, ext[...]), experts)
        mine = (lane == place[1] + LEAD).astype(F32)
        value = jnp.sum(gates * mine, axis=-1, keepdims=True)
        grad_expert = (value * dy).astype(BF)
        act, slope = gelu_parts(dot(rows, held[0]))
        act = act.astype(BF)
        grad_pre = (dot_t(grad_expert, held[1]) * slope).astype(BF)
        grad = dot_t(grad_pre, held[0])
        if with_out:
            result = dot(act, held[1])
            results[i][...] = result.astype(BF)
            grad_gate = jnp.sum(dy * result, axis=-1, keepdims=True)
            grad_logits = (grad_gate * value * (mine - gates)).astype(BF)
            grad = grad + dot_t(grad_logits, ext[...])
        grads[i][...] = grad.astype(BF)
        keep[0, at, :] = rows
        keep[1, at, :] = grad_pre
        keep[2, at, :] = act
        keep[3, at, :] = grad_expert
        leaving += begin(
            [
                pltpu.make_async_copy(
                    keep.at[:, pl.ds(i * each, each), :],
                    keep_out.at[:, pl.ds(i * each, each), :],
                    more_sems.at[1 + count + i],
                )
            ]
        )
    finish(leaving)


def attn_backward(layer, seq, width, experts, shards, own_rows, table_rows, *refs):
    place, info, held_in = refs[:3]
    refs = refs[3:]
    dy_ref, acts_in, probs_in, floats_in = refs[:4]
    refs = refs[4:]
    if layer == 0:
        tok_in, refs = refs[0], refs[1:]
    parts, refs = refs[:shards], refs[shards:]
    dx_ref, ship, stay, side_grad = refs[:4]
    held, sem, acts, probs_all, floats, tok_keep, gj, g_rel, in_sems = refs[4:]
    loads = [
        pltpu.make_async_copy(floats_in, floats, in_sems.at[0]),
        pltpu.make_async_copy(acts_in, acts, in_sems.at[1]),
        pltpu.make_async_copy(probs_in, probs_all, in_sems.at[2]),
    ]
    if layer == 0:
        loads.append(pltpu.make_async_copy(tok_in, tok_keep, in_sems.at[3]))
    begin(loads)
    copies = begin([pltpu.make_async_copy(held_in, held, sem)])
    dy = dy_ref[...].astype(F32)
    grad_norm_two = sum(p[...].astype(F32) for p in parts)
    route = as_column(info[1 + layer : 2 + layer, :seq])
    bucket = as_column(info[3:4, :], 2 * seq - 2).astype(F32)
    bucket_row, head_sel = table_places(width, own_rows, table_rows)
    buckets = (bucket == bucket_row).astype(BF)
    finish(loads)
    hidden = floats[:, :width]
    x = acts[:, 6 * width :].astype(F32)
    state = acts
    finish(copies)
    side = held[0, :, 2 * width : 2 * width + EXT]
    gain_one, gain_two, _ = gain_rows(side)
    side_grad[...] = jnp.zeros_like(side_grad)
    if layer == 0:
        gates = floats[:, width : width + EXT]
        lane = lax.broadcasted_iota(jnp.int32, gates.shape, 1)
        hot = (lane == route + LEAD).astype(F32)
        grad_gate = jnp.sum(dy * tok_keep[...].astype(F32), axis=-1, keepdims=True)
        value = floats[:, width + EXT : width + EXT + 1]
        grad_logits = (grad_gate * value * (hot - gates)).astype(BF)
        grad_norm_two = grad_norm_two + dot_t(grad_logits, side)
        router_rows = t_dot(grad_logits, acts[:, 5 * width : 6 * width])
        side_grad[...] = router_rows[: side_grad.shape[0]]
    back, gain_two_grad = norm_back(hidden, gain_two, grad_norm_two)
    grad_hidden = dy + back
    grad_hidden_low = grad_hidden.astype(BF)
    grad_context = dot_t(grad_hidden_low, held[1, :, width : 2 * width]).astype(BF)
    scale = 1.0 / math.sqrt(HEAD_DIM)
    mirror = (
        lax.broadcasted_iota(jnp.int32, (seq, 2 * seq), 0)
        + lax.broadcasted_iota(jnp.int32, (seq, 2 * seq), 1)
        == seq - 1
    ).astype(BF)
    for p in range(HEADS // 2):
        lanes = slice(128 * p, 128 * p + 128)
        q2 = pair_rows(state[:, width + 128 * p : width + 128 * p + 128])
        keys = state[:, 2 * width + 128 * p : 2 * width + 128 * p + 128]
        vals = state[:, 3 * width + 128 * p : 3 * width + 128 * p + 128]
        g2 = pair_rows(grad_context[:, lanes])
        probs = probs_all[p]
        grad_probs = dot_t(g2, vals)
        grad_scores = probs * (
            grad_probs - jnp.sum(probs * grad_probs, axis=-1, keepdims=True)
        )
        grad_scores = grad_scores.astype(BF)
        gj[:, lanes] = (pair_lanes(dot(grad_scores, keys)) * scale).astype(BF)
        gj[:, width + 128 * p : width + 128 * p + 128] = (t_dot(grad_scores, q2) * scale).astype(BF)
        gj[:, 2 * width + 128 * p : 2 * width + 128 * p + 128] = t_dot(
            probs.astype(BF), g2
        ).astype(BF)
        turned = dot(grad_scores, mirror)
        for h in range(2):
            shifted = pltpu.roll(turned[h * seq : (h + 1) * seq], 0, axis=1, stride=1, stride_axis=0)
            g_rel[2 * p + h : 2 * p + h + 1, :] = jnp.sum(shifted, axis=0, keepdims=True)
    g_rel[HEADS:, :] = jnp.zeros_like(g_rel[HEADS:, :])
    offsets = g_rel[...]
    high = offsets.astype(BF)
    low = (offsets - high.astype(F32)).astype(BF)
    by_row = dot(high, buckets) + dot(low, buckets)
    side_grad[2:3, :] = jnp.sum(by_row * head_sel, axis=0, keepdims=True)
    side_grad[1:2, :] = gain_two_grad
    grad_normed = dot_t(gj[:, : 2 * width], held[0, :, : 2 * width]) + dot_t(
        gj[:, 2 * width :], held[1, :, :width]
    )
    back, gain_one_grad = norm_back(x, gain_one, grad_normed)
    side_grad[0:1, :] = gain_one_grad
    dx_ref[...] = (grad_hidden + back).astype(BF)
    normed = state[:, :width]
    halves = (ship, stay)
    for core in range(2):

        @pl.when(place[0] == core)
        def _(core=core):
            halves[1 - core][:, :width] = normed
            halves[1 - core][:, width : 3 * width] = gj[:, : 2 * width]
            halves[1 - core][:, 3 * width :] = jnp.zeros_like(normed)
            halves[core][:, :width] = normed
            halves[core][:, width : 2 * width] = gj[:, 2 * width :]
            halves[core][:, 2 * width : 3 * width] = state[:, 4 * width : 5 * width]
            halves[core][:, 3 * width :] = grad_hidden_low


def last_output(seq, width, experts, shards, *refs):
    info, dy_ref, acts_in, floats_in, side_in = refs[:5]
    parts, refs = refs[5 : 5 + shards], refs[5 + shards :]
    out_ref, side_grad, normed, floats, sems = refs
    loads = begin(
        [
            pltpu.make_async_copy(floats_in, floats, sems.at[0]),
            pltpu.make_async_copy(acts_in.at[:, pl.ds(5 * width, width)], normed, sems.at[1]),
        ]
    )
    tok = sum(p[...].astype(F32) for p in parts).astype(BF).astype(F32)
    finish(loads)
    value = floats[:, width + EXT : width + EXT + 1]
    out_ref[...] = (floats[:, :width] + value * tok).astype(BF)
    gates = floats[:, width : width + EXT]
    lane = lax.broadcasted_iota(jnp.int32, gates.shape, 1)
    hot = (lane == as_column(info[2:3, :seq]) + LEAD).astype(F32)
    grad_gate = jnp.sum(dy_ref[...].astype(F32) * tok, axis=-1, keepdims=True)
    grad_logits = (grad_gate * value * (hot - gates)).astype(BF)
    side_grad[...] = side_in[...] + t_dot(grad_logits, normed[...])[: side_grad.shape[0]]


def attn_weights(width, count, parts, *refs):
    place, stay, came = refs[:3]
    total = refs[-1]
    blocks = refs[-1 - count : -1]
    sides = refs[3 : -1 - count]

    def both(first, last):
        return jnp.concatenate([stay[:, first:last], came[:, first:last]], axis=0)

    for i, part in enumerate(parts):
        at = slice(i * width, (i + 1) * width)

        @pl.when(place[0] == 0)
        def _(part=part, at=at):
            total[:, at] = t_dot(
                both(0, width), both((1 + part) * width, (2 + part) * width)
            ).astype(BF)

        @pl.when(place[0] != 0)
        def _(part=part, at=at):
            total[:, at] = t_dot(
                both(2 * part * width, (2 * part + 1) * width),
                both((2 * part + 1) * width, (2 * part + 2) * width),
            ).astype(BF)

    if sides:
        block = jnp.zeros((width, EXT), F32)
        for layer in range(2):
            rows = sides[2 * layer][...] + sides[2 * layer + 1][...]
            pick = (
                lax.broadcasted_iota(jnp.int32, (rows.shape[0], EXT), 0) + layer * (EXT // 2)
                == lax.broadcasted_iota(jnp.int32, (rows.shape[0], EXT), 1)
            ).astype(BF)
            block = block + t_dot(rows.astype(BF), pick)
        total[:, len(parts) * width :] = block.astype(BF)

    rows = blocks[0].shape[0]
    for i in range(count):
        first = pl.multiple_of(place[2 + i] * rows, rows) if count > 1 else 0
        blocks[i][...] = total[pl.ds(first, rows), :]


def last_swap(width, *refs):
    place, zero, one_left, one_right, send = refs

    @pl.when(place[0] == 0)
    def _():
        send[:, :width] = one_left[...]
        send[:, width : 2 * width] = one_right[...]
        send[:, 2 * width :] = zero[:, 2 * width :]

    @pl.when(place[0] != 0)
    def _():
        send[...] = zero[...]


def last_grads(width, experts, *refs):
    place, zero, one_left, one_right, came = refs[:5]
    query, key, value, out_proj, gain_a, gain_f, table, router = refs[5:]

    def put(half_a, side_at, values, outs):
        query[...] = half_a[:, :width]
        key[...] = half_a[:, width : 2 * width]
        value[...] = values
        out_proj[...] = outs
        side = half_a[:, 2 * width + side_at : 2 * width + side_at + EXT // 2]
        n = side.shape[0]
        across = lax.broadcasted_iota(jnp.int32, (n, n), 1)
        down = lax.broadcasted_iota(jnp.int32, (n, n), 0)

        def turned(i):
            return jnp.sum(
                jnp.where(across == down, side[:, i : i + 1], 0.0), axis=0, keepdims=True
            )

        for i, target in enumerate((gain_a, gain_f, table)):
            target[...] = turned(i)[:, : target.shape[1]]
        for e in range(experts):
            router[e : e + 1, :] = turned(LEAD + e)

    @pl.when(place[0] == 0)
    def _():
        put(zero, 0, came[:, :width], came[:, width : 2 * width])

    @pl.when(place[0] != 0)
    def _():
        put(came, EXT // 2, one_left[...], one_right[...])


def sum_blocks(count, at, *refs):
    place, parts = refs[0], refs[1 : 1 + count]
    blocks, total = refs[1 + count : -1], refs[-1]
    total[...] = sum(p[...].astype(F32) for p in parts)
    rows = blocks[0].shape[0]
    for i, block in enumerate(blocks):
        first = pl.multiple_of(place[at + i] * rows, rows) if len(blocks) > 1 else 0
        block[...] = total[pl.ds(first, rows), :].astype(block.dtype)


def join_rows(*refs):
    place, kept, came, dy = refs[:4]
    parts, (whole, later, dy_out) = refs[4:-3], refs[-3:]
    rows = parts[0].shape[0]
    for i, part in enumerate(parts):
        whole[i * rows : (i + 1) * rows, :] = part[...]
    dy_out[...] = dy[...]

    @pl.when(place[0] == 0)
    def _():
        later[...] = came[...]

    @pl.when(place[0] != 0)
    def _():
        later[...] = kept[...]


def join_columns(cut, *refs):
    parts, (left, right) = refs[:-2], refs[-2:]
    rows = parts[0].shape[0]
    for i, part in enumerate(parts):
        left[i * rows : (i + 1) * rows, :] = part[:, :cut]
        right[i * rows : (i + 1) * rows, :] = part[:, cut:]


def pack_weights(width, experts, table_rows, *refs):
    place, query, key, value, out_proj, gain_a, gain_f, table, router = refs[:9]
    send, keep, row_a, row_f, row_t, rows_r, sems = refs[9:]
    own_rows = row_a.shape[1]
    small = begin(
        [
            pltpu.make_async_copy(source, target, sems.at[4 + i])
            for i, (source, target) in enumerate(
                ((gain_a, row_a), (gain_f, row_f), (table, row_t), (router, rows_r))
            )
        ]
    )
    halves = (keep, send)
    for core in range(2):

        @pl.when(place[0] == core)
        def _(core=core):
            begin(
                [
                    pltpu.make_async_copy(
                        source,
                        halves[(core + i // 2) % 2].at[:, pl.ds(i % 2 * width, width)],
                        sems.at[i],
                    )
                    for i, source in enumerate((query, key, value, out_proj))
                ]
            )

    finish(small)
    columns = [as_column(row_a[...].astype(F32)), as_column(row_f[...].astype(F32))]
    line = row_t[...].astype(F32)
    down = lax.broadcasted_iota(jnp.int32, (own_rows, table_rows), 0)
    across = lax.broadcasted_iota(jnp.int32, (own_rows, table_rows), 1)
    columns.append(jnp.sum(jnp.where(down == across, line, 0.0), axis=1, keepdims=True))
    lines = rows_r[...].astype(F32)
    columns += [as_column(lines[e : e + 1]) for e in range(experts)]
    lane = lax.broadcasted_iota(jnp.int32, (own_rows, EXT), 1)
    block = jnp.zeros((own_rows, EXT), F32)
    for i, column in enumerate(columns):
        block = jnp.where(lane == i, column, block)
    keep[:, 2 * width :] = block.astype(BF)
    send[:, 2 * width :] = block.astype(BF)
    finish(
        [
            pltpu.make_async_copy(source, keep.at[:, pl.ds(0, width)], sems.at[i])
            for i, source in enumerate((query, key, value, out_proj))
        ]
    )


def expert_weights(other, *refs):
    place, keeps, refs = refs[0], refs[1:3], refs[3:]
    if other:
        in_ref, out_ref, held, sem = refs
    else:
        came_in, came_out, in_ref, out_ref, held, sem = refs
    for layer in range(2):

        @pl.when((place[0] == layer) != other)
        def _(layer=layer):
            pltpu.make_async_copy(keeps[layer], held, sem).start()

    pltpu.make_async_copy(keeps[0], held, sem).wait()
    grad_in = t_dot(held[0], held[1])
    grad_out = t_dot(held[2], held[3])
    if not other:
        grad_in = grad_in + came_in[...].astype(F32)
        grad_out = grad_out + came_out[...].astype(F32)
    in_ref[...] = grad_in.astype(in_ref.dtype)
    out_ref[...] = grad_out.astype(out_ref.dtype)


def body(
    feed, segments, routes, rel_bucket, gain_attn, gain_ffn, w_query, w_key, w_value, w_out_attn,
    rel_table, router, expert_in, expert_out,
):
    seq = feed.shape[2]
    width = feed.shape[3]
    experts = lax.axis_size("expert")
    shards = lax.axis_size("shard")
    cap = max(2, 2 * seq // experts)
    own_rows = w_query.shape[1]
    table_rows = rel_table.shape[1]
    quick = direct("expert") and direct("shard")
    blocks_count = experts if quick else 1
    wide = 2 * width + EXT
    side_rows = -(-(LEAD + experts) // 16) * 16
    sec = lax.axis_index("section")
    first = sec == 0
    place = jnp.concatenate(
        [
            jnp.stack([sec, lax.axis_index("expert")]).astype(jnp.int32),
            peer_ids("expert"),
            peer_ids("shard"),
        ]
    )
    row = out((seq, width))
    sems = pltpu.SemaphoreType.DMA

    small = [gain_attn, gain_ffn, rel_table, router[0].T]
    send, kept = call(
        functools.partial(pack_weights, width, experts, table_rows),
        [out((own_rows, wide))] * 2,
        [place, w_query[0], w_key[0], w_value[0], w_out_attn[0], *small],
        [SM] + [HB] * 8,
        [pltpu.VMEM(one.shape, BF) for one in small] + [sems((8,))],
    )
    came = swap(send)
    part_zero = jnp.where(first, kept, came)

    feed_own = feed[0]
    routes_own = routes[0, :, 0]
    layer_x, layer_dy, info = call(
        functools.partial(pick_inputs, seq),
        [row, row, out((8, 2 * seq), jnp.int32)],
        [
            place, feed_own, swap(feed_own), segments[:, 0], routes_own, swap(routes_own),
            rel_bucket[None, :],
        ],
        [SM, HB, AN] + [VM] * 4,
        [sems((2,))],
    )

    def both_halves(mine):
        return mine + [swap(piece) for piece in mine]

    shard_all = tuple(range(shards))
    cut = 8 * EXT
    if quick:
        own, *others = spread(part_zero, "shard")
        joined, part_one, dy_late = call(
            join_rows,
            [out(((shards - 1) * own_rows, wide)), out((own_rows, wide)), row],
            [place, kept, came, layer_dy, *others],
            [SM] + [VM] * (2 + shards),
        )
        weights_zero = both_halves(spread(own, "expert") + spread(joined, "expert"))
        columns = call(
            functools.partial(join_columns, cut),
            [out((shards * own_rows, cut)), out((shards * own_rows, wide - cut))],
            spread(part_one, "shard"),
            [VM] * shards,
            after=weights_zero[-1:],
        )
        layouts = [
            (((0,), 0), (shard_all[1:], 0)),
            ((shard_all, 0), (shard_all, cut)),
        ]
    else:
        part_one = jnp.where(first, came, kept)
        dy_late = layer_dy
        weights_zero, weights_one = [
            both_halves([lax.all_gather(part, ("expert", "shard"), axis=0, tiled=True)])
            for part in (part_zero, part_one)
        ]
        layouts = [(), ()]

    own_experts = [expert_in[0, 0], expert_out[0, 0]]
    came_experts = [swap(expert_in[0, 0]), swap(expert_out[0, 0])]

    infos = spread(info, "shard")
    if quick:
        (slots,) = call(
            functools.partial(routing_slots, shards, seq, experts, cap),
            [out((2 * shards, seq), jnp.int32)],
            [place, *infos],
            [SM] + [VM] * shards,
        )
    else:
        all_routes = jnp.stack([one[1:3, :seq] for one in infos], axis=1)
        hot = (all_routes[..., None] == peer_ids("expert")).astype(BF)
        positions = jnp.arange(seq, dtype=jnp.int32)
        before = (positions[:, None] > positions[None, :]).astype(BF)
        rank = jnp.einsum("ij,lzje->lzie", before, hot, preferred_element_type=F32)
        slot_in = jnp.arange(cap, dtype=jnp.int32).astype(F32)
        back_hot = (hot[..., None] * (rank[..., None] == slot_in).astype(BF)).reshape(
            2, shards, seq, experts * cap
        )
        to_hot = jnp.swapaxes(back_hot, 2, 3)

    block = out((shards * cap * experts // blocks_count, width))
    acts_kind = out((seq, 7 * width))
    probs_kind = out((HEADS // 2, 2 * seq, seq), F32)
    floats_kind = out((seq, width + 2 * EXT), F32)

    def buffer(kind):
        return pltpu.VMEM(kind.shape, kind.dtype)

    expert_scratch = [pltpu.VMEM((2, expert_in.shape[2], expert_in.shape[3]), BF), sems((2,))]
    expert_specs = [SM] + [AN] * 4

    def to_experts(layer, tokens, after=()):
        every = spread(tokens, "shard")
        if not quick:
            slot_rows = jnp.einsum(
                "zcs,zsd->czd", to_hot[layer], jnp.stack(every), preferred_element_type=F32
            )
            slot_rows = slot_rows.astype(BF).reshape(experts, cap * shards, width)
            moved = exchange([slot_rows[i] for i in range(experts)], "expert")
            return [jnp.concatenate(moved, axis=0)]
        blocks = call(
            functools.partial(dispatch_rows, layer, experts, shards, cap),
            [block] * experts,
            [slots, *every],
            [VM] * (1 + shards),
            after=after,
        )
        return exchange(blocks, "expert")

    def to_tokens(layer, blocks, later=()):
        if not quick:
            rows = blocks[0].reshape(experts, cap * shards, width)
            back = jnp.stack(exchange([rows[i] for i in range(experts)], "expert"))
            back = back.reshape(experts * cap, shards, width)
            tokens = jnp.einsum(
                "zsc,czd->zsd", back_hot[layer], back, preferred_element_type=F32
            ).astype(BF)
            return exchange([tokens[i] for i in range(shards)], "shard"), list(later)
        back = exchange(blocks, "expert")
        results = call(
            functools.partial(combine_rows, layer, experts, shards, cap),
            [row] * shards + [out(one.shape, one.dtype) for one in later],
            [slots, *back, *later],
            [VM] * (1 + experts + len(later)),
        )
        return exchange(results[:shards], "shard"), results[shards:]

    held_kind = out((2, width, wide))

    def attention(layer, pieces, ins, in_specs):
        count = len(pieces)
        first_outs = [row, row, row] if layer else [row]
        return call(
            functools.partial(
                attn_forward, layer, seq, width, experts, layouts[layer], count, shards, own_rows,
                table_rows,
            ),
            first_outs + [acts_kind, probs_kind, floats_kind, out((width, EXT)), held_kind],
            [place, info, *pieces, *ins],
            [SM, VM] + [VM] * count + in_specs,
            [
                buffer(held_kind), sems(()), buffer(acts_kind),
                buffer(probs_kind), buffer(floats_kind), pltpu.VMEM((width, EXT), BF), buffer(row),
                sems((5,)),
            ],
            out_specs=([VM, VM, HB] if layer else [VM]) + [HB] * 5,
        )

    def attention_back(layer, dy, state, tok, parts, after=()):
        acts, probs, floats, _, held = state
        return call(
            functools.partial(
                attn_backward, layer, seq, width, experts, shards, own_rows, table_rows,
            ),
            [
                row,
                out((seq, 4 * width)),
                out((seq, 4 * width)),
                out((side_rows, width), F32),
            ],
            [place, info, held, dy, acts, probs, floats, *tok, *parts],
            [SM, VM, HB, VM] + [HB] * (3 + len(tok)) + [VM] * shards,
            [
                buffer(held_kind), sems(()), buffer(acts_kind),
                buffer(probs_kind), buffer(floats_kind), buffer(row),
                pltpu.VMEM((seq, 3 * width), BF), pltpu.VMEM((16, 2 * seq), F32), sems((4,)),
            ],
            after=after,
        )

    keep_kind = out((4, shards * cap * experts, width))

    def back_expert(layer, rows, dys, ext_side, with_out):
        results = call(
            functools.partial(expert_backward, layer, blocks_count, experts, with_out),
            [block] * (blocks_count * (2 if with_out else 1)) + [keep_kind],
            [place, *own_experts, *came_experts, ext_side, *rows, *dys],
            expert_specs + [HB]
            + ([VM] * blocks_count + [AN] * blocks_count if with_out else [HB] + [VM] * blocks_count),
            expert_scratch + [
                buffer(keep_kind), pltpu.VMEM((width, EXT), BF),
                pltpu.VMEM(keep_kind.shape[1:], BF), sems((1 + 2 * blocks_count,)),
            ],
            out_specs=[VM] * (blocks_count * (2 if with_out else 1)) + [HB],
        )
        return results[:blocks_count], results[blocks_count:-1], results[-1]

    row_parts = experts if quick else 1

    def weight_blocks(stay, came, parts, sides=(), after=()):
        columns = len(parts) * width + (EXT if sides else 0)
        return call(
            functools.partial(attn_weights, width, row_parts, parts),
            [out((width // row_parts, columns))] * row_parts,
            [place, stay, came, *sides],
            [SM] + [VM] * (2 + len(sides)),
            [pltpu.VMEM((width, columns), BF)],
            after=after,
        )

    def sum_planes(blocks):
        if not quick:
            return blocks
        columns = blocks[0].shape[1]
        return call(
            functools.partial(sum_blocks, experts, 2 + experts),
            [out((own_rows, columns))] * shards,
            [place, *exchange(blocks, "expert")],
            [SM] + [VM] * experts,
            [pltpu.VMEM((shards * own_rows, columns), F32)],
        )

    def sum_rows(blocks):
        if not quick:
            return scatter_rows(blocks[0])
        columns = blocks[0].shape[1]
        (total,) = call(
            functools.partial(sum_blocks, shards, 0),
            [out((own_rows, columns), F32)],
            [place, *exchange(blocks, "shard")],
            [SM] + [VM] * shards,
            [pltpu.VMEM((own_rows, columns), F32)],
        )
        return total

    n2_zero, *state_zero = attention(0, weights_zero, [layer_x], [VM])
    if quick:
        weights_one = both_halves(spread(columns[0], "expert"))
    rows_zero = to_experts(0, n2_zero)
    *results, rows_zero = call(
        functools.partial(expert_forward, 0, blocks_count),
        [block] * blocks_count + [out(keep_kind.shape[1:])],
        [place, *own_experts, *came_experts, *rows_zero],
        expert_specs + [VM] * blocks_count,
        expert_scratch + [pltpu.VMEM(keep_kind.shape[1:], BF), sems(())],
        out_specs=[VM] * blocks_count + [HB],
    )
    toks, later = to_tokens(0, results, columns[1:] if quick else ())
    if quick:
        more = both_halves(spread(later[0], "expert"))
        half = len(more) // 2
        weights_one = weights_one[:half] + more[:half] + weights_one[half:] + more[half:]
    out_zero, n2_one, tok_zero, *state_one = attention(
        1, weights_one, [state_zero[2], *toks], [HB] + [VM] * shards
    )
    dys_one = to_experts(1, dy_late)
    rows_one = to_experts(1, n2_one)
    grads, results, keep_one = back_expert(1, rows_one, dys_one, state_one[3], True)
    parts_one, results = to_tokens(1, grads, results)
    toks_one, _ = to_tokens(1, results)
    dx_one, ship_one, stay_one, side_one = attention_back(
        1, layer_dy, state_one, [], parts_one, after=toks_one[:1]
    )
    came_one = swap(ship_one)
    left_one = weight_blocks(stay_one, came_one, (0,))
    dys_zero = to_experts(0, dx_one, after=left_one)
    out_one, side_one = call(
        functools.partial(last_output, seq, width, experts, shards),
        [row, out((side_rows, width), F32)],
        [info, layer_dy, state_one[0], state_one[2], side_one, *toks_one],
        [VM, VM, HB, HB, VM] + [VM] * shards,
        [buffer(row), buffer(floats_kind), sems((2,))],
    )
    side_one_came = swap(side_one)
    grads, _, keep_zero = back_expert(0, [rows_zero], dys_zero, state_zero[3], False)
    left_one = sum_planes(left_one)
    matrix = (expert_in.shape[2], expert_in.shape[3])
    keep_scratch = [pltpu.VMEM(keep_one.shape, BF), sems(())]
    sent = call(
        functools.partial(expert_weights, True),
        [out(matrix)] * 2,
        [place, keep_zero, keep_one],
        [SM, HB, HB],
        keep_scratch,
    )
    came_grads = [swap(grad) for grad in sent]
    parts_zero, _ = to_tokens(0, grads)
    right_one = weight_blocks(stay_one, came_one, (1,), after=parts_zero[:1])
    dx_zero, ship_zero, stay_zero, side_zero = attention_back(
        0, dx_one, state_zero, [tok_zero], parts_zero, after=left_one + right_one
    )
    blocks_zero = weight_blocks(
        stay_zero, swap(ship_zero), (0, 1), (side_zero, swap(side_zero), side_one, side_one_came)
    )
    sum_left = sum_rows(left_one)
    planes_right = sum_planes(right_one)
    planes_zero = sum_planes(blocks_zero)
    sum_right = sum_rows(planes_right)
    sum_zero = sum_rows(planes_zero)
    own_grads = call(
        functools.partial(expert_weights, False),
        [out(matrix, F32)] * 2,
        [place, keep_zero, keep_one, *came_grads],
        [SM, HB, HB, VM, VM],
        keep_scratch,
        after=blocks_zero[:1],
    )

    (send,) = call(
        functools.partial(last_swap, width),
        [out((own_rows, wide), F32)],
        [place, sum_zero, sum_left, sum_right],
        [SM, VM, VM, VM],
    )
    matrix_kind = out((own_rows, width), F32)
    weight_grads = call(
        functools.partial(last_grads, width, experts),
        [matrix_kind] * 4
        + [out((1, own_rows), F32)] * 2
        + [out((1, table_rows), F32), out((experts, own_rows), F32)],
        [place, sum_zero, sum_left, sum_right, swap(send)],
        [SM] + [VM] * 4,
    )

    def by_batch(zero, one):
        came = swap(jnp.where(first, one, zero))
        kept = jnp.where(first, zero, one)
        return jnp.stack([jnp.where(first, kept, came), jnp.where(first, came, kept)])

    grad_query, grad_key, grad_value, grad_out, grad_a, grad_f, grad_table, grad_router = weight_grads
    return (
        by_batch(out_zero, out_one)[None],
        by_batch(dx_zero, dx_one)[None],
        grad_a,
        grad_f,
        grad_query[None],
        grad_key[None],
        grad_value[None],
        grad_out[None],
        grad_table,
        grad_router.T[None],
        own_grads[0][None, None],
        own_grads[1][None, None],
    )


def solution(mesh):
    rows = ("expert", "shard")
    tokens = P("section", None, rows, None)
    matrix = P("section", rows, None)
    vector = P("section", rows)
    expert_specs = (P("section", "expert", None, "shard"), P("section", "expert", "shard", None))
    in_specs = (
        tokens, P(None, rows, None), tokens, P(), vector, vector, matrix, matrix, matrix, matrix,
        vector, matrix, *expert_specs,
    )
    out_specs = (
        tokens, tokens, vector, vector, matrix, matrix, matrix, matrix, vector, matrix,
        *expert_specs,
    )
    return jax.shard_map(body, mesh=mesh, in_specs=in_specs, out_specs=out_specs, check_vma=False)
```

time: 456 us -> 385 us (0.84)
  local copies, waits for them, and re-layouts: 57.9 us -> 9.2 us
  Pallas kernels: 113 us -> 67.1 us
  starting transfers between devices: 123 us -> 161 us
  other arithmetic: 7.59 us -> 1.56 us
  waiting for transfers between devices: 145 us -> 139 us
    pallas_call x26 -> x34, Pallas kernels: 113 us -> 67.1 us  [call(): pl.pallas_call(run, out_shape=list(outs), in_specs=list(specs) + [AN] * l...]
    unnamed x254 -> x28, local copies, waits for them, and re-layouts: 42.1 us -> 9.2 us
    ppermute x75 -> x87, starting transfers between devices: 81.6 us -> 110 us  [hop(): return lax.ppermute(value, axis, [(i, i ^ step) for i in range(count)])]
    ppermute x22 -> x30, starting transfers between devices: 41.2 us -> 50.9 us  [swap(): return lax.ppermute(value, 'section', [(0, 1), (1, 0)])]
    squeeze x5 -> x0, local copies, waits for them, and re-layouts: 6.36 us -> none  [the longest x2 2.62 us: to_tokens(): back_hot[layer]]
    ppermute x75 -> x87, waiting for transfers between devices: 143 us -> 137 us  [hop(): return lax.ppermute(value, axis, [(i, i ^ step) for i in range(count)])]
  transfers between devices with their start and end apart: 97 -> 117, of which waited for: 32 -> 40; matrix products, arithmetic and copies ran while one was open for 4% -> 0% of each run, Pallas kernels for 21% -> 10%
where the time goes in v3:
time: 385 us; the launch traced here: 380 us
  starting transfers between devices  161 us (42%)
  waiting for transfers between devices  139 us (36%)
  Pallas kernels  67.1 us (17%)
  local copies, waits for them, and re-layouts  9.2 us (2%)
    ppermute x87, waiting for transfers between devices, hop(): return lax.ppermute(value, axis, [(i, i ^ step) for i in range(count)])  137 us
    ppermute x87, starting transfers between devices, hop(): return lax.ppermute(value, axis, [(i, i ^ step) for i in range(count)])  110 us
    pallas_call x34, Pallas kernels, call(): pl.pallas_call(run, out_shape=list(outs), in_specs=list(specs) + [AN] * l...  67.1 us
    ppermute x30, starting transfers between devices, swap(): return lax.ppermute(value, 'section', [(0, 1), (1, 0)])  50.9 us
    unnamed x28, local copies, waits for them, and re-layouts  9.2 us
  transfers between devices with their start and end apart: 117, of which 40 were waited for; matrix products, arithmetic and copies ran while one was open for 0% of the time, Pallas kernels for 10%

profile of v3, /device:TPU:1, one launch (start us, length us, event | category | flops | bytes accessed | tf_op | source)
XLA Modules:
  0.0 379.6 jit_solution(8530287844249099111)
XLA Ops:
  9.3 2.5 collective-permute-start.3
  11.8 2.3 collective-permute-start.4
  19.9 4.9 %collective-permute-done.5.refs_6_ = bf16[48,1664]{1,0:T(8,128)(2,1)S(1)} collective-permute-done((bf16[48,1664]{1,0:T(8,128)(2,1)S(1)}, bf16[48,1664]{1,0:T(8,128)(2,1)S(1)}, u32[]{:S(2)}, u32[]{:S(2)}) %collective-permute-start.5) | collective-permute-done | bytes 159776 | tf_op jit(solution)/shard_map/ppermute | solution.py:56
  25.4 2.2 collective-permute-start.9
  30.3 3.6 collective-permute-start.24
  33.8 6.1 %collective-permute-done.19.refs_3_ = bf16[48,1664]{1,0:T(8,128)(2,1)S(1)} collective-permute-done((bf16[48,1664]{1,0:T(8,128)(2,1)S(1)}, bf16[48,1664]{1,0:T(8,128)(2,1)S(1)}, u32[]{:S(2)}, u32[]{:S(2)}) %collective-permute-start.19) | collective-permute-done | bytes 159776 | tf_op jit(solution)/shard_map/ppermute | solution.py:56
  39.9 5.0 %collective-permute-start.25 = (bf16[48,1664]{1,0:T(8,128)(2,1)S(1)}, bf16[48,1664]{1,0:T(8,128)(2,1)S(1)}, u32[]{:S(2)}, u32[]{:S(2)}) collective-permute-start(bf16[48,1664]{1,0:T(8,128)(2,1)S(1)} %collective-permute-done.19.refs_3_), channel_id=1, source_target_pairs={{0,16},{16,0},{1,17},{17,1},{2,18},{18,2},{3,19},{19,3},{4,20},{20... | collective-permute-start | bytes 479240 | tf_op jit(solution)/shard_map/ppermute | solution.py:40
  50.2 9.0 %collective-permute-done.22.refs_7_ = bf16[144,1664]{1,0:T(8,128)(2,1)S(1)} collective-permute-done((bf16[144,1664]{1,0:T(8,128)(2,1)S(1)}, bf16[144,1664]{1,0:T(8,128)(2,1)S(1)}, u32[]{:S(2)}, u32[]{:S(2)}) %collective-permute-start.22) | collective-permute-done | bytes 479264 | tf_op jit(solution)/shard_map/ppermute | solution.py:56
  61.5 3.6 collective-permute-start.14
  68.4 4.8 %shard_map.234 = (bf16[64,768]{1,0:T(8,128)(2,1)S(1)}, bf16[64,5376]{1,0:T(8,128)(2,1)S(1)}, f32[6,128,64]{2,1,0:T(8,128)S(1)}, f32[64,1024]{1,0:T(8,128)S(1)}, ...) custom-call(s32[10]{0:T(128)S(1)} %pad_add_fusion.refs_0_, ...), custom_call_target="tpu_custom_call" | custom-call | bytes 11767848 | tf_op jit(solution)/shard_map/pallas_call | solution.py:95
  73.2 2.5 collective-permute-start.32
  77.8 4.0 %collective-permute-done.33.refs_4_ = bf16[64,768]{1,0:T(8,128)(2,1)S(1)} collective-permute-done((bf16[64,768]{1,0:T(8,128)(2,1)S(1)}, bf16[64,768]{1,0:T(8,128)(2,1)S(1)}, u32[]{:S(2)}, u32[]{:S(2)}) %collective-permute-start.33) | collective-permute-done | bytes 98336 | tf_op jit(solution)/shard_map/ppermute | solution.py:56
  84.8 2.6 collective-permute-start.6
  91.0 3.6 shard_map.236
  96.2 2.5 collective-permute-start.60
  100.4 2.5 collective-permute-done.60.refs_2_
  108.3 5.1 %collective-permute-start.43 = (bf16[192,1024]{1,0:T(8,128)(2,1)S(1)}, bf16[192,1024]{1,0:T(8,128)(2,1)S(1)}, u32[]{:S(2)}, u32[]{:S(2)}) collective-permute-start(bf16[192,1024]{1,0:T(8,128)(2,1)S(1)} %get-tuple-element.144.refs_2_), channel_id=1, source_target_pairs={{0,16},{16,0},{1,17},{17,1},{2,18},{18,2},{3,19},{19,3},{4,20},{20... | collective-permute-start | bytes 1179656 | tf_op jit(solution)/shard_map/ppermute | solution.py:40
  113.4 8.8 %collective-permute-done.39.refs_4_ = bf16[128,768]{1,0:T(8,128)(2,1)S(1)} collective-permute-done((bf16[128,768]{1,0:T(8,128)(2,1)S(1)}, bf16[128,768]{1,0:T(8,128)(2,1)S(1)}, u32[]{:S(2)}, u32[]{:S(2)}) %collective-permute-start.39) | collective-permute-done | bytes 196640 | tf_op jit(solution)/shard_map/ppermute | solution.py:56
  122.2 2.3 collective-permute-start.62
  124.7 2.7 collective-permute-done.62.refs_4_
  130.7 5.5 %collective-permute-start.44 = (bf16[192,1024]{1,0:T(8,128)(2,1)S(1)}, bf16[192,1024]{1,0:T(8,128)(2,1)S(1)}, u32[]{:S(2)}, u32[]{:S(2)}) collective-permute-start(bf16[192,1024]{1,0:T(8,128)(2,1)S(1)} %collective-permute-done.11.refs_3_), channel_id=1, source_target_pairs={{0,16},{16,0},{1,17},{17,1},{2,18},{18,2},{3,19},{19,3},{4,20},{20... | collective-permute-start | bytes 1179656 | tf_op jit(solution)/shard_map/ppermute | solution.py:40
  138.6 7.3 %collective-permute-done.52.refs_21_ = bf16[64,768]{1,0:T(8,128)(2,1)S(1)} collective-permute-done((bf16[64,768]{1,0:T(8,128)(2,1)S(1)}, bf16[64,768]{1,0:T(8,128)(2,1)S(1)}, u32[]{:S(2)}, u32[]{:S(2)}) %collective-permute-start.52) | collective-permute-done | bytes 98336 | tf_op jit(solution)/shard_map/ppermute | solution.py:56
  148.7 4.6 %collective-permute-done.42.refs_9_ = bf16[192,640]{1,0:T(8,128)(2,1)S(1)} collective-permute-done((bf16[192,640]{1,0:T(8,128)(2,1)S(1)}, bf16[192,640]{1,0:T(8,128)(2,1)S(1)}, u32[]{:S(2)}, u32[]{:S(2)}) %collective-permute-start.42) | collective-permute-done | bytes 245792 | tf_op jit(solution)/shard_map/ppermute | solution.py:56
  157.0 5.0 %shard_map.238 = (bf16[64,768]{1,0:T(8,128)(2,1)S(1)}, bf16[64,768]{1,0:T(8,128)(2,1)S(1)}, bf16[64,768]{1,0:T(8,128)(2,1)S(1)}, bf16[64,5376]{1,0:T(8,128)(2,1)...) custom-call(s32[10]{0:T(128)S(1)} %pad_add_fusion.refs_0_, ...), custom_call_target="tpu_custom_call" | custom-call | bytes 12521512 | tf_op jit(solution)/shard_map/pallas_call | solution.py:95
  174.0 3.7 collective-permute-done.57.refs_7_
  177.6 6.2 %collective-permute-done.58.refs_8_ = bf16[128,768]{1,0:T(8,128)(2,1)S(1)} collective-permute-done((bf16[128,768]{1,0:T(8,128)(2,1)S(1)}, bf16[128,768]{1,0:T(8,128)(2,1)S(1)}, u32[]{:S(2)}, u32[]{:S(2)}) %collective-permute-start.58) | collective-permute-done | bytes 196640 | tf_op jit(solution)/shard_map/ppermute | solution.py:56
  183.8 11.2 %shard_map.241 = (bf16[128,768]{1,0:T(8,128)(2,1)S(1)}, bf16[128,768]{1,0:T(8,128)(2,1)S(1)}, bf16[128,768]{1,0:T(8,128)(2,1)S(1)}, bf16[128,768]{1,0:T(8,128)(2...) custom-call(s32[10]{0:T(128)S(1)} %pad_add_fusion.refs_0_, ...), custom_call_target="tpu_custom_call" | custom-call | bytes 11206696 | tf_op jit(solution)/shard_map/pallas_call | solution.py:95
  201.4 3.7 collective-permute-done.68.refs_4_
  211.7 2.8 collective-permute-done.73.refs_3_
  215.4 5.8 %shard_map.244 = (bf16[64,768]{1,0:T(8,128)(2,1)S(1)}, bf16[64,3072]{1,0:T(8,128)(2,1)S(1)}, bf16[64,3072]{1,0:T(8,128)(2,1)S(1)}, f32[16,768]{1,0:T(8,128)S(1)}) custom-call(s32[10]{0:T(128)S(1)} %pad_add_fusion.refs_0_, s32[8,128]{1,0:T(8,128)S(1)} %get-tuple-element.138.refs_1_.refs_0_, bf16[2,768,1664]{2,1,0:T(8,128)(2,1)S(1)} %get-tuple-element.165.refs_2_, ...), custom_call_target="tpu_custom_call" | custom-call | bytes 7688232 | tf_op jit(solution)/shard_map/pallas_call | solution.py:95
  221.3 6.1 %collective-permute-start.82 = (bf16[64,3072]{1,0:T(8,128)(2,1)S(1)}, bf16[64,3072]{1,0:T(8,128)(2,1)S(1)}, u32[]{:S(2)}, u32[]{:S(2)}) collective-permute-start(bf16[64,3072]{1,0:T(8,128)(2,1)S(1)} %get-tuple-element.208), channel_id=1, source_target_pairs={{0,16},{16,0},{1,17},{17,1},{2,18},{18,2},{3,19},{19,3},{4,20},{20... | collective-permute-start | bytes 1179656 | tf_op jit(solution)/shard_map/ppermute | solution.py:40
  233.0 3.8 collective-permute-done.80.refs_3_
  242.1 3.7 collective-permute-done.84.refs_9_
  245.8 7.4 %shard_map.248 = (bf16[128,768]{1,0:T(8,128)(2,1)S(1)}, bf16[128,768]{1,0:T(8,128)(2,1)S(1)}, bf16[128,768]{1,0:T(8,128)(2,1)S(1)}, bf16[128,768]{1,0:T(8,128)(2,1)S(1)}, bf16[4,512,768]{2,1,0:T(8,128)(2,1)S(1)}) custom-call(s32[10]{0:T(128)S(1)} %pad_add_fusion.refs_0_, bf16[768,768]{1,0:T(8,128)(2,1)S(1)} %bitcast.39, bf16[768,768]{1,0:T(8,128)(2,1)S(1)} %bitcast.43, ...), custom_call_target="tpu_custom_call" | custom-call | bytes 10420264 | tf_op jit(solution)/shard_map/pallas_call | solution.py:95
  260.1 6.1 %collective-permute-done.87.refs_3_ = bf16[128,768]{1,0:T(8,128)(2,1)S(1)} collective-permute-done((bf16[128,768]{1,0:T(8,128)(2,1)S(1)}, bf16[128,768]{1,0:T(8,128)(2,1)S(1)}, u32[]{:S(2)}, u32[]{:S(2)}) %collective-permute-start.87) | collective-permute-done | bytes 196640 | tf_op jit(solution)/shard_map/ppermute | solution.py:56
  266.2 2.6 collective-permute-done.88.refs_4_
  269.1 3.6 collective-permute-start.89
  275.5 3.4 collective-permute-start.76
  278.9 2.2 collective-permute-start.77
  283.1 6.0 %shard_map.252 = (bf16[64,768]{1,0:T(8,128)(2,1)S(1)}, bf16[64,3072]{1,0:T(8,128)(2,1)S(1)}, bf16[64,3072]{1,0:T(8,128)(2,1)S(1)}, f32[16,768]{1,0:T(8,128)S(1)}) custom-call(s32[10]{0:T(128)S(1)} %pad_add_fusion.refs_0_, s32[8,128]{1,0:T(8,128)S(1)} %get-tuple-element.138.refs_1_.refs_0_, bf16[2,768,1664]{2,1,0:T(8,128)(2,1)S(1)} %get-tuple-element.200.refs_2_, ...), custom_call_target="tpu_custom_call" | custom-call | bytes 7786536 | tf_op jit(solution)/shard_map/pallas_call | solution.py:95
  289.1 8.7 %collective-permute-start.96 = (bf16[64,3072]{1,0:T(8,128)(2,1)S(1)}, bf16[64,3072]{1,0:T(8,128)(2,1)S(1)}, u32[]{:S(2)}, u32[]{:S(2)}) collective-permute-start(bf16[64,3072]{1,0:T(8,128)(2,1)S(1)} %get-tuple-element.235), channel_id=1, source_target_pairs={{0,16},{16,0},{1,17},{17,1},{2,18},{18,2},{3,19},{19,3},{4,20},{20... | collective-permute-start | bytes 1179656 | tf_op jit(solution)/shard_map/ppermute | solution.py:40
  309.6 2.9 collective-permute-done.107.refs_4_
  314.6 2.4 shard_map.261
  317.1 29.2 %collective-permute-done.109.refs_3_ = bf16[192,768]{1,0:T(8,128)(2,1)S(1)} collective-permute-done((bf16[192,768]{1,0:T(8,128)(2,1)S(1)}, bf16[192,768]{1,0:T(8,128)(2,1)S(1)}, u32[]{:S(2)}, u32[]{:S(2)}) %collective-permute-start.109) | collective-permute-done | bytes 294944 | tf_op jit(solution)/shard_map/ppermute | solution.py:56
  358.3 4.1 %collective-permute-done.102.refs_2_ = bf16[48,1664]{1,0:T(8,128)(2,1)S(1)} collective-permute-done((bf16[48,1664]{1,0:T(8,128)(2,1)S(1)}, bf16[48,1664]{1,0:T(8,128)(2,1)S(1)}, u32[]{:S(2)}, u32[]{:S(2)}) %collective-permute-start.102) | collective-permute-done | bytes 159776 | tf_op jit(solution)/shard_map/ppermute | solution.py:56
  365.2 2.9 collective-permute-done.103.refs_3_
  369.3 3.7 collective-permute-start.114
  373.8 4.0 %shard_map.262 = (f32[768,768]{1,0:T(8,128)}, f32[768,768]{1,0:T(8,128)}) custom-call(s32[10]{0:T(128)S(1)} %pad_add_fusion.refs_0_, bf16[4,512,768]{2,1,0:T(8,128)(2,1)S(1)} %get-tuple-element.258.refs_1_, bf16[4,512,768]{2,1,0:T(8,128)(2,1)S(1)} %get-tuple-element.259.refs_2_, bf16[768,768]{1,0:T(8,128)(2,1)S(1)} %collective-permute-done.115.refs_3_, ...), custom_call_target="tpu_custom_call" | custom-call | bytes 13369384 | tf_op jit(solution)/shard_map/pallas_call | solution.py:95
  (257 shorter events, 139.2 us)
Async XLA Ops:
  9.3 10.6 %collective-permute-start.3 = (bf16[48,1664]{1,0:T(8,128)(2,1)S(1)}, bf16[48,1664]{1,0:T(8,128)(2,1)S(1)}, u32[]{:S(2)}, u32[]{:S(2)}) collective-permute-start(bf16[48,1664]{1,0:T(8,128)(2,1)S(1)} %broadcast_select_fusion.refs_2_), channel_id=1, source_target_pairs={{0,1},{1,0},{2,3},{3,2},{4,5},{5,4},{6,7},{7,6},{8,9},{9,8},{10,11... | collective-permute-start | bytes 479240 | tf_op jit(solution)/shard_map/ppermute | solution.py:56
  14.1 10.6 %collective-permute-start.5 = (bf16[48,1664]{1,0:T(8,128)(2,1)S(1)}, bf16[48,1664]{1,0:T(8,128)(2,1)S(1)}, u32[]{:S(2)}, u32[]{:S(2)}) collective-permute-start(bf16[48,1664]{1,0:T(8,128)(2,1)S(1)} %broadcast_select_fusion.refs_2_), channel_id=1, source_target_pairs={{0,3},{1,2},{2,1},{3,0},{4,7},{5,6},{6,5},{7,4},{8,11},{9,10},{10,... | collective-permute-start | bytes 479240 | tf_op jit(solution)/shard_map/ppermute | solution.py:56
  25.4 24.3 %collective-permute-start.9 = (bf16[144,1664]{1,0:T(8,128)(2,1)S(1)}, bf16[144,1664]{1,0:T(8,128)(2,1)S(1)}, u32[]{:S(2)}, u32[]{:S(2)}) collective-permute-start(bf16[144,1664]{1,0:T(8,128)(2,1)S(1)} %get-tuple-element.143.refs_6_), channel_id=1, source_target_pairs={{0,12},{4,8},{8,4},{12,0},{1,13},{5,9},{9,5},{13,1},{2,14},{6,10},... | collective-permute-start | bytes 1437704 | tf_op jit(solution)/shard_map/ppermute | solution.py:56
  27.6 12.3 %collective-permute-start.19 = (bf16[48,1664]{1,0:T(8,128)(2,1)S(1)}, bf16[48,1664]{1,0:T(8,128)(2,1)S(1)}, u32[]{:S(2)}, u32[]{:S(2)}) collective-permute-start(bf16[48,1664]{1,0:T(8,128)(2,1)S(1)} %broadcast_select_fusion.refs_2_), channel_id=1, source_target_pairs={{0,4},{4,0},{8,12},{12,8},{1,5},{5,1},{9,13},{13,9},{2,6},{6,2},{1... | collective-permute-start | bytes 479240 | tf_op jit(solution)/shard_map/ppermute | solution.py:56
  27.9 17.1 %collective-permute-start.20 = (bf16[48,1664]{1,0:T(8,128)(2,1)S(1)}, bf16[48,1664]{1,0:T(8,128)(2,1)S(1)}, u32[]{:S(2)}, u32[]{:S(2)}) collective-permute-start(bf16[48,1664]{1,0:T(8,128)(2,1)S(1)} %broadcast_select_fusion.refs_2_), channel_id=1, source_target_pairs={{0,8},{4,12},{8,0},{12,4},{1,9},{5,13},{9,1},{13,5},{2,10},{6,14},... | collective-permute-start | bytes 479240 | tf_op jit(solution)/shard_map/ppermute | solution.py:56
  28.1 16.9 %collective-permute-start.21 = (bf16[48,1664]{1,0:T(8,128)(2,1)S(1)}, bf16[48,1664]{1,0:T(8,128)(2,1)S(1)}, u32[]{:S(2)}, u32[]{:S(2)}) collective-permute-start(bf16[48,1664]{1,0:T(8,128)(2,1)S(1)} %broadcast_select_fusion.refs_2_), channel_id=1, source_target_pairs={{0,12},{4,8},{8,4},{12,0},{1,13},{5,9},{9,5},{13,1},{2,14},{6,10},... | collective-permute-start | bytes 479240 | tf_op jit(solution)/shard_map/ppermute | solution.py:56
  30.3 16.3 %collective-permute-start.24 = (bf16[48,1664]{1,0:T(8,128)(2,1)S(1)}, bf16[48,1664]{1,0:T(8,128)(2,1)S(1)}, u32[]{:S(2)}, u32[]{:S(2)}) collective-permute-start(bf16[48,1664]{1,0:T(8,128)(2,1)S(1)} %broadcast_select_fusion.refs_2_), channel_id=1, source_target_pairs={{0,16},{16,0},{1,17},{17,1},{2,18},{18,2},{3,19},{19,3},{4,20},{20... | collective-permute-start | bytes 479240 | tf_op jit(solution)/shard_map/ppermute | solution.py:40
  46.6 12.6 %collective-permute-start.22 = (bf16[144,1664]{1,0:T(8,128)(2,1)S(1)}, bf16[144,1664]{1,0:T(8,128)(2,1)S(1)}, u32[]{:S(2)}, u32[]{:S(2)}) collective-permute-start(bf16[144,1664]{1,0:T(8,128)(2,1)S(1)} %get-tuple-element.143.refs_6_), channel_id=1, source_target_pairs={{0,4},{4,0},{8,12},{12,8},{1,5},{5,1},{9,13},{13,9},{2,6},{6,2},{1... | collective-permute-start | bytes 1437704 | tf_op jit(solution)/shard_map/ppermute | solution.py:56
  47.8 12.3 %collective-permute-start.23 = (bf16[144,1664]{1,0:T(8,128)(2,1)S(1)}, bf16[144,1664]{1,0:T(8,128)(2,1)S(1)}, u32[]{:S(2)}, u32[]{:S(2)}) collective-permute-start(bf16[144,1664]{1,0:T(8,128)(2,1)S(1)} %get-tuple-element.143.refs_6_), channel_id=1, source_target_pairs={{0,8},{4,12},{8,0},{12,4},{1,9},{5,13},{9,1},{13,5},{2,10},{6,14},... | collective-permute-start | bytes 1437704 | tf_op jit(solution)/shard_map/ppermute | solution.py:56
  49.1 12.1 %collective-permute-start.28 = (bf16[144,1664]{1,0:T(8,128)(2,1)S(1)}, bf16[144,1664]{1,0:T(8,128)(2,1)S(1)}, u32[]{:S(2)}, u32[]{:S(2)}) collective-permute-start(bf16[144,1664]{1,0:T(8,128)(2,1)S(1)} %get-tuple-element.143.refs_6_), channel_id=1, source_target_pairs={{0,16},{16,0},{1,17},{17,1},{2,18},{18,2},{3,19},{19,3},{4,20},{20... | collective-permute-start | bytes 1437704 | tf_op jit(solution)/shard_map/ppermute | solution.py:40
  49.6 35.2 %collective-permute-start.17 = (bf16[768,768]{1,0:T(8,128)(2,1)S(1)}, bf16[768,768]{1,0:T(8,128)(2,1)S(1)}, u32[]{:S(2)}, u32[]{:S(2)}) collective-permute-start(bf16[768,768]{1,0:T(8,128)(2,1)S(1)} %bitcast.36), channel_id=1, source_target_pairs={{0,16},{16,0},{1,17},{17,1},{2,18},{18,2},{3,19},{19,3},{4,20},{20... | collective-permute-start | bytes 3538952 | tf_op jit(solution)/shard_map/ppermute | solution.py:40
  49.7 37.7 %collective-permute-start.18 = (bf16[768,768]{1,0:T(8,128)(2,1)}, bf16[768,768]{1,0:T(8,128)(2,1)S(1)}, u32[]{:S(2)}, u32[]{:S(2)}) collective-permute-start(bf16[768,768]{1,0:T(8,128)(2,1)} %bitcast.40), channel_id=1, source_target_pairs={{0,16},{16,0},{1,17},{17,1},{2,18},{18,2},{3,19},{19,3},{4,20},{20... | collective-permute-start | bytes 3538952 | tf_op jit(solution)/shard_map/ppermute | solution.py:40
  61.5 11.7 %collective-permute-start.14 = (s32[8,128]{1,0:T(8,128)S(1)}, s32[8,128]{1,0:T(8,128)S(1)}, u32[]{:S(2)}, u32[]{:S(2)}) collective-permute-start(s32[8,128]{1,0:T(8,128)S(1)} %get-tuple-element.138.refs_1_.refs_0_), channel_id=1, source_target_pairs={{0,1},{1,0},{2,3},{3,2},{4,5},{5,4},{6,7},{7,6},{8,9},{9,8},{10,11... | collective-permute-start | bytes 12296 | tf_op jit(solution)/shard_map/ppermute | solution.py:56
  84.8 11.3 %collective-permute-start.6 = (bf16[48,1664]{1,0:T(8,128)(2,1)S(1)}, bf16[48,1664]{1,0:T(8,128)(2,1)S(1)}, u32[]{:S(2)}, u32[]{:S(2)}) collective-permute-start(bf16[48,1664]{1,0:T(8,128)(2,1)S(1)} %get-tuple-element.142.refs_0_), channel_id=1, source_target_pairs={{0,1},{1,0},{2,3},{3,2},{4,5},{5,4},{6,7},{7,6},{8,9},{9,8},{10,11... | collective-permute-start | bytes 479240 | tf_op jit(solution)/shard_map/ppermute | solution.py:56
  87.4 11.3 %collective-permute-start.7 = (bf16[48,1664]{1,0:T(8,128)(2,1)S(1)}, bf16[48,1664]{1,0:T(8,128)(2,1)S(1)}, u32[]{:S(2)}, u32[]{:S(2)}) collective-permute-start(bf16[48,1664]{1,0:T(8,128)(2,1)S(1)} %get-tuple-element.142.refs_0_), channel_id=1, source_target_pairs={{0,2},{1,3},{2,0},{3,1},{4,6},{5,7},{6,4},{7,5},{8,10},{9,11},{10,... | collective-permute-start | bytes 479240 | tf_op jit(solution)/shard_map/ppermute | solution.py:56
  88.2 11.1 %collective-permute-start.8 = (bf16[48,1664]{1,0:T(8,128)(2,1)S(1)}, bf16[48,1664]{1,0:T(8,128)(2,1)S(1)}, u32[]{:S(2)}, u32[]{:S(2)}) collective-permute-start(bf16[48,1664]{1,0:T(8,128)(2,1)S(1)} %get-tuple-element.142.refs_0_), channel_id=1, source_target_pairs={{0,3},{1,2},{2,1},{3,0},{4,7},{5,6},{6,5},{7,4},{8,11},{9,10},{10,... | collective-permute-start | bytes 479240 | tf_op jit(solution)/shard_map/ppermute | solution.py:56
  94.6 12.5 %collective-permute-start.37 = (bf16[128,768]{1,0:T(8,128)(2,1)S(1)}, bf16[128,768]{1,0:T(8,128)(2,1)S(1)}, u32[]{:S(2)}, u32[]{:S(2)}) collective-permute-start(bf16[128,768]{1,0:T(8,128)(2,1)S(1)} %get-tuple-element.152), channel_id=1, source_target_pairs={{0,4},{4,0},{8,12},{12,8},{1,5},{5,1},{9,13},{13,9},{2,6},{6,2},{1... | collective-permute-start | bytes 589832 | tf_op jit(solution)/shard_map/ppermute | solution.py:56
  95.9 12.4 %collective-permute-start.38 = (bf16[128,768]{1,0:T(8,128)(2,1)S(1)}, bf16[128,768]{1,0:T(8,128)(2,1)S(1)}, u32[]{:S(2)}, u32[]{:S(2)}) collective-permute-start(bf16[128,768]{1,0:T(8,128)(2,1)S(1)} %get-tuple-element.153), channel_id=1, source_target_pairs={{0,8},{4,12},{8,0},{12,4},{1,9},{5,13},{9,1},{13,5},{2,10},{6,14},... | collective-permute-start | bytes 589832 | tf_op jit(solution)/shard_map/ppermute | solution.py:56
  99.4 29.2 %collective-permute-start.11 = (bf16[192,1024]{1,0:T(8,128)(2,1)S(1)}, bf16[192,1024]{1,0:T(8,128)(2,1)S(1)}, u32[]{:S(2)}, u32[]{:S(2)}) collective-permute-start(bf16[192,1024]{1,0:T(8,128)(2,1)S(1)} %get-tuple-element.144.refs_2_), channel_id=1, source_target_pairs={{0,4},{4,0},{8,12},{12,8},{1,5},{5,1},{9,13},{13,9},{2,6},{6,2},{1... | collective-permute-start | bytes 1179656 | tf_op jit(solution)/shard_map/ppermute | solution.py:56
  102.9 26.9 %collective-permute-start.12 = (bf16[192,1024]{1,0:T(8,128)(2,1)S(1)}, bf16[192,1024]{1,0:T(8,128)(2,1)S(1)}, u32[]{:S(2)}, u32[]{:S(2)}) collective-permute-start(bf16[192,1024]{1,0:T(8,128)(2,1)S(1)} %get-tuple-element.144.refs_2_), channel_id=1, source_target_pairs={{0,8},{4,12},{8,0},{12,4},{1,9},{5,13},{9,1},{13,5},{2,10},{6,14},... | collective-permute-start | bytes 1179656 | tf_op jit(solution)/shard_map/ppermute | solution.py:56
  105.9 24.8 %collective-permute-start.13 = (bf16[192,1024]{1,0:T(8,128)(2,1)S(1)}, bf16[192,1024]{1,0:T(8,128)(2,1)S(1)}, u32[]{:S(2)}, u32[]{:S(2)}) collective-permute-start(bf16[192,1024]{1,0:T(8,128)(2,1)S(1)} %get-tuple-element.144.refs_2_), channel_id=1, source_target_pairs={{0,12},{4,8},{8,4},{12,0},{1,13},{5,9},{9,5},{13,1},{2,14},{6,10},... | collective-permute-start | bytes 1179656 | tf_op jit(solution)/shard_map/ppermute | solution.py:56
  107.2 15.0 %collective-permute-start.39 = (bf16[128,768]{1,0:T(8,128)(2,1)S(1)}, bf16[128,768]{1,0:T(8,128)(2,1)S(1)}, u32[]{:S(2)}, u32[]{:S(2)}) collective-permute-start(bf16[128,768]{1,0:T(8,128)(2,1)S(1)} %get-tuple-element.154), channel_id=1, source_target_pairs={{0,12},{4,8},{8,4},{12,0},{1,13},{5,9},{9,5},{13,1},{2,14},{6,10},... | collective-permute-start | bytes 589832 | tf_op jit(solution)/shard_map/ppermute | solution.py:56
  108.3 28.0 %collective-permute-start.43 = (bf16[192,1024]{1,0:T(8,128)(2,1)S(1)}, bf16[192,1024]{1,0:T(8,128)(2,1)S(1)}, u32[]{:S(2)}, u32[]{:S(2)}) collective-permute-start(bf16[192,1024]{1,0:T(8,128)(2,1)S(1)} %get-tuple-element.144.refs_2_), channel_id=1, source_target_pairs={{0,16},{16,0},{1,17},{17,1},{2,18},{18,2},{3,19},{19,3},{4,20},{20... | collective-permute-start | bytes 1179656 | tf_op jit(solution)/shard_map/ppermute | solution.py:40
  127.4 20.8 %collective-permute-start.40 = (bf16[192,640]{1,0:T(8,128)(2,1)S(1)}, bf16[192,640]{1,0:T(8,128)(2,1)S(1)}, u32[]{:S(2)}, u32[]{:S(2)}) collective-permute-start(bf16[192,640]{1,0:T(8,128)(2,1)S(1)} %get-tuple-element.156.refs_6_), channel_id=1, source_target_pairs={{0,4},{4,0},{8,12},{12,8},{1,5},{5,1},{9,13},{13,9},{2,6},{6,2},{1... | collective-permute-start | bytes 737288 | tf_op jit(solution)/shard_map/ppermute | solution.py:56
  129.9 18.4 %collective-permute-start.41 = (bf16[192,640]{1,0:T(8,128)(2,1)S(1)}, bf16[192,640]{1,0:T(8,128)(2,1)S(1)}, u32[]{:S(2)}, u32[]{:S(2)}) collective-permute-start(bf16[192,640]{1,0:T(8,128)(2,1)S(1)} %get-tuple-element.156.refs_6_), channel_id=1, source_target_pairs={{0,8},{4,12},{8,0},{12,4},{1,9},{5,13},{9,1},{13,5},{2,10},{6,14},... | collective-permute-start | bytes 737288 | tf_op jit(solution)/shard_map/ppermute | solution.py:56
  130.7 24.4 %collective-permute-start.44 = (bf16[192,1024]{1,0:T(8,128)(2,1)S(1)}, bf16[192,1024]{1,0:T(8,128)(2,1)S(1)}, u32[]{:S(2)}, u32[]{:S(2)}) collective-permute-start(bf16[192,1024]{1,0:T(8,128)(2,1)S(1)} %collective-permute-done.11.refs_3_), channel_id=1, source_target_pairs={{0,16},{16,0},{1,17},{17,1},{2,18},{18,2},{3,19},{19,3},{4,20},{20... | collective-permute-start | bytes 1179656 | tf_op jit(solution)/shard_map/ppermute | solution.py:40
  156.0 17.1 %collective-permute-start.63 = (bf16[128,768]{1,0:T(8,128)(2,1)S(1)}, bf16[128,768]{1,0:T(8,128)(2,1)S(1)}, u32[]{:S(2)}, u32[]{:S(2)}) collective-permute-start(bf16[128,768]{1,0:T(8,128)(2,1)S(1)} %get-tuple-element.175), channel_id=1, source_target_pairs={{0,4},{4,0},{8,12},{12,8},{1,5},{5,1},{9,13},{13,9},{2,6},{6,2},{1... | collective-permute-start | bytes 589832 | tf_op jit(solution)/shard_map/ppermute | solution.py:56
  172.0 11.9 %collective-permute-start.58 = (bf16[128,768]{1,0:T(8,128)(2,1)S(1)}, bf16[128,768]{1,0:T(8,128)(2,1)S(1)}, u32[]{:S(2)}, u32[]{:S(2)}) collective-permute-start(bf16[128,768]{1,0:T(8,128)(2,1)S(1)} %get-tuple-element.171), channel_id=1, source_target_pairs={{0,8},{4,12},{8,0},{12,4},{1,9},{5,13},{9,1},{13,5},{2,10},{6,14},... | collective-permute-start | bytes 589832 | tf_op jit(solution)/shard_map/ppermute | solution.py:56
  173.1 10.7 %collective-permute-start.59 = (bf16[128,768]{1,0:T(8,128)(2,1)S(1)}, bf16[128,768]{1,0:T(8,128)(2,1)S(1)}, u32[]{:S(2)}, u32[]{:S(2)}) collective-permute-start(bf16[128,768]{1,0:T(8,128)(2,1)S(1)} %get-tuple-element.172), channel_id=1, source_target_pairs={{0,12},{4,8},{8,4},{12,0},{1,13},{5,9},{9,5},{13,1},{2,14},{6,10},... | collective-permute-start | bytes 589832 | tf_op jit(solution)/shard_map/ppermute | solution.py:56
  253.8 18.9 %collective-permute-start.92 = (bf16[192,768]{1,0:T(8,128)(2,1)S(1)}, bf16[192,768]{1,0:T(8,128)(2,1)S(1)}, u32[]{:S(2)}, u32[]{:S(2)}) collective-permute-start(bf16[192,768]{1,0:T(8,128)(2,1)S(1)} %get-tuple-element.210.refs_6_), channel_id=1, source_target_pairs={{0,4},{4,0},{8,12},{12,8},{1,5},{5,1},{9,13},{13,9},{2,6},{6,2},{1... | collective-permute-start | bytes 884744 | tf_op jit(solution)/shard_map/ppermute | solution.py:56
  254.7 20.2 %collective-permute-start.93 = (bf16[192,768]{1,0:T(8,128)(2,1)S(1)}, bf16[192,768]{1,0:T(8,128)(2,1)S(1)}, u32[]{:S(2)}, u32[]{:S(2)}) collective-permute-start(bf16[192,768]{1,0:T(8,128)(2,1)S(1)} %get-tuple-element.211.refs_7_), channel_id=1, source_target_pairs={{0,8},{4,12},{8,0},{12,4},{1,9},{5,13},{9,1},{13,5},{2,10},{6,14},... | collective-permute-start | bytes 884744 | tf_op jit(solution)/shard_map/ppermute | solution.py:56
  256.4 12.4 %collective-permute-start.88 = (bf16[128,768]{1,0:T(8,128)(2,1)S(1)}, bf16[128,768]{1,0:T(8,128)(2,1)S(1)}, u32[]{:S(2)}, u32[]{:S(2)}) collective-permute-start(bf16[128,768]{1,0:T(8,128)(2,1)S(1)} %get-tuple-element.220), channel_id=1, source_target_pairs={{0,12},{4,8},{8,4},{12,0},{1,13},{5,9},{9,5},{13,1},{2,14},{6,10},... | collective-permute-start | bytes 589832 | tf_op jit(solution)/shard_map/ppermute | solution.py:56
  258.5 17.0 %collective-permute-start.94 = (bf16[192,768]{1,0:T(8,128)(2,1)S(1)}, bf16[192,768]{1,0:T(8,128)(2,1)S(1)}, u32[]{:S(2)}, u32[]{:S(2)}) collective-permute-start(bf16[192,768]{1,0:T(8,128)(2,1)S(1)} %get-tuple-element.212.refs_8_), channel_id=1, source_target_pairs={{0,12},{4,8},{8,4},{12,0},{1,13},{5,9},{9,5},{13,1},{2,14},{6,10},... | collective-permute-start | bytes 884744 | tf_op jit(solution)/shard_map/ppermute | solution.py:56
  274.9 22.8 %collective-permute-start.75 = (bf16[64,768]{1,0:T(8,128)(2,1)S(1)}, bf16[64,768]{1,0:T(8,128)(2,1)S(1)}, u32[]{:S(2)}, u32[]{:S(2)}) collective-permute-start(bf16[64,768]{1,0:T(8,128)(2,1)S(1)} %get-tuple-element.196), channel_id=1, source_target_pairs={{0,1},{1,0},{2,3},{3,2},{4,5},{5,4},{6,7},{7,6},{8,9},{9,8},{10,11... | collective-permute-start | bytes 294920 | tf_op jit(solution)/shard_map/ppermute | solution.py:56
  275.5 22.2 %collective-permute-start.76 = (bf16[64,768]{1,0:T(8,128)(2,1)S(1)}, bf16[64,768]{1,0:T(8,128)(2,1)S(1)}, u32[]{:S(2)}, u32[]{:S(2)}) collective-permute-start(bf16[64,768]{1,0:T(8,128)(2,1)S(1)} %get-tuple-element.197), channel_id=1, source_target_pairs={{0,2},{1,3},{2,0},{3,1},{4,6},{5,7},{6,4},{7,5},{8,10},{9,11},{10,... | collective-permute-start | bytes 294920 | tf_op jit(solution)/shard_map/ppermute | solution.py:56
  278.9 18.9 %collective-permute-start.77 = (bf16[64,768]{1,0:T(8,128)(2,1)S(1)}, bf16[64,768]{1,0:T(8,128)(2,1)S(1)}, u32[]{:S(2)}, u32[]{:S(2)}) collective-permute-start(bf16[64,768]{1,0:T(8,128)(2,1)S(1)} %get-tuple-element.198), channel_id=1, source_target_pairs={{0,3},{1,2},{2,1},{3,0},{4,7},{5,6},{6,5},{7,4},{8,11},{9,10},{10,... | collective-permute-start | bytes 294920 | tf_op jit(solution)/shard_map/ppermute | solution.py:56
  289.1 13.2 %collective-permute-start.96 = (bf16[64,3072]{1,0:T(8,128)(2,1)S(1)}, bf16[64,3072]{1,0:T(8,128)(2,1)S(1)}, u32[]{:S(2)}, u32[]{:S(2)}) collective-permute-start(bf16[64,3072]{1,0:T(8,128)(2,1)S(1)} %get-tuple-element.235), channel_id=1, source_target_pairs={{0,16},{16,0},{1,17},{17,1},{2,18},{18,2},{3,19},{19,3},{4,20},{20... | collective-permute-start | bytes 1179656 | tf_op jit(solution)/shard_map/ppermute | solution.py:40
  298.4 15.8 %collective-permute-start.108 = (bf16[192,768]{1,0:T(8,128)(2,1)S(1)}, bf16[192,768]{1,0:T(8,128)(2,1)S(1)}, u32[]{:S(2)}, u32[]{:S(2)}) collective-permute-start(bf16[192,768]{1,0:T(8,128)(2,1)S(1)} %get-tuple-element.230.refs_17_), channel_id=1, source_target_pairs={{0,4},{4,0},{8,12},{12,8},{1,5},{5,1},{9,13},{13,9},{2,6},{6,2},{1... | collective-permute-start | bytes 884744 | tf_op jit(solution)/shard_map/ppermute | solution.py:56
  304.3 44.3 %collective-permute-start.100 = (bf16[192,1664]{1,0:T(8,128)(2,1)S(1)}, bf16[192,1664]{1,0:T(8,128)(2,1)S(1)}, u32[]{:S(2)}, u32[]{:S(2)}) collective-permute-start(bf16[192,1664]{1,0:T(8,128)(2,1)S(1)} %get-tuple-element.240), channel_id=1, source_target_pairs={{0,8},{4,12},{8,0},{12,4},{1,9},{5,13},{9,1},{13,5},{2,10},{6,14},... | collective-permute-start | bytes 1916936 | tf_op jit(solution)/shard_map/ppermute | solution.py:56
  306.1 43.4 %collective-permute-start.101 = (bf16[192,1664]{1,0:T(8,128)(2,1)S(1)}, bf16[192,1664]{1,0:T(8,128)(2,1)S(1)}, u32[]{:S(2)}, u32[]{:S(2)}) collective-permute-start(bf16[192,1664]{1,0:T(8,128)(2,1)S(1)} %get-tuple-element.241), channel_id=1, source_target_pairs={{0,12},{4,8},{8,4},{12,0},{1,13},{5,9},{9,5},{13,1},{2,14},{6,10},... | collective-permute-start | bytes 1916936 | tf_op jit(solution)/shard_map/ppermute | solution.py:56
  306.9 44.1 %collective-permute-start.99 = (bf16[192,1664]{1,0:T(8,128)(2,1)S(1)}, bf16[192,1664]{1,0:T(8,128)(2,1)S(1)}, u32[]{:S(2)}, u32[]{:S(2)}) collective-permute-start(bf16[192,1664]{1,0:T(8,128)(2,1)S(1)} %get-tuple-element.239), channel_id=1, source_target_pairs={{0,4},{4,0},{8,12},{12,8},{1,5},{5,1},{9,13},{13,9},{2,6},{6,2},{1... | collective-permute-start | bytes 1916936 | tf_op jit(solution)/shard_map/ppermute | solution.py:56
  312.4 33.8 %collective-permute-start.109 = (bf16[192,768]{1,0:T(8,128)(2,1)S(1)}, bf16[192,768]{1,0:T(8,128)(2,1)S(1)}, u32[]{:S(2)}, u32[]{:S(2)}) collective-permute-start(bf16[192,768]{1,0:T(8,128)(2,1)S(1)} %get-tuple-element.231.refs_18_), channel_id=1, source_target_pairs={{0,8},{4,12},{8,0},{12,4},{1,9},{5,13},{9,1},{13,5},{2,10},{6,14},... | collective-permute-start | bytes 884744 | tf_op jit(solution)/shard_map/ppermute | solution.py:56
  314.2 33.6 %collective-permute-start.110 = (bf16[192,768]{1,0:T(8,128)(2,1)S(1)}, bf16[192,768]{1,0:T(8,128)(2,1)S(1)}, u32[]{:S(2)}, u32[]{:S(2)}) collective-permute-start(bf16[192,768]{1,0:T(8,128)(2,1)S(1)} %get-tuple-element.232.refs_19_), channel_id=1, source_target_pairs={{0,12},{4,8},{8,4},{12,0},{1,13},{5,9},{9,5},{13,1},{2,14},{6,10},... | collective-permute-start | bytes 884744 | tf_op jit(solution)/shard_map/ppermute | solution.py:56
  346.2 27.6 %collective-permute-start.115 = (bf16[768,768]{1,0:T(8,128)(2,1)S(1)}, bf16[768,768]{1,0:T(8,128)(2,1)S(1)}, u32[]{:S(2)}, u32[]{:S(2)}) collective-permute-start(bf16[768,768]{1,0:T(8,128)(2,1)S(1)} %get-tuple-element.260), channel_id=1, source_target_pairs={{0,16},{16,0},{1,17},{17,1},{2,18},{18,2},{3,19},{19,3},{4,20},{20... | collective-permute-start | bytes 3538952 | tf_op jit(solution)/shard_map/ppermute | solution.py:40
  347.8 26.0 %collective-permute-start.116 = (bf16[768,768]{1,0:T(8,128)(2,1)S(1)}, bf16[768,768]{1,0:T(8,128)(2,1)S(1)}, u32[]{:S(2)}, u32[]{:S(2)}) collective-permute-start(bf16[768,768]{1,0:T(8,128)(2,1)S(1)} %get-tuple-element.261), channel_id=1, source_target_pairs={{0,16},{16,0},{1,17},{17,1},{2,18},{18,2},{3,19},{19,3},{4,20},{20... | collective-permute-start | bytes 3538952 | tf_op jit(solution)/shard_map/ppermute | solution.py:40
  354.1 14.0 %collective-permute-start.103 = (bf16[48,1664]{1,0:T(8,128)(2,1)S(1)}, bf16[48,1664]{1,0:T(8,128)(2,1)S(1)}, u32[]{:S(2)}, u32[]{:S(2)}) collective-permute-start(bf16[48,1664]{1,0:T(8,128)(2,1)S(1)} %get-tuple-element.244), channel_id=1, source_target_pairs={{0,2},{1,3},{2,0},{3,1},{4,6},{5,7},{6,4},{7,5},{8,10},{9,11},{10,... | collective-permute-start | bytes 479240 | tf_op jit(solution)/shard_map/ppermute | solution.py:56
  356.2 11.9 %collective-permute-start.104 = (bf16[48,1664]{1,0:T(8,128)(2,1)S(1)}, bf16[48,1664]{1,0:T(8,128)(2,1)S(1)}, u32[]{:S(2)}, u32[]{:S(2)}) collective-permute-start(bf16[48,1664]{1,0:T(8,128)(2,1)S(1)} %get-tuple-element.245), channel_id=1, source_target_pairs={{0,3},{1,2},{2,1},{3,0},{4,7},{5,6},{6,5},{7,4},{8,11},{9,10},{10,... | collective-permute-start | bytes 479240 | tf_op jit(solution)/shard_map/ppermute | solution.py:56
  362.4 10.7 %collective-permute-start.95 = (bf16[64,768]{1,0:T(8,128)(2,1)S(1)}, bf16[64,768]{1,0:T(8,128)(2,1)S(1)}, u32[]{:S(2)}, u32[]{:S(2)}) collective-permute-start(bf16[64,768]{1,0:T(8,128)(2,1)S(1)} %broadcast_select_fusion.1), channel_id=1, source_target_pairs={{0,16},{16,0},{1,17},{17,1},{2,18},{18,2},{3,19},{19,3},{4,20},{20... | collective-permute-start | bytes 294920 | tf_op jit(solution)/shard_map/ppermute | solution.py:40
  (83 other events, 522.1 us)
